TPU v7x, 512 devices: a whole 4x4x16 slice. The times are simulated.
512 devices in a mesh: mem: 32 (over x, y, z_hi), tile: 16 (over z_lo, core).
Axes of the slice: x: 4, y: 4, z: 16 (z_hi: 2, z_lo: 8; z = z_hi * 8 + z_lo), core: 2. Of those that a mesh axis runs over, the one named last changes fastest.
Arguments:
- starting_ensemble: bfloat16 [64, 8, 128, 1120], P('mem', None, 'tile'), may hold values from -6 to 6
- patch_lifting: bfloat16 [1120, 768], P('mem'), may hold values from -0.1875 to 0.1875
- query_keyvalue_lift: bfloat16 [768, 2304], P(None, 'mem'), may hold values from -0.21875 to 0.21875
- output_combiner: bfloat16 [768, 768], P(None, 'mem'), may hold values from -0.21875 to 0.21875
- decoder_linear_map: bfloat16 [768, 1120], P(None, 'mem'), may hold values from -0.21875 to 0.21875
- cosine_logit_scale: float32 [12], replicated, may hold values from 2 to 30
- sensor_variable_loadings: bfloat16 [16, 70], replicated, may hold values from -0.75 to 0.75
- sensor_gridpoint: int32 [32, 16, 256], P('mem', 'tile'), may hold values from 0 to 31, as said below
- sensor_domain_index: int32 [32, 16, 256], P('mem', 'tile'), may hold values from 0 to 1, as said below
- sensor_channel_list: int32 [32, 16, 256], P('mem', 'tile'), may hold values from 0 to 15
- sensor_reading: float32 [32, 16, 256], P('mem', 'tile'), may hold values from -6 to 6
- sensor_noise_deviation: float32 [32, 16, 256], P('mem', 'tile'), may hold values from 0.5 to 2
Outputs:
- analysis: bfloat16 [64, 8, 128, 1120], P('mem', None, 'tile')
Inputs may be any that keep to these rules, and one draw needn't show every extreme that they name: `sensor_gridpoint`: a point of the piece's 2 tokens. `sensor_domain_index`: differs by at most one from sensor_gridpoint // 16 of the same observation.
All inputs are finite; a program needn't handle non-finite values. Where the computation divides by a largest or mean magnitude, that divisor is 1e-20 or more.
Results may differ from a plain program's by a relative error of at most 0.039.
Values may be sent and summed in bfloat16 or wider, within the bound.
No kernel may reach another device: no remote copies, remote signals or barrier semaphores. Data moves between devices by JAX's collectives and lax.ppermute only.
A program may use at most 64 MiB of HBM per device.

v0:
```python
import jax
import jax.numpy as jnp
from jax import lax
from jax.sharding import PartitionSpec as P

PANE_SIDE = 8
NS_ITERS = 5


eps_norm = 1e-05
normalizing_guard = 1e-06


def passed_along(value, axis, by):
    devices = lax.axis_size(axis)
    return lax.ppermute(value, axis, [(i, (i + by) % devices) for i in range(devices)])


def layer_norm(values):
    values = values.astype(jnp.float32)
    center = values - jnp.mean(values, axis=-1, keepdims=True)
    spread = jnp.mean(center * center, axis=-1, keepdims=True)
    return center * lax.rsqrt(spread + eps_norm)


def unit_rows(values):
    values = values.astype(jnp.float32)
    return (
        values * lax.rsqrt(jnp.sum(values * values, axis=-1, keepdims=True) + normalizing_guard)
    ).astype(jnp.bfloat16)


def pane_cosine_mixer(padded_part, query_keyvalue_lift, cosine_logit_scale):
    members, rows, cols, attention_span = padded_part.shape
    focus_groups = cosine_logit_scale.shape[0]
    head_dim = attention_span // focus_groups
    qkv = jnp.dot(
        padded_part.reshape(-1, attention_span),
        query_keyvalue_lift,
        preferred_element_type=jnp.float32,
    ).astype(jnp.bfloat16)
    qkv = qkv.reshape(
        members, rows // PANE_SIDE, PANE_SIDE, cols // PANE_SIDE, PANE_SIDE, 3 * attention_span
    )
    qkv = qkv.transpose(0, 1, 3, 2, 4, 5).reshape(
        -1, PANE_SIDE * PANE_SIDE, 3, focus_groups, head_dim
    )
    query = unit_rows(qkv[:, :, 0])
    key_rows = unit_rows(qkv[:, :, 1])
    value_rows = qkv[:, :, 2]
    affinity_logits = jnp.einsum(
        "bihd,bjhd->bhij", query, key_rows, preferred_element_type=jnp.float32
    )
    affinity_logits = affinity_logits * cosine_logit_scale[None, :, None, None]
    weights = jnp.exp(affinity_logits)
    probs = (weights / jnp.sum(weights, axis=-1, keepdims=True)).astype(jnp.bfloat16)
    mixed_outcome = jnp.einsum(
        "bhij,bjhd->bihd", probs, value_rows, preferred_element_type=jnp.float32
    )
    mixed_outcome = mixed_outcome.astype(jnp.bfloat16).reshape(
        members, rows // PANE_SIDE, cols // PANE_SIDE, PANE_SIDE, PANE_SIDE, attention_span
    )
    return mixed_outcome.transpose(0, 1, 3, 2, 4, 5).reshape(members, rows, cols, attention_span)


def batched(left, right):
    return jnp.einsum("rij,rjk->rik", left, right, precision=lax.Precision.HIGHEST)


def local_analysis(
    embedded_patches,
    decoder_linear_map,
    sensor_gridpoint,
    sensor_domain_index,
    sensor_channel_list,
    sensor_reading,
    sensor_noise_deviation,
    sensor_variable_loadings,
):
    members, regions, attention_span = embedded_patches.shape
    feats = decoder_linear_map.shape[1]
    channels, variables = sensor_variable_loadings.shape
    points = feats // variables
    count = sensor_gridpoint.shape[0]
    prior_member_grids = jnp.dot(
        embedded_patches.reshape(-1, attention_span),
        decoder_linear_map,
        preferred_element_type=jnp.float32,
    ).astype(jnp.bfloat16)
    token = sensor_gridpoint // points
    point = sensor_gridpoint - token * points
    pick_point = (point[:, None] == jnp.arange(points, dtype=jnp.int32)[None, :]).astype(
        jnp.float32
    )
    pick_chan = (
        sensor_channel_list[:, None] == jnp.arange(channels, dtype=jnp.int32)[None, :]
    ).astype(jnp.float32)
    rows_h = jnp.dot(
        pick_chan, sensor_variable_loadings.astype(jnp.float32), precision=lax.Precision.HIGHEST
    )
    measurement_mapping = (
        (pick_point[:, :, None] * rows_h[:, None, :]).reshape(count, feats).astype(jnp.bfloat16)
    )
    mapped_samples = lax.dot_general(
        prior_member_grids,
        measurement_mapping,
        (((1,), (1,)), ((), ())),
        preferred_element_type=jnp.float32,
    )
    mapped_samples = mapped_samples.reshape(members, regions, count)
    pick_token = (token[None, :] == jnp.arange(regions, dtype=jnp.int32)[:, None]).astype(
        jnp.float32
    )
    ens_obs = jnp.sum(mapped_samples * pick_token[None], axis=1)
    mean_obs = jnp.mean(ens_obs, axis=0)
    pert_obs = ens_obs - mean_obs[None, :]
    innovation = sensor_reading - mean_obs
    distance = (token - sensor_domain_index).astype(jnp.float32)
    obs_weight = jnp.exp(-0.5 * distance * distance) / (
        sensor_noise_deviation * sensor_noise_deviation
    )
    pick_region = (
        sensor_domain_index[:, None] == jnp.arange(regions, dtype=jnp.int32)[None, :]
    ).astype(jnp.float32)
    weighted = pert_obs * obs_weight[None, :]
    gram = jnp.einsum(
        "kj,jr,lj->rkl", weighted, pick_region, pert_obs, precision=lax.Precision.HIGHEST
    )
    drive = jnp.einsum(
        "kj,jr,j->rk", weighted, pick_region, innovation, precision=lax.Precision.HIGHEST
    )
    eye = jnp.eye(members, dtype=jnp.float32)
    system = eye[None] + gram / (members - 1.0)
    bound = jnp.max(jnp.sum(jnp.abs(system), axis=2), axis=1)
    iterate = system / bound[:, None, None]
    inverse_root = jnp.broadcast_to(eye, system.shape)
    for step in range(NS_ITERS):
        factor = 1.5 * eye[None] - 0.5 * batched(inverse_root, iterate)
        iterate = batched(iterate, factor)
        inverse_root = batched(factor, inverse_root)
    root = inverse_root * lax.rsqrt(bound)[:, None, None]
    inner = jnp.einsum("rkl,rl->rk", root, drive, precision=lax.Precision.HIGHEST)
    mean_weight = jnp.einsum("rkl,rl->rk", root, inner, precision=lax.Precision.HIGHEST) / (
        members - 1.0
    )
    transform_matrix = root + mean_weight[:, :, None]
    values = embedded_patches.astype(jnp.float32)
    center = jnp.mean(values, axis=0)
    spread = values - center[None]
    posterior = center[None] + jnp.einsum(
        "ktf,tkm->mtf", spread, transform_matrix, precision=lax.Precision.HIGHEST
    )
    return posterior.astype(jnp.bfloat16)


def per_device(
    starting_ensemble,
    patch_lifting,
    query_keyvalue_lift,
    output_combiner,
    decoder_linear_map,
    cosine_logit_scale,
    sensor_variable_loadings,
    sensor_gridpoint,
    sensor_domain_index,
    sensor_channel_list,
    sensor_reading,
    sensor_noise_deviation,
):
    members, rows, cols, feats = starting_ensemble.shape
    full_embed, entire_triplet_product, full_out, full_head = (
        lax.all_gather(patch_lifting, "mem", axis=0, tiled=True),
        lax.all_gather(query_keyvalue_lift, "mem", axis=1, tiled=True),
        lax.all_gather(output_combiner, "mem", axis=1, tiled=True),
        lax.all_gather(decoder_linear_map, "mem", axis=1, tiled=True),
    )
    attention_span = full_embed.shape[1]
    hidden = jnp.dot(
        starting_ensemble.reshape(-1, feats), full_embed, preferred_element_type=jnp.float32
    )
    hidden = hidden.astype(jnp.bfloat16).reshape(members, rows, cols, attention_span)
    normed = layer_norm(hidden).astype(jnp.bfloat16)
    half = PANE_SIDE // 2
    incoming_rows = passed_along(normed[:, :, :half], "tile", -1)
    padded_sequence = jnp.concatenate([normed[:, :, half:], incoming_rows], axis=2)
    mixed_outcome_padded = pane_cosine_mixer(
        padded_sequence, entire_triplet_product, cosine_logit_scale
    )
    returned = passed_along(mixed_outcome_padded[:, :, cols - half :], "tile", 1)
    mixed_outcome = jnp.concatenate([returned, mixed_outcome_padded[:, :, : cols - half]], axis=2)
    mixed = hidden.astype(jnp.float32) + jnp.dot(
        mixed_outcome.reshape(-1, attention_span), full_out, preferred_element_type=jnp.float32
    ).reshape(members, rows, cols, attention_span)
    embedded_patches = layer_norm(mixed).astype(jnp.bfloat16)
    tile_tokens = rows * cols
    moved = lax.all_to_all(
        embedded_patches.reshape(members, tile_tokens, attention_span),
        "mem",
        split_axis=1,
        concat_axis=0,
        tiled=True,
    )
    ensemble, regions = (moved.shape[0], moved.shape[1])
    posterior = local_analysis(
        moved,
        full_head,
        sensor_gridpoint.reshape(-1),
        sensor_domain_index.reshape(-1),
        sensor_channel_list.reshape(-1),
        sensor_reading.reshape(-1),
        sensor_noise_deviation.reshape(-1),
        sensor_variable_loadings,
    )
    produced = jnp.dot(
        posterior.reshape(-1, attention_span), full_head, preferred_element_type=jnp.float32
    )
    produced = produced.astype(jnp.bfloat16).reshape(ensemble, regions, feats)
    analysed = lax.all_to_all(produced, "mem", split_axis=0, concat_axis=1, tiled=True)
    return analysed.reshape(members, rows, cols, feats)


def solution(mesh):
    return jax.shard_map(
        per_device,
        mesh=mesh,
        in_specs=(
            P("mem", None, "tile", None),
            P("mem", None),
            P(None, "mem"),
            P(None, "mem"),
            P(None, "mem"),
            P(),
            P(),
            P("mem", "tile", None),
            P("mem", "tile", None),
            P("mem", "tile", None),
            P("mem", "tile", None),
            P("mem", "tile", None),
        ),
        out_specs=P("mem", None, "tile", None),
        check_vma=False,
    )
```

profile of v0, /device:TPU:192, one launch (start us, length us, event | category | flops | bytes accessed | tf_op | source)
XLA Modules:
  0.0 572.6 jit_solution(16573928906230880486)
XLA Ops:
  6.5 0.7 all-gather.11.cloned.1.call-update
  7.3 0.7 all-gather.7.cloned.1.call-update
  8.1 0.7 all-gather.9.cloned.1.call-update
  8.8 0.5 all-gather.13.cloned.1.call-update
  9.3 0.8 mul.191
  10.1 0.9 fusion.27
  11.0 0.7 fusion.51
  11.7 121.5 %all-gather.11.cloned.1.call-done = bf16[32,35,768]{2,1,0:T(8,128)(2,1)} async-done(((bf16[1,35,768]{2,1,0:T(8,128)(2,1)}), bf16[32,35,768]{2,1,0:T(8,128)(2,1)}) %all-gather.11.cloned.1.call-update) | async-done | bytes 1720336 | tf_op jit(solution)/shard_map/all_gather | solution.py:172
  133.3 1.8 reshape.284
  135.1 0.5 fusion.67
  135.7 0.2 multiply_reduce_fusion.1
  136.2 4.4 collective-permute-start
  140.6 2.2 collective-permute-done
  142.9 145.5 %all-gather.7.cloned.1.call-done = bf16[768,2304]{0,1:T(8,128)(2,1)} async-done(((bf16[768,72]{0,1:T(8,128)(2,1)}), bf16[768,2304]{0,1:T(8,128)(2,1)}) %all-gather.7.cloned.1.call-update) | async-done | bytes 3538960 | tf_op jit(solution)/shard_map/all_gather | solution.py:173
  288.4 3.3 convolution_convert_fusion
  291.7 0.3 copy.107
  292.0 0.5 reshape_transpose_reshape.6
  292.5 1.0 fusion.12
  293.6 0.3 slice.30
  293.9 0.8 fusion.13
  294.7 0.3 fusion
  295.0 0.3 fusion.1
  295.3 0.4 copy.112
  295.7 0.3 reshape_transpose_reshape.7
  296.1 1.9 collective-permute-start.1
  298.1 95.3 %all-gather.9.cloned.1.call-done = bf16[768,768]{0,1:T(8,128)(2,1)} async-done(((bf16[768,24]{0,1:T(8,128)(2,1)}), bf16[768,768]{0,1:T(8,128)(2,1)}) %all-gather.9.cloned.1.call-update) | async-done | bytes 1179664 | tf_op jit(solution)/shard_map/all_gather | solution.py:174
  393.3 1.9 fusion.68
  395.6 0.9 copy.113
  396.5 13.3 %all-to-all-start = ((bf16[2,64,768]{2,0,1:T(2,128)(2,1)}), bf16[2,64,768]{2,0,1:T(2,128)(2,1)S(1)}, u32[]{:S(2)}, u32[]{:S(2)}) async-start(bf16[2,64,768]{2,0,1:T(2,128)(2,1)} %copy.113), calls=%async_computation | async-start | bytes 393216 | tf_op jit(solution)/shard_map/all_to_all | solution.py:196
  410.2 108.1 %all-gather.13.cloned.1.call-done = bf16[32,35,768]{2,1,0:T(8,128)(2,1)} async-done(((bf16[1,35,768]{2,1,0:T(8,128)(2,1)}), bf16[32,35,768]{2,1,0:T(8,128)(2,1)}) %all-gather.13.cloned.1.call-update) | async-done | bytes 1720336 | tf_op jit(solution)/shard_map/all_gather | solution.py:175
  518.3 1.8 reshape.286
  520.4 0.6 convolution_convert_fusion.2
  521.0 0.2 copy.116
  521.3 0.3 fusion.64
  521.6 0.3 abs_reduce_fusion
  522.1 0.3 fusion.10
  522.4 0.4 fusion.47
  522.8 0.2 fusion.41
  525.2 0.2 fusion.6
  525.8 0.2 fusion.75
  526.2 0.2 copy.122
  526.6 0.6 fusion.5
  527.2 0.2 copy.125
  527.5 0.6 convolution_convert_fusion.1
  528.1 0.2 copy.126
  528.5 36.5 %all_to_all.30 = bf16[64,2,1120]{2,1,0:T(2,128)(2,1)S(1)} all-to-all(bf16[64,2,1120]{2,1,0:T(2,128)(2,1)S(1)} %reshape.277), channel_id=1, replica_groups=mesh['mem'=32,'tile'=16] {'mem'}, dimensions={0} | all-to-all | bytes 573440 | tf_op jit(solution)/shard_map/all_to_all | solution.py:218
  565.0 0.2 copy.127
  565.2 0.9 reshape.278
  (64 shorter events, 4.9 us)
Async XLA Ops:
  6.5 128.5 %copy-start = (bf16[2,8,8,1120]{3,2,1,0:T(8,128)(2,1)S(1)}, bf16[2,8,8,1120]{3,2,1,0:T(8,128)(2,1)}, u32[]{:S(2)}) copy-start(bf16[2,8,8,1120]{3,2,1,0:T(8,128)(2,1)} %param.12) | copy-start | bytes 860164
  6.5 126.7 %all-gather.11.cloned.1.call-start = ((), (), s32[]{:S(2)}) async-start(), calls=%async_computation.4 | async-start | bytes 2027520 | tf_op jit(solution)/shard_map/all_gather | solution.py:172
  7.3 281.2 %all-gather.7.cloned.1.call-start = ((), (), s32[]{:S(2)}) async-start(), calls=%async_computation.2 | async-start | bytes 3649536 | tf_op jit(solution)/shard_map/all_gather | solution.py:173
  8.0 385.3 %all-gather.9.cloned.1.call-start = ((), (), s32[]{:S(2)}) async-start(), calls=%async_computation.3 | async-start | bytes 1216512 | tf_op jit(solution)/shard_map/all_gather | solution.py:174
  8.7 509.6 %all-gather.13.cloned.1.call-start = ((), (), s32[]{:S(2)}) async-start(), calls=%async_computation.5 | async-start | bytes 2027520 | tf_op jit(solution)/shard_map/all_gather | solution.py:175
  135.1 5.5 copy-start.2
  136.2 6.6 %collective-permute-start = (bf16[2,8,4,768]{3,2,1,0:T(4,128)(2,1)S(1)}, bf16[2,8,4,768]{3,2,1,0:T(4,128)(2,1)S(1)}, u32[]{:S(2)}, u32[]{:S(2)}) collective-permute-start(bf16[2,8,4,768]{3,2,1,0:T(4,128)(2,1)S(1)} %get-tuple-element.16), channel_id=1, source_target_pairs={{0,15},{1,0},{2,1},{3,2},{4,3},{5,4},{6,5},{7,6},{8,7},{9,8},{10,9... | collective-permute-start | bytes 294920 | tf_op jit(solution)/shard_map/ppermute | solution.py:16
  292.5 2.2 copy-start.4
  296.1 97.2 %collective-permute-start.1 = (bf16[2,8,4,768]{3,2,1,0:T(4,128)(2,1)S(1)}, bf16[2,8,4,768]{3,2,1,0:T(4,128)(2,1)S(1)}, u32[]{:S(2)}, u32[]{:S(2)}) collective-permute-start(bf16[2,8,4,768]{3,2,1,0:T(4,128)(2,1)S(1)} %get-tuple-element.13), channel_id=1, source_target_pairs={{0,1},{1,2},{2,3},{3,4},{4,5},{5,6},{6,7},{7,8},{8,9},{9,10},{10,1... | collective-permute-start | bytes 294920 | tf_op jit(solution)/shard_map/ppermute | solution.py:16
  395.4 14.7 %copy-start.1 = (s32[1,1,256]{2,1,0:T(1,128)S(1)}, s32[1,1,256]{2,1,0:T(1,128)}, u32[]{:S(2)}) copy-start(s32[1,1,256]{2,1,0:T(1,128)} %param.20) | copy-start | bytes 3076
  396.5 123.7 %all-to-all-start = ((bf16[2,64,768]{2,0,1:T(2,128)(2,1)}), bf16[2,64,768]{2,0,1:T(2,128)(2,1)S(1)}, u32[]{:S(2)}, u32[]{:S(2)}) async-start(bf16[2,64,768]{2,0,1:T(2,128)(2,1)} %copy.113), calls=%async_computation | async-start | bytes 393216 | tf_op jit(solution)/shard_map/all_to_all | solution.py:196
  520.4 1.2 copy-start.3
Sparse Core Ops, SparseCore 0:
  11.6 121.6 all-gather.10
  137.5 150.8 all-gather.6
  292.7 100.6 all-gather.8
  397.5 120.8 all-gather.12
where the time goes:
time: 574 us; the launch traced here: 573 us
  waiting for transfers between devices  475 us (83%)
  blocking collectives  36.5 us (6%)
  starting transfers between devices  19.8 us (3%)
  between operations  13.7 us (2%)
  matrix products  13.3 us (2%)
  local copies, waits for them, and re-layouts  9.32 us (2%)
    all_gather x1, waiting for transfers between devices, per_device(): lax.all_gather(query_keyvalue_lift, 'mem', axis=1, tiled=True)  146 us
    all_gather x1, waiting for transfers between devices, per_device(): lax.all_gather(patch_lifting, 'mem', axis=0, tiled=True)  122 us
    all_gather x1, waiting for transfers between devices, per_device(): lax.all_gather(decoder_linear_map, 'mem', axis=1, tiled=True)  108 us
    all_gather x1, waiting for transfers between devices, per_device(): lax.all_gather(output_combiner, 'mem', axis=1, tiled=True)  95.3 us
    all_to_all x1, blocking collectives, per_device(): lax.all_to_all(produced, 'mem', split_axis=0, concat_axis=1, tiled=True)  36.5 us
    all_to_all x1, starting transfers between devices, per_device(): lax.all_to_all(embedded_patches.reshape(members, tile_tokens, attention_s...  13.3 us
  transfers between devices with their start and end apart: 7, of which 5 were waited for; matrix products, arithmetic and copies ran while one was open for 3% of the time, Pallas kernels for 0%

commit v1 on v0

v1 whole, which is shorter than its diff:
```python
import numpy as np
import jax
import jax.numpy as jnp
from jax import lax
from jax.sharding import Mesh, PartitionSpec as P

PANE_SIDE = 8
HALF = PANE_SIDE // 2
NS_ITERS = 5
PLANE = ("x", "y")
MEM = ("x", "y", "zh")
TILE = ("zl", "core")
BLOCK = 40

eps_norm = 1e-05
normalizing_guard = 1e-06
bf16 = jnp.bfloat16
f32 = jnp.float32


def swapped(value, axis):
    return lax.ppermute(value, axis, [(0, 1), (1, 0)])


def passed_along(value, axis, by):
    devices = lax.axis_size(axis)
    return lax.ppermute(value, axis, [(i, (i + by) % devices) for i in range(devices)])


def gathered_plane(part):
    copies = lax.optimization_barrier(jnp.broadcast_to(part[None], (16,) + part.shape))
    return lax.all_to_all(copies, PLANE, split_axis=0, concat_axis=0, tiled=True)


def layer_norm(values):
    values = values.astype(f32)
    center = values - jnp.mean(values, axis=-1, keepdims=True)
    spread = jnp.mean(center * center, axis=-1, keepdims=True)
    return center * lax.rsqrt(spread + eps_norm)


def unit_rows(values):
    values = values.astype(f32)
    return (
        values * lax.rsqrt(jnp.sum(values * values, axis=-1, keepdims=True) + normalizing_guard)
    ).astype(bf16)


def times(left, right):
    return jnp.dot(left, right, preferred_element_type=f32)


def times_t(left, right):
    return lax.dot_general(left, right, (((1,), (1,)), ((), ())), preferred_element_type=f32)


def in_order(flag, first, second, axis):
    low = jnp.where(flag == 0, first, second)
    high = jnp.where(flag == 0, second, first)
    return jnp.concatenate([low, high], axis=axis)


def halves(flag, value):
    width = value.shape[-1] // 2
    low, high = value[..., :width], value[..., width:]
    return jnp.where(flag == 0, low, high), jnp.where(flag == 0, high, low)


def batched(left, right):
    return jnp.einsum("rij,rjk->rik", left, right, precision=lax.Precision.HIGHEST)


def attention(qkv, scale):
    panes = qkv.shape[0]
    heads = scale.shape[0]
    own = PANE_SIDE * HALF
    width = qkv.shape[-1] // 3
    split = qkv.reshape(panes, PANE_SIDE * PANE_SIDE, 3, heads, width // heads)
    query = unit_rows(split[:, :own, 0])
    key_rows = unit_rows(split[:, :, 1])
    value_rows = split[:, :, 2]
    scores = jnp.einsum("bihd,bjhd->bhij", query, key_rows, preferred_element_type=f32)
    weights = jnp.exp(scores * scale[None, :, None, None])
    probs = (weights / jnp.sum(weights, axis=-1, keepdims=True)).astype(bf16)
    context = jnp.einsum("bhij,bjhd->bihd", probs, value_rows, preferred_element_type=f32)
    return context.astype(bf16).reshape(panes * own, width)


def obs_setup(obs, loadings):
    points = 16
    grid = obs[:, 0].astype(jnp.int32)
    block = jnp.arange(2, dtype=jnp.int32)[:, None] * 2
    token = grid // points
    point = (grid - token * points).reshape(-1)
    domain = obs[:, 1].astype(jnp.int32)
    channel = obs[:, 2].astype(jnp.int32).reshape(-1)
    distance = (token - domain).astype(f32)
    noise = obs[:, 4]
    weight = (jnp.exp(-0.5 * distance * distance) / (noise * noise)).reshape(-1)
    token = (token + block).reshape(-1)
    domain = (domain + block).reshape(-1)
    pick_point = (point[:, None] == jnp.arange(points, dtype=jnp.int32)[None, :]).astype(bf16)
    pick_chan = (channel[:, None] == jnp.arange(16, dtype=jnp.int32)[None, :]).astype(bf16)
    rows_h = times(pick_chan, loadings).astype(bf16)
    mapping = (pick_point[:, :, None] * rows_h[:, None, :]).reshape(point.shape[0], -1)
    pick_token = (token[None, :] == jnp.arange(4, dtype=jnp.int32)[:, None]).astype(f32)
    pick_region = (domain[None, :] == jnp.arange(4, dtype=jnp.int32)[:, None]).astype(f32)
    return mapping, pick_token, pick_region * weight[None, :], obs[:, 3].reshape(-1)


def transforms(ens_obs, region_weight, reading, own_members):
    members = ens_obs.shape[0]
    mean_obs = jnp.mean(ens_obs, axis=0)
    pert = ens_obs - mean_obs[None, :]
    innovation = reading - mean_obs
    weighted = pert[None] * region_weight[:, None, :]
    gram = jnp.einsum("rkj,lj->rkl", weighted, pert, precision=lax.Precision.HIGHEST)
    drive = jnp.einsum("rkj,j->rk", weighted, innovation, precision=lax.Precision.HIGHEST)
    eye = jnp.eye(members, dtype=f32)
    system = eye[None] + gram / (members - 1.0)
    bound = jnp.max(jnp.sum(jnp.abs(system), axis=2), axis=1)
    iterate = system / bound[:, None, None]
    inverse_root = jnp.broadcast_to(eye, system.shape)
    for step in range(NS_ITERS):
        factor = 1.5 * eye[None] - 0.5 * batched(inverse_root, iterate)
        iterate = batched(iterate, factor)
        inverse_root = batched(factor, inverse_root)
    root = inverse_root * lax.rsqrt(bound)[:, None, None]
    inner = jnp.einsum("rkl,rl->rk", root, drive, precision=lax.Precision.HIGHEST)
    mean_weight = jnp.einsum("rkl,rl->rk", root, inner, precision=lax.Precision.HIGHEST) / (
        members - 1.0
    )
    return root[:, :, :own_members] + mean_weight[:, :, None]


def per_device(
    starting_ensemble,
    patch_lifting,
    query_keyvalue_lift,
    output_combiner,
    decoder_linear_map,
    cosine_logit_scale,
    sensor_variable_loadings,
    sensor_gridpoint,
    sensor_domain_index,
    sensor_channel_list,
    sensor_reading,
    sensor_noise_deviation,
):
    members, rows, cols, feats = starting_ensemble.shape
    width = patch_lifting.shape[1]
    core = lax.axis_index("core")
    zh = lax.axis_index("zh")
    shard = patch_lifting.shape[0]

    fill = ((0, BLOCK - shard), (0, 0))
    packed = jnp.concatenate(
        [
            jnp.pad(patch_lifting, fill),
            query_keyvalue_lift.T,
            output_combiner.T,
            jnp.pad(decoder_linear_map.T, fill),
        ],
        axis=0,
    )
    mine, _ = halves(core, packed)
    front = BLOCK + query_keyvalue_lift.shape[1] + output_combiner.shape[1]
    theirs = swapped(mine, "zh")
    own_front = gathered_plane(mine[:front])
    theirs, own_front = lax.optimization_barrier((theirs, own_front))
    other_front = gathered_plane(theirs[:front])
    tail_rows = in_order(zh, mine[front:], theirs[front:], 0)
    tail_rows, other_front = lax.optimization_barrier((tail_rows, other_front))
    tail_mine = gathered_plane(tail_rows)
    own_front_p = swapped(own_front, "core")
    other_front_p = swapped(other_front, "core")
    tail_part = swapped(tail_mine, "core")

    obs = jnp.stack(
        [
            sensor_gridpoint.reshape(-1).astype(f32),
            sensor_domain_index.reshape(-1).astype(f32),
            sensor_channel_list.reshape(-1).astype(f32),
            sensor_reading.reshape(-1),
            sensor_noise_deviation.reshape(-1),
        ]
    )
    obs = in_order(zh, obs[None], swapped(obs, "zh")[None], 0)
    mapping, pick_token, region_weight, reading = obs_setup(obs, sensor_variable_loadings)

    own_x = starting_ensemble.reshape(members, rows, 2, HALF, feats).transpose(0, 2, 1, 3, 4)
    own_x = own_x.reshape(members, 2, rows * HALF, feats)
    both = jnp.concatenate([own_x, swapped(own_x, "zh")], axis=0)
    west = passed_along(both[:, 1], TILE, 1)
    east = passed_along(both[:, 0], TILE, -1)
    halo = jnp.stack([west, east], axis=1)
    panes = jnp.concatenate([both, halo], axis=2)
    count = 4 * members * rows * cols
    states = panes.reshape(count, feats)

    place = jnp.arange(2 * 16 * BLOCK, dtype=jnp.int32)
    side, rest = place // (16 * BLOCK), place % (16 * BLOCK)
    plane, inside = rest // BLOCK, rest % BLOCK
    source = (plane * 2 + jnp.where(side == 0, zh, 1 - zh)) * shard + inside
    source = jnp.where(inside < shard, source, -1)
    pick = (jnp.arange(feats, dtype=jnp.int32)[:, None] == source[None, :]).astype(bf16)
    spread_states = times(states, pick).astype(bf16)
    xa, xb = spread_states[:, : 16 * BLOCK], spread_states[:, 16 * BLOCK :]

    def embed(own, other):
        return times(xa, own[:, :BLOCK].reshape(-1, own.shape[-1])) + times(
            xb, other[:, :BLOCK].reshape(-1, own.shape[-1])
        )

    hidden = in_order(
        core, embed(own_front, other_front), embed(own_front_p, other_front_p), 1
    ).astype(bf16)
    normed = layer_norm(hidden).astype(bf16)

    def lay(own, other, start, stop):
        own, other = own[:, None, start:stop], other[:, None, start:stop]
        return in_order(zh, own, other, 1).reshape(-1, own.shape[-1])

    q_end = BLOCK + query_keyvalue_lift.shape[1]
    n_mine, n_part = halves(core, normed)
    qkv = (
        times_t(n_mine, lay(own_front, other_front, BLOCK, q_end))
        + times_t(n_part, lay(own_front_p, other_front_p, BLOCK, q_end))
    ).astype(bf16)
    context = attention(
        qkv.reshape(4 * members, PANE_SIDE * PANE_SIDE, qkv.shape[-1]), cosine_logit_scale
    )
    c_mine, c_part = halves(core, context)
    mixed = (
        times_t(c_mine, lay(own_front, other_front, q_end, front))
        + times_t(c_part, lay(own_front_p, other_front_p, q_end, front))
    )
    own_hidden = hidden.reshape(4 * members, 2, rows * HALF, width)[:, 0].reshape(-1, width)
    latent = layer_norm(own_hidden.astype(f32) + mixed).astype(bf16)

    latent = latent.reshape(2 * members, 2, rows, HALF, width).transpose(2, 1, 0, 3, 4)
    moved = lax.all_to_all(
        latent.reshape(16, 2 * members, HALF, width), PLANE, split_axis=0, concat_axis=0, tiled=True
    )
    ensemble = jnp.concatenate(
        [
            moved[:, :members].reshape(16 * members, HALF, width),
            moved[:, members:].reshape(16 * members, HALF, width),
        ],
        axis=0,
    )
    own_members = 16 * members

    def strip(tail):
        return tail.reshape(32, BLOCK, -1)[:, :shard].reshape(feats, -1)

    dec_mine, dec_part = strip(tail_mine), strip(tail_part)

    def decode(values):
        v_mine, v_part = halves(core, values)
        return (times_t(v_mine, dec_mine) + times_t(v_part, dec_part)).astype(bf16)

    forecast = decode(ensemble.reshape(-1, width))
    mapped = times_t(forecast, mapping).reshape(2 * own_members, HALF, -1)
    ens_obs = jnp.sum(mapped * pick_token[None], axis=1)
    transform = transforms(ens_obs, region_weight, reading, own_members)
    values = ensemble.astype(f32)
    center = jnp.mean(values, axis=0)
    posterior = center[None] + jnp.einsum(
        "ktf,tkm->mtf", values - center[None], transform, precision=lax.Precision.HIGHEST
    )
    posterior = posterior.astype(bf16).reshape(16, members, HALF, width)
    back = lax.all_to_all(posterior, PLANE, split_axis=0, concat_axis=0, tiled=True)
    back = back.reshape(rows, 2, members, HALF, width).transpose(2, 0, 1, 3, 4)
    return decode(back.reshape(-1, width)).reshape(members, rows, cols, feats)


def solution(mesh):
    fine = Mesh(
        np.asarray(mesh.devices).reshape(4, 4, 2, 8, 2), ("x", "y", "zh", "zl", "core")
    )
    return jax.shard_map(
        per_device,
        mesh=fine,
        in_specs=(
            P(MEM, None, TILE, None),
            P(MEM, None),
            P(None, MEM),
            P(None, MEM),
            P(None, MEM),
            P(),
            P(),
            P(MEM, TILE, None),
            P(MEM, TILE, None),
            P(MEM, TILE, None),
            P(MEM, TILE, None),
            P(MEM, TILE, None),
        ),
        out_specs=P(MEM, None, TILE, None),
        check_vma=False,
    )
```

time: 574 us -> 227 us (0.40)
  the two profiles are of different devices: /device:TPU:192 before, /device:TPU:8 now
where the time goes in v1:
time: 227 us; the launch traced here: 225 us
  starting transfers between devices  67.6 us (30%)
  waiting for transfers between devices  45 us (20%)
  local copies, waits for them, and re-layouts  44.1 us (19%)
  matrix products  29.7 us (13%)
  other arithmetic  26.6 us (12%)
  blocking collectives  11.5 us (5%)
    ppermute x6, starting transfers between devices, swapped(): return lax.ppermute(value, axis, [(0, 1), (1, 0)])  36.8 us
    all_to_all x3, starting transfers between devices, gathered_plane(): lax.all_to_all(copies, PLANE, split_axis=0, concat_axis=0, tiled=True)  21.5 us
    ppermute x6, waiting for transfers between devices, swapped(): return lax.ppermute(value, axis, [(0, 1), (1, 0)])  19.4 us
    all_to_all x3, waiting for transfers between devices, gathered_plane(): lax.all_to_all(copies, PLANE, split_axis=0, concat_axis=0, tiled=True)  19.2 us
    all_to_all x1, blocking collectives, per_device(): lax.all_to_all(posterior, PLANE, split_axis=0, concat_axis=0, tiled=True)  11.5 us
    dot_general x9, matrix products, times_t(): lax.dot_general(left, right, (((1,), (1,)), ((), ())), preferred_element_...  8.72 us
    dot_general x6, matrix products, times(): return jnp.dot(left, right, preferred_element_type=f32)  8.38 us
    unnamed x62, local copies, waits for them, and re-layouts  7.76 us
  transfers between devices with their start and end apart: 12, of which 4 were waited for; matrix products, arithmetic and copies ran while one was open for 36% of the time, Pallas kernels for 0%

profile of v1, /device:TPU:8, one launch (start us, length us, event | category | flops | bytes accessed | tf_op | source)
XLA Modules:
  0.0 225.3 jit_solution(10369012302603377939)
XLA Ops:
  2.1 15.7 %collective-permute-start.7 = (f32[5,256]{1,0:T(8,128)S(1)}, f32[5,256]{1,0:T(8,128)S(1)}, u32[]{:S(2)}, u32[]{:S(2)}) collective-permute-start(f32[5,256]{1,0:T(8,128)S(1)} %stack.18), channel_id=1, source_target_pairs={{0,16},{16,0},{1,17},{17,1},{2,18},{18,2},{3,19},{19,3},{4,20},{20... | collective-permute-start | bytes 15368 | tf_op jit(solution)/shard_map/ppermute | solution.py:22
  18.9 1.9 collective-permute-start.3
  22.1 12.6 %collective-permute-start = (bf16[2,2,32,1120]{3,1,2,0:T(2,128)(2,1)S(1)}, bf16[2,2,32,1120]{3,1,2,0:T(2,128)(2,1)S(1)}, u32[]{:S(2)}, u32[]{:S(2)}) collective-permute-start(bf16[2,2,32,1120]{3,1,2,0:T(2,128)(2,1)S(1)} %bitcast.186), channel_id=1, source_target_pairs={{0,16},{16,0},{1,17},{17,1},{2,18},{18,2},{3,19},{19,3},{4,20},{20... | collective-permute-start | bytes 860168 | tf_op jit(solution)/shard_map/ppermute | solution.py:22
  34.8 1.4 broadcast_in_dim.21
  36.1 7.4 %all-to-all-start = ((bf16[16,136,384]{2,1,0:T(8,128)(2,1)}), bf16[16,136,384]{2,1,0:T(8,128)(2,1)S(1)}, u32[]{:S(2)}, u32[]{:S(2)}) async-start(bf16[16,136,384]{2,1,0:T(8,128)(2,1)} %broadcast_in_dim.21), calls=%async_computation | async-start | bytes 3342336 | tf_op jit(solution)/shard_map/all_to_all | solution.py:32
  47.6 19.4 %collective-permute-done = bf16[2,2,32,1120]{3,1,2,0:T(2,128)(2,1)S(1)} collective-permute-done((bf16[2,2,32,1120]{3,1,2,0:T(2,128)(2,1)S(1)}, bf16[2,2,32,1120]{3,1,2,0:T(2,128)(2,1)S(1)}, u32[]{:S(2)}, u32[]{:S(2)}) %collective-permute-start) | collective-permute-done | bytes 286752 | tf_op jit(solution)/shard_map/ppermute | solution.py:22
  69.6 1.9 collective-permute-start.2
  71.5 2.4 %collective-permute-start.1 = (bf16[4,32,1120]{2,1,0:T(8,128)(2,1)}, bf16[4,32,1120]{2,1,0:T(8,128)(2,1)}, u32[]{:S(2)}, u32[]{:S(2)}) collective-permute-start(bf16[4,32,1120]{2,1,0:T(8,128)(2,1)} %bitcast.173), channel_id=1, source_target_pairs={{0,1},{1,2},{2,3},{3,4},{4,5},{5,6},{6,7},{7,8},{8,9},{9,10},{10,1... | collective-permute-start | bytes 860168 | tf_op jit(solution)/shard_map/ppermute | solution.py:27
  74.0 1.4 broadcast_in_dim.22
  75.3 7.4 %all-to-all-start.1 = ((bf16[16,136,384]{2,1,0:T(8,128)(2,1)}), bf16[16,136,384]{2,1,0:T(8,128)(2,1)S(1)}, u32[]{:S(2)}, u32[]{:S(2)}) async-start(bf16[16,136,384]{2,1,0:T(8,128)(2,1)} %broadcast_in_dim.22), calls=%async_computation.1 | async-start | bytes 3342336 | tf_op jit(solution)/shard_map/all_to_all | solution.py:32
  82.7 1.8 broadcast_multiply_fusion
  84.6 2.2 reshape.459
  86.8 1.5 copy.128
  88.3 1.4 copy.127
  89.7 4.1 %maximum_maximum_fusion = bf16[4,2,64,1120]{3,1,2,0:T(2,128)(2,1)S(1)} fusion(bf16[4,1,32,1120]{3,1,2,0:T(2,128)(2,1)S(1)} %copy.128, bf16[4,1,32,1120]{3,1,2,0:T(2,128)(2,1)S(1)} %copy.127, bf16[2,2,32,1120]{3,1,2,0:T(2,128)(2,1)S(1)} %copy-done.14, bf16[2,2,32,1120]{3,1,2,0:T(2,128)(2,1)S(1)} %bitcast.188), kind=kLoop, calls=%fused_computation.43 | loop fusion | flops 4587520 | bytes 2293760 | tf_op jit(solution)/shard_map/concatenate | solution.py:197
  93.8 1.2 copy.129
  95.0 2.4 %collective-permute-start.4 = (bf16[16,136,384]{2,1,0:T(8,128)(2,1)S(1)}, bf16[16,136,384]{2,1,0:T(8,128)(2,1)}, u32[]{:S(2)}, u32[]{:S(2)}) collective-permute-start(bf16[16,136,384]{2,1,0:T(8,128)(2,1)S(1)} %all-to-all-done), channel_id=1, source_target_pairs={{0,1},{1,0},{2,3},{3,2},{4,5},{5,4},{6,7},{7,6},{8,9},{9,8},{10,11... | collective-permute-start | bytes 5013512 | tf_op jit(solution)/shard_map/ppermute | solution.py:22
  98.2 9.3 %all-to-all-done.1 = bf16[16,136,384]{2,1,0:T(8,128)(2,1)S(1)} async-done(((bf16[16,136,384]{2,1,0:T(8,128)(2,1)}), bf16[16,136,384]{2,1,0:T(8,128)(2,1)S(1)}, u32[]{:S(2)}, u32[]{:S(2)}) %all-to-all-start.1) | async-done | bytes 1671200 | tf_op jit(solution)/shard_map/all_to_all | solution.py:32
  107.5 1.9 collective-permute-start.5
  109.4 3.2 %fusion.6 = bf16[512,1280]{1,0:T(8,128)(2,1)S(1)} fusion(bf16[512,1120]{1,0:T(8,128)(2,1)} %bitcast.196, s32[1280]{0:T(1024)S(1)} %copy-done.22), kind=kOutput, calls=%fused_computation.12 | convolution fusion | flops 1470095360 | bytes 2462720 | tf_op jit(solution)/shard_map/dot_general | solution.py:50
  113.7 1.4 fusion.48
  116.2 6.7 %all-to-all-start.3 = ((bf16[16,80,384]{2,1,0:T(8,128)(2,1)}), bf16[16,80,384]{2,1,0:T(8,128)(2,1)}, u32[]{:S(2)}, u32[]{:S(2)}) async-start(bf16[16,80,384]{2,1,0:T(8,128)(2,1)} %broadcast_in_dim.27), calls=%async_computation.3 | async-start | bytes 1966080 | tf_op jit(solution)/shard_map/all_to_all | solution.py:32
  124.1 1.4 pad_maximum_fusion
  126.3 1.3 convolution_add_fusion.5
  127.6 1.9 slice.184
  129.4 9.9 %all-to-all-done.3 = bf16[16,80,384]{2,1,0:T(8,128)(2,1)} async-done(((bf16[16,80,384]{2,1,0:T(8,128)(2,1)}), bf16[16,80,384]{2,1,0:T(8,128)(2,1)}, u32[]{:S(2)}, u32[]{:S(2)}) %all-to-all-start.3) | async-done | bytes 983072 | tf_op jit(solution)/shard_map/all_to_all | solution.py:32
  139.3 2.2 collective-permute-start.6
  142.6 1.6 fusion.44
  145.4 1.6 select_bitcast_fusion.1
  148.7 1.4 fusion.53
  150.1 2.9 %fusion.1 = bf16[512,2304]{1,0:T(8,128)(2,1)} fusion(f32[512,2304]{1,0:T(8,128)S(1)} %fusion.53, bf16[2304,384]{1,0:T(8,128)(2,1)S(1)} %bitcast.183, pred[]{:T(512)S(6)} %eq.139, bf16[512,768]{1,0:T(8,128)(2,1)S(1)} %fusion.13), kind=kOutput, calls=%fused_computation.3 | convolution fusion | flops 908525568 | bytes 9633793 | tf_op jit(solution)/shard_map/dot_general | solution.py:54
  153.0 4.3 %copy.132 = bf16[512,2304]{0,1:T(8,128)(2,1)} copy(bf16[512,2304]{1,0:T(8,128)(2,1)} %fusion.1) | data formatting | bytes 4718592 | tf_op jit(solution)/shard_map/convert_element_type | solution.py:229
  157.3 7.0 %reshape_reshape.3 = bf16[8,64,3,12,64]{1,0,4,3,2:T(8,128)(2,1)} reshape(bf16[512,2304]{0,1:T(8,128)(2,1)} %copy.132) | data formatting | bytes 4718592 | tf_op jit(solution)/shard_map/reshape;reshape | solution.py:78
  164.4 1.8 fusion.4
  166.2 1.8 fusion.2
  168.0 1.3 select_bitcast_fusion.5
  170.5 1.5 fusion.3
  172.0 1.6 fusion.5
  173.7 2.0 copy.164
  175.6 2.7 %multiply_exponential_fusion = f32[8,12,32,64]{3,2,1,0:T(8,128)S(1)} fusion(bf16[8,64,12,64]{1,0,3,2:T(8,128)(2,1)} %fusion.5, bf16[8,32,12,64]{1,0,3,2:T(8,128)(2,1)} %fusion.3, f32[12]{0:T(128)S(1)} %copy-done.27), kind=kOutput, calls=%fused_computation.34 | convolution fusion | flops 25362432 | bytes 1966128 | tf_op jit(solution)/shard_map/bihd,bjhd->bhij/dot_general | solution.py:82
  178.4 3.0 %fusion.27 = bf16[8,32,12,64]{3,1,2,0:T(8,128)(2,1)} fusion(bf16[8,64,1,12,64]{4,1,3,0,2:T(8,128)(2,1)} %copy.164, f32[8,12,32,64]{3,2,1,0:T(8,128)S(1)} %multiply_exponential_fusion), kind=kOutput, calls=%fused_computation.38 | convolution fusion | flops 25758784 | bytes 1966080 | tf_op jit(solution)/shard_map/bhij,bjhd->bihd/dot_general | solution.py:85
  181.3 1.5 copy.136
  186.2 4.9 %all-to-all-start.2 = ((bf16[16,4,4,768]{3,2,1,0:T(4,128)(2,1)}), bf16[16,4,4,768]{3,2,1,0:T(4,128)(2,1)S(1)}, u32[]{:S(2)}, u32[]{:S(2)}) async-start(bf16[16,4,4,768]{3,2,1,0:T(4,128)(2,1)} %bitcast.36), calls=%async_computation.2 | async-start | bytes 786432 | tf_op jit(solution)/shard_map/all_to_all | solution.py:242
  191.2 1.5 reshape.449
  192.7 1.5 reshape.451
  194.1 6.4 %all-to-all-done.2 = bf16[16,4,4,768]{3,2,1,0:T(4,128)(2,1)S(1)} async-done(((bf16[16,4,4,768]{3,2,1,0:T(4,128)(2,1)}), bf16[16,4,4,768]{3,2,1,0:T(4,128)(2,1)S(1)}, u32[]{:S(2)}, u32[]{:S(2)}) %all-to-all-start.2) | async-done | bytes 393248 | tf_op jit(solution)/shard_map/all_to_all | solution.py:242
  202.6 1.8 fusion.131
  211.9 11.5 %all_to_all.25 = bf16[16,2,4,768]{3,1,2,0:T(2,128)(2,1)S(1)} all-to-all(bf16[16,2,4,768]{3,1,2,0:T(2,128)(2,1)S(1)} %copy.149), channel_id=1, replica_groups=mesh['x'=4,'y'=4,'zh'=2,'zl'=8,'core'=2] {'x','y'}, dimensions={0} | all-to-all | bytes 393216 | tf_op jit(solution)/shard_map/all_to_all | solution.py:273
  (166 shorter events, 35.5 us)
Async XLA Ops:
  0.0 47.3 %copy-start = (bf16[16,70]{1,0:T(8,128)(2,1)S(1)}, bf16[16,70]{1,0:T(8,128)(2,1)}, u32[]{:S(2)}) copy-start(bf16[16,70]{1,0:T(8,128)(2,1)} %param.18) | copy-start | bytes 6724
  2.1 43.4 %collective-permute-start.7 = (f32[5,256]{1,0:T(8,128)S(1)}, f32[5,256]{1,0:T(8,128)S(1)}, u32[]{:S(2)}, u32[]{:S(2)}) collective-permute-start(f32[5,256]{1,0:T(8,128)S(1)} %stack.18), channel_id=1, source_target_pairs={{0,16},{16,0},{1,17},{17,1},{2,18},{18,2},{3,19},{19,3},{4,20},{20... | collective-permute-start | bytes 15368 | tf_op jit(solution)/shard_map/ppermute | solution.py:22
  18.9 55.0 %collective-permute-start.3 = (bf16[176,384]{1,0:T(8,128)(2,1)S(1)}, bf16[176,384]{1,0:T(8,128)(2,1)S(1)}, u32[]{:S(2)}, u32[]{:S(2)}) collective-permute-start(bf16[176,384]{1,0:T(8,128)(2,1)S(1)} %slice_select_fusion), channel_id=1, source_target_pairs={{0,16},{16,0},{1,17},{17,1},{2,18},{18,2},{3,19},{19,3},{4,20},{20... | collective-permute-start | bytes 405512 | tf_op jit(solution)/shard_map/ppermute | solution.py:22
  22.1 44.9 %copy-start.8 = (bf16[2,8,2,4,1120]{4,2,3,1,0:T(2,128)(2,1)}, bf16[2,8,2,4,1120]{4,2,3,1,0:T(2,128)(2,1)S(1)}, u32[]{:S(2)}) copy-start(bf16[2,8,2,4,1120]{4,2,3,1,0:T(2,128)(2,1)S(1)} %copy.126) | copy-start | bytes 860164
  22.1 44.9 %collective-permute-start = (bf16[2,2,32,1120]{3,1,2,0:T(2,128)(2,1)S(1)}, bf16[2,2,32,1120]{3,1,2,0:T(2,128)(2,1)S(1)}, u32[]{:S(2)}, u32[]{:S(2)}) collective-permute-start(bf16[2,2,32,1120]{3,1,2,0:T(2,128)(2,1)S(1)} %bitcast.186), channel_id=1, source_target_pairs={{0,16},{16,0},{1,17},{17,1},{2,18},{18,2},{3,19},{19,3},{4,20},{20... | collective-permute-start | bytes 860168 | tf_op jit(solution)/shard_map/ppermute | solution.py:22
  36.1 37.8 %all-to-all-start = ((bf16[16,136,384]{2,1,0:T(8,128)(2,1)}), bf16[16,136,384]{2,1,0:T(8,128)(2,1)S(1)}, u32[]{:S(2)}, u32[]{:S(2)}) async-start(bf16[16,136,384]{2,1,0:T(8,128)(2,1)} %broadcast_in_dim.21), calls=%async_computation | async-start | bytes 3342336 | tf_op jit(solution)/shard_map/all_to_all | solution.py:32
  46.1 23.5 %copy-start.18 = (s32[2,1,256]{2,1,0:T(1,128)}, s32[2,1,256]{2,1,0:T(1,128)S(1)}, u32[]{:S(2)}) copy-start(s32[2,1,256]{2,1,0:T(1,128)S(1)} %get-tuple-element.35) | copy-start | bytes 6148
  46.1 23.5 %copy-start.20 = (s32[2,1,256]{2,1,0:T(1,128)}, s32[2,1,256]{2,1,0:T(1,128)S(1)}, u32[]{:S(2)}) copy-start(s32[2,1,256]{2,1,0:T(1,128)S(1)} %get-tuple-element.37) | copy-start | bytes 6148
  67.0 2.6 %copy-start.13 = (bf16[2,2,32,1120]{3,1,2,0:T(2,128)(2,1)}, bf16[2,2,32,1120]{3,1,2,0:T(2,128)(2,1)S(1)}, u32[]{:S(2)}) copy-start(bf16[2,2,32,1120]{3,1,2,0:T(2,128)(2,1)S(1)} %collective-permute-done) | copy-start | bytes 860164
  69.6 17.2 %collective-permute-start.2 = (bf16[4,32,1120]{2,1,0:T(8,128)(2,1)}, bf16[4,32,1120]{2,1,0:T(8,128)(2,1)}, u32[]{:S(2)}, u32[]{:S(2)}) collective-permute-start(bf16[4,32,1120]{2,1,0:T(8,128)(2,1)} %bitcast.172), channel_id=1, source_target_pairs={{0,15},{1,0},{2,1},{3,2},{4,3},{5,4},{6,5},{7,6},{8,7},{9,8},{10,9... | collective-permute-start | bytes 860168 | tf_op jit(solution)/shard_map/ppermute | solution.py:27
  71.5 16.8 %collective-permute-start.1 = (bf16[4,32,1120]{2,1,0:T(8,128)(2,1)}, bf16[4,32,1120]{2,1,0:T(8,128)(2,1)}, u32[]{:S(2)}, u32[]{:S(2)}) collective-permute-start(bf16[4,32,1120]{2,1,0:T(8,128)(2,1)} %bitcast.173), channel_id=1, source_target_pairs={{0,1},{1,2},{2,3},{3,4},{4,5},{5,6},{6,7},{7,8},{8,9},{9,10},{10,1... | collective-permute-start | bytes 860168 | tf_op jit(solution)/shard_map/ppermute | solution.py:27
  73.9 1.4 copy-start.17
  75.3 32.2 %all-to-all-start.1 = ((bf16[16,136,384]{2,1,0:T(8,128)(2,1)}), bf16[16,136,384]{2,1,0:T(8,128)(2,1)S(1)}, u32[]{:S(2)}, u32[]{:S(2)}) async-start(bf16[16,136,384]{2,1,0:T(8,128)(2,1)} %broadcast_in_dim.22), calls=%async_computation.1 | async-start | bytes 3342336 | tf_op jit(solution)/shard_map/all_to_all | solution.py:32
  82.7 4.0 %copy-start.23 = (s32[512]{0:T(512)S(1)}, s32[512]{0:T(512)}, u32[]{:S(2)}) copy-start(s32[512]{0:T(512)} %get-tuple-element.42) | copy-start | bytes 6148
  86.8 2.9 %copy-start.9 = (bf16[2,8,2,4,1120]{4,2,3,1,0:T(2,128)(2,1)S(1)}, bf16[2,8,2,4,1120]{4,2,3,1,0:T(2,128)(2,1)}, u32[]{:S(2)}) copy-start(bf16[2,8,2,4,1120]{4,2,3,1,0:T(2,128)(2,1)} %copy-done.8) | copy-start | bytes 860164
  86.8 3.0 %copy-start.14 = (bf16[2,2,32,1120]{3,1,2,0:T(2,128)(2,1)S(1)}, bf16[2,2,32,1120]{3,1,2,0:T(2,128)(2,1)}, u32[]{:S(2)}) copy-start(bf16[2,2,32,1120]{3,1,2,0:T(2,128)(2,1)} %copy-done.13) | copy-start | bytes 860164
  93.8 15.6 %copy-start.22 = (s32[1280]{0:T(1024)S(1)}, s32[1280]{0:T(1024)}, u32[]{:S(2)}) copy-start(s32[1280]{0:T(1024)} %fusion.109) | copy-start | bytes 15364
  95.0 32.6 %collective-permute-start.4 = (bf16[16,136,384]{2,1,0:T(8,128)(2,1)S(1)}, bf16[16,136,384]{2,1,0:T(8,128)(2,1)}, u32[]{:S(2)}, u32[]{:S(2)}) collective-permute-start(bf16[16,136,384]{2,1,0:T(8,128)(2,1)S(1)} %all-to-all-done), channel_id=1, source_target_pairs={{0,1},{1,0},{2,3},{3,2},{4,5},{5,4},{6,7},{7,6},{8,9},{9,8},{10,11... | collective-permute-start | bytes 5013512 | tf_op jit(solution)/shard_map/ppermute | solution.py:22
  107.5 34.0 %collective-permute-start.5 = (bf16[16,136,384]{2,1,0:T(8,128)(2,1)S(1)}, bf16[16,136,384]{2,1,0:T(8,128)(2,1)}, u32[]{:S(2)}, u32[]{:S(2)}) collective-permute-start(bf16[16,136,384]{2,1,0:T(8,128)(2,1)S(1)} %all-to-all-done.1), channel_id=1, source_target_pairs={{0,1},{1,0},{2,3},{3,2},{4,5},{5,4},{6,7},{7,6},{8,9},{9,8},{10,11... | collective-permute-start | bytes 5013512 | tf_op jit(solution)/shard_map/ppermute | solution.py:22
  112.6 1.1 copy-start.4
  116.2 23.1 %all-to-all-start.3 = ((bf16[16,80,384]{2,1,0:T(8,128)(2,1)}), bf16[16,80,384]{2,1,0:T(8,128)(2,1)}, u32[]{:S(2)}, u32[]{:S(2)}) async-start(bf16[16,80,384]{2,1,0:T(8,128)(2,1)} %broadcast_in_dim.27), calls=%async_computation.3 | async-start | bytes 1966080 | tf_op jit(solution)/shard_map/all_to_all | solution.py:32
  124.1 1.7 copy-start.5
  124.1 2.2 copy-start.7
  129.4 14.8 %copy-start.6 = (bf16[512,1280]{1,0:T(8,128)(2,1)S(1)}, bf16[512,1280]{1,0:T(8,128)(2,1)}, u32[]{:S(2)}) copy-start(bf16[512,1280]{1,0:T(8,128)(2,1)} %copy-done.4) | copy-start | bytes 3932164
  139.3 5.0 %copy-start.11 = (bf16[16,40,384]{2,1,0:T(8,128)(2,1)S(1)}, bf16[16,40,384]{2,1,0:T(8,128)(2,1)}, u32[]{:S(2)}) copy-start(bf16[16,40,384]{2,1,0:T(8,128)(2,1)} %slice.184) | copy-start | bytes 1474564
  139.3 5.0 %copy-start.12 = (bf16[512,384]{1,0:T(8,128)(2,1)S(1)}, bf16[512,384]{1,0:T(8,128)(2,1)}, u32[]{:S(2)}) copy-start(bf16[512,384]{1,0:T(8,128)(2,1)} %convolution_add_fusion.5) | copy-start | bytes 1179652
  139.3 53.4 %collective-permute-start.6 = (bf16[16,80,384]{2,1,0:T(8,128)(2,1)}, bf16[16,80,384]{2,1,0:T(8,128)(2,1)}, u32[]{:S(2)}, u32[]{:S(2)}) collective-permute-start(bf16[16,80,384]{2,1,0:T(8,128)(2,1)} %all-to-all-done.3), channel_id=1, source_target_pairs={{0,1},{1,0},{2,3},{3,2},{4,5},{5,4},{6,7},{7,6},{8,9},{9,8},{10,11... | collective-permute-start | bytes 2949128 | tf_op jit(solution)/shard_map/ppermute | solution.py:22
  147.3 1.5 copy-start.3
  168.0 2.5 %copy-start.2 = (bf16[8,64,3,12,64]{1,0,4,3,2:T(8,128)(2,1)S(1)}, bf16[8,64,3,12,64]{1,0,4,3,2:T(8,128)(2,1)}, u32[]{:S(2)}) copy-start(bf16[8,64,3,12,64]{1,0,4,3,2:T(8,128)(2,1)} %reshape_reshape.3) | copy-start | bytes 7077892
  172.0 1.6 slice-start
  173.7 2.0 copy-start.27
  182.8 1.1 copy-start.10
  185.0 6.1 %copy-start.19 = (s32[2,1,256]{2,1,0:T(1,128)S(1)}, s32[2,1,256]{2,1,0:T(1,128)}, u32[]{:S(2)}) copy-start(s32[2,1,256]{2,1,0:T(1,128)} %copy-done.18) | copy-start | bytes 6148
  185.0 6.1 %copy-start.21 = (s32[2,1,256]{2,1,0:T(1,128)S(1)}, s32[2,1,256]{2,1,0:T(1,128)}, u32[]{:S(2)}) copy-start(s32[2,1,256]{2,1,0:T(1,128)} %copy-done.20) | copy-start | bytes 6148
  185.0 6.1 %copy-start.26 = (f32[2,1,256]{2,1,0:T(1,128)S(1)}, f32[2,1,256]{2,1,0:T(1,128)}, u32[]{:S(2)}) copy-start(f32[2,1,256]{2,1,0:T(1,128)} %get-tuple-element.34) | copy-start | bytes 6148
  185.0 6.2 %copy-start.24 = (s32[512]{0:T(512)S(1)}, s32[512]{0:T(512)}, u32[]{:S(2)}) copy-start(s32[512]{0:T(512)} %get-tuple-element.44) | copy-start | bytes 6148
  186.2 14.4 %all-to-all-start.2 = ((bf16[16,4,4,768]{3,2,1,0:T(4,128)(2,1)}), bf16[16,4,4,768]{3,2,1,0:T(4,128)(2,1)S(1)}, u32[]{:S(2)}, u32[]{:S(2)}) async-start(bf16[16,4,4,768]{3,2,1,0:T(4,128)(2,1)} %bitcast.36), calls=%async_computation.2 | async-start | bytes 786432 | tf_op jit(solution)/shard_map/all_to_all | solution.py:242
  202.5 1.8 copy-start.25
  202.5 1.9 copy-start.16
  202.6 2.9 %copy-start.15 = (f32[64,64]{1,0:T(8,128)S(1)}, f32[64,64]{1,0:T(8,128)}, u32[]{:S(2)}) copy-start(f32[64,64]{1,0:T(8,128)} %copy.140) | copy-start | bytes 49156
  223.6 1.7 copy-start.1

commit v2 on v1

v2 whole, which is shorter than its diff:
```python
import functools

import numpy as np
import jax
import jax.numpy as jnp
from jax import lax
from jax.experimental import pallas as pl
from jax.experimental.pallas import tpu as pltpu
from jax.sharding import Mesh, PartitionSpec as P

PANE_SIDE = 8
HALF = PANE_SIDE // 2
NS_ITERS = 5
PLANE = ("x", "y")
MEM = ("x", "y", "zh")
TILE = ("zl", "core")
BLOCK = 40
SHARD = 35
SIDE = 16 * BLOCK
HEAD = 64
GROUP = 4 * HEAD
OWN = PANE_SIDE * HALF

eps_norm = 1e-05
normalizing_guard = 1e-06
bf16 = jnp.bfloat16
f32 = jnp.float32


def swapped(value, axis):
    return lax.ppermute(value, axis, [(0, 1), (1, 0)])


def passed_along(value, axis, by):
    devices = lax.axis_size(axis)
    return lax.ppermute(value, axis, [(i, (i + by) % devices) for i in range(devices)])


def copies_of(part):
    return lax.optimization_barrier(jnp.broadcast_to(part[None], (16,) + part.shape))


def exchanged(blocks):
    return lax.all_to_all(blocks, PLANE, split_axis=0, concat_axis=0, tiled=True)


def times(left, right):
    return jnp.dot(left, right, preferred_element_type=f32)


def times_t(left, right):
    return lax.dot_general(left, right, (((1,), (1,)), ((), ())), preferred_element_type=f32)


def normalized(values):
    center = values - jnp.mean(values, axis=-1, keepdims=True)
    spread = jnp.mean(center * center, axis=-1, keepdims=True)
    return center * lax.rsqrt(spread + eps_norm)


def in_order(flag, first, second, axis):
    low = jnp.where(flag == 0, first, second)
    high = jnp.where(flag == 0, second, first)
    return jnp.concatenate([low, high], axis=axis)


def halves(flag, value):
    width = value.shape[-1] // 2
    low, high = value[..., :width], value[..., width:]
    return jnp.where(flag == 0, low, high), jnp.where(flag == 0, high, low)


def two_parts(value):
    high = value.astype(bf16)
    return high, (value - high.astype(f32)).astype(bf16)


def three_parts(value):
    high = value.astype(bf16)
    rest = value - high.astype(f32)
    middle = rest.astype(bf16)
    return high, middle, (rest - middle.astype(f32)).astype(bf16)


def iota(shape, axis):
    return lax.broadcasted_iota(jnp.int32, shape, axis)


def one_hot(order, width):
    return jnp.asarray(np.asarray(order)[:, None] == np.arange(width)[None, :], bf16)


def attention_kernel(
    flags, own_x, west_x, east_x, e_mine, e_part, w_mine, w_part, scale, hidden_out, context_out
):
    core, zh = flags[0], flags[1]
    members = own_x.shape[2] // OWN
    x = jnp.concatenate(
        [own_x[0, 0], own_x[0, 1], west_x[0], east_x[0]], axis=0
    )
    x_own, x_other = halves(zh, x)
    x = jnp.concatenate([x_own, x_other], axis=1)
    hidden = in_order(core, times(x, e_mine[...]), times(x, e_part[...]), 1).astype(bf16)
    normed = normalized(hidden.astype(f32)).astype(bf16)
    n_mine, n_part = halves(core, normed)
    own_rows = 2 * members * OWN
    hidden_out[...] = hidden[:own_rows]
    width = hidden.shape[1]

    same = (iota((GROUP, GROUP), 0) // HEAD) == (iota((GROUP, GROUP), 1) // HEAD)
    ones = same.astype(bf16)
    lane_head = iota((PANE_SIDE * PANE_SIDE, GROUP), 1) // HEAD

    def projected(left, right, start):
        rows = pl.ds(start, GROUP)
        return (times_t(left, w_mine[rows, :]) + times_t(right, w_part[rows, :])).astype(bf16)

    def unit(values):
        values = values.astype(f32)
        high, low = two_parts(values * values)
        total = times(high, ones) + times(low, ones)
        return (values * lax.rsqrt(total + normalizing_guard)).astype(bf16)

    def diagonal(rows):
        zero = jnp.zeros_like(rows)
        return jnp.concatenate(
            [jnp.where(lane_head == h, rows, zero) for h in range(4)], axis=0
        )

    def pane_rows(values, w, m):
        own = values[(w * members + m) * OWN : (w * members + m + 1) * OWN]
        start = own_rows + (w * members + m) * OWN
        return jnp.concatenate([own, values[start : start + OWN]], axis=0)

    for g in range(width // GROUP):
        at = g * GROUP
        query = unit(projected(n_mine[:own_rows], n_part[:own_rows], at))
        key_rows = unit(projected(n_mine, n_part, width + at))
        value_rows = projected(n_mine, n_part, 2 * width + at)
        scores = []
        for w in range(2):
            for m in range(members):
                first = (w * members + m) * OWN
                scores.append(
                    times_t(query[first : first + OWN], diagonal(pane_rows(key_rows, w, m)))
                )
        weights = jnp.exp(jnp.concatenate(scores, axis=0) * scale[:, at : at + GROUP]).astype(bf16)
        total = times(weights, ones)
        mixed = []
        for w in range(2):
            for m in range(members):
                first = (w * members + m) * OWN
                mixed.append(
                    times(weights[first : first + OWN], diagonal(pane_rows(value_rows, w, m)))
                )
        context_out[:, at : at + GROUP] = (jnp.concatenate(mixed, axis=0) / total).astype(bf16)


def attention(flags, own_x, west_x, east_x, e_mine, e_part, w_mine, w_part, scale):
    groups, panes, pane_own, wide = own_x.shape
    rows = panes * pane_own
    width = 2 * e_mine.shape[1]

    def whole(array):
        return pl.BlockSpec(array.shape, lambda i: (0,) * array.ndim)

    return pl.pallas_call(
        attention_kernel,
        grid=(groups,),
        in_specs=[
            pl.BlockSpec(memory_space=pltpu.SMEM),
            pl.BlockSpec((1, panes, pane_own, wide), lambda i: (i, 0, 0, 0)),
            pl.BlockSpec((1,) + west_x.shape[1:], lambda i: (i, 0, 0)),
            pl.BlockSpec((1,) + east_x.shape[1:], lambda i: (i, 0, 0)),
            whole(e_mine),
            whole(e_part),
            whole(w_mine),
            whole(w_part),
            whole(scale),
        ],
        out_specs=[pl.BlockSpec((rows, width), lambda i: (i, 0))] * 2,
        out_shape=[jax.ShapeDtypeStruct((groups * rows, width), bf16)] * 2,
        compiler_params=pltpu.CompilerParams(vmem_limit_bytes=40 * 1024 * 1024),
        name="attention",
    )(flags, own_x, west_x, east_x, e_mine, e_part, w_mine, w_part, scale)


def latent_kernel(flags, context, hidden, order, t_mine, t_part, latent_out):
    c_mine, c_part = halves(flags[0], context[...])
    outs = t_mine.shape[1] - 16

    def combiner(ref):
        return ref[:, :outs, :].reshape(16 * outs, ref.shape[2])

    mixed = times_t(c_mine, combiner(t_mine)) + times_t(c_part, combiner(t_part))
    latent = normalized(hidden[...].astype(f32) + mixed).astype(bf16)
    latent_out[...] = times(order[...], latent).astype(bf16)


def latent_rows(flags, context, hidden, order, t_mine, t_part):
    vmem = pl.BlockSpec(memory_space=pltpu.VMEM)
    return pl.pallas_call(
        latent_kernel,
        in_specs=[pl.BlockSpec(memory_space=pltpu.SMEM)] + [vmem] * 5,
        out_specs=vmem,
        out_shape=jax.ShapeDtypeStruct(context.shape, bf16),
        compiler_params=pltpu.CompilerParams(vmem_limit_bytes=32 * 1024 * 1024),
        name="latent",
    )(flags, context, hidden, order, t_mine, t_part)


def product(left, right):
    l_high, l_low = two_parts(left)
    r_high, r_low = two_parts(right)
    return times(
        jnp.concatenate([l_high, l_high, l_low], axis=1),
        jnp.concatenate([r_high, r_low, r_high], axis=0),
    )


def product_t(left, right):
    l_high, l_low = two_parts(left)
    r_high, r_low = two_parts(right)
    return times_t(
        jnp.concatenate([l_high, l_high, l_low], axis=1),
        jnp.concatenate([r_high, r_low, r_high], axis=1),
    )


def analysis_kernel(flags, moved, order, back_order, obs, t_mine, t_part, posterior_out):
    core, zh = flags[0], flags[1]
    width = moved.shape[1]
    latent = times(order[...], moved[...]).astype(bf16)
    members = latent.shape[0] // HALF
    l_mine, l_part = halves(core, latent)
    outs = t_mine.shape[1] - 16

    def readers(ref):
        return ref[:, outs:, :].reshape(16 * 16, ref.shape[2])

    seen = times_t(l_mine, readers(t_mine)) + times_t(l_part, readers(t_part))
    places = seen.shape[1]
    eye = (iota((members, members), 0) == iota((members, members), 1)).astype(f32)
    systems, drives = [], []
    for block in range(2):
        ens = [seen[(2 * block + t) * members : (2 * block + t + 1) * members] for t in range(2)]
        mean = [jnp.mean(e, axis=0, keepdims=True) for e in ens]
        pert = jnp.concatenate([e - m for e, m in zip(ens, mean)], axis=1)
        mean = jnp.concatenate(mean, axis=1)
        for r in range(2):
            weight = obs[block, r : r + 1, :]
            read = obs[block, 2 + r : 3 + r, :]
            gram = product_t(pert * weight, pert)
            drives.append(jnp.sum(pert * (read - weight * mean), axis=1, keepdims=True))
            systems.append(eye + gram / (members - 1.0))
    bounds = [
        jnp.max(jnp.sum(jnp.abs(s), axis=1, keepdims=True), axis=0, keepdims=True) for s in systems
    ]
    iterates = [s / b for s, b in zip(systems, bounds)]
    factors = [1.5 * eye - 0.5 * y for y in iterates]
    iterates = [product(y, f) for y, f in zip(iterates, factors)]
    roots = factors
    for step in range(1, NS_ITERS):
        factors = [1.5 * eye - 0.5 * product(z, y) for z, y in zip(roots, iterates)]
        if step + 1 < NS_ITERS:
            iterates = [product(y, f) for y, f in zip(iterates, factors)]
        roots = [product(f, z) for f, z in zip(factors, roots)]
    results = []
    for region in range(2 * 2):
        root = roots[region] * lax.rsqrt(bounds[region])
        inner = jnp.sum(root * drives[region], axis=0, keepdims=True)
        mean_weight = jnp.sum(root * inner, axis=1, keepdims=True) / (members - 1.0)
        transform = root + mean_weight
        own = jnp.where(zh == 0, transform[:, : members // 2], transform[:, members // 2 :])
        values = latent[region * members : (region + 1) * members]
        center = jnp.mean(values.astype(f32), axis=0, keepdims=True)
        own_t = own.T
        high, middle, low = three_parts(own_t)
        left = jnp.concatenate([high, middle, low], axis=1)
        moved_part = times(left, jnp.concatenate([values] * 3, axis=0))
        share = 1.0 - jnp.sum(own_t, axis=1, keepdims=True)
        results.append((moved_part + share * center).astype(bf16))
    posterior = jnp.concatenate(results, axis=0)
    posterior_out[...] = times(back_order[...], posterior).astype(bf16)


def analysis(flags, moved, order, back_order, obs, t_mine, t_part):
    vmem = pl.BlockSpec(memory_space=pltpu.VMEM)
    return pl.pallas_call(
        analysis_kernel,
        in_specs=[pl.BlockSpec(memory_space=pltpu.SMEM)] + [vmem] * 6,
        out_specs=vmem,
        out_shape=jax.ShapeDtypeStruct((back_order.shape[0], moved.shape[1]), bf16),
        compiler_params=pltpu.CompilerParams(vmem_limit_bytes=32 * 1024 * 1024),
        name="analysis",
    )(flags, moved, order, back_order, obs, t_mine, t_part)


def packed_obs(grid, domain, channel, reading, noise, width):
    rows = [grid.astype(bf16), domain.astype(bf16), channel.astype(bf16)]
    rows += list(three_parts(reading)) + list(three_parts(noise))
    table = jnp.stack(rows)
    return jnp.pad(table, ((0, 16 - len(rows)), (0, width - table.shape[1])))


def weighted_places(table, count):
    table = table[:, :, :count].astype(f32)
    grid = table[:, 0].astype(jnp.int32)
    domain = table[:, 1].astype(jnp.int32)
    channel = table[:, 2].astype(jnp.int32)
    reading = table[:, 3] + (table[:, 4] + table[:, 5])
    noise = table[:, 6] + (table[:, 7] + table[:, 8])
    token = grid // 16
    distance = (token - domain).astype(f32)
    weight = jnp.exp(-0.5 * distance * distance) / (noise * noise)
    region = (domain[:, None, :] == jnp.arange(2, dtype=jnp.int32)[None, :, None]).astype(f32)
    weight = region * weight[:, None, :]
    left = jnp.concatenate([weight, weight * reading[:, None, :]], axis=1)
    place = grid * 16 + channel
    pick = (place[:, :, None] == jnp.arange(512, dtype=jnp.int32)[None, None, :]).astype(f32)
    return jnp.einsum("bcj,bjp->bcp", left, pick, precision=lax.Precision.HIGHEST)


def per_device(
    starting_ensemble,
    patch_lifting,
    query_keyvalue_lift,
    output_combiner,
    decoder_linear_map,
    cosine_logit_scale,
    sensor_variable_loadings,
    sensor_gridpoint,
    sensor_domain_index,
    sensor_channel_list,
    sensor_reading,
    sensor_noise_deviation,
):
    members, rows, cols, feats = starting_ensemble.shape
    width = patch_lifting.shape[1]
    core = lax.axis_index("core")
    zh = lax.axis_index("zh")
    flags = jnp.stack([core, zh]).astype(jnp.int32)

    fill = ((0, BLOCK - SHARD), (0, 0))
    packed = jnp.concatenate(
        [
            jnp.pad(patch_lifting, fill),
            query_keyvalue_lift.T,
            output_combiner.T,
            jnp.pad(decoder_linear_map.T, fill),
        ],
        axis=0,
    )
    mine, _ = halves(core, packed)
    q_end = BLOCK + query_keyvalue_lift.shape[1]
    o_end = q_end + output_combiner.shape[1]
    theirs = swapped(mine, "zh")
    own_front = exchanged(copies_of(mine[:q_end]))
    other_copies, own_front = lax.optimization_barrier((copies_of(theirs[:q_end]), own_front))
    other_front = exchanged(other_copies)
    combiner = in_order(zh, mine[q_end:o_end], theirs[q_end:o_end], 0)
    decoder = in_order(zh, mine[o_end:], theirs[o_end:], 0)
    loadings = jnp.pad(
        sensor_variable_loadings.reshape(16, 2, SHARD), ((0, 0), (0, 0), (0, BLOCK - SHARD))
    ).reshape(16, 2 * BLOCK)
    readers = times(loadings, decoder).astype(bf16)
    tail_copies, other_front = lax.optimization_barrier(
        (copies_of(jnp.concatenate([combiner, readers], axis=0)), other_front)
    )
    tail_mine = exchanged(tail_copies)
    dec_mine = lax.all_gather(decoder, PLANE, axis=0, tiled=True)
    own_front_p = swapped(own_front, "core")
    other_front_p = swapped(other_front, "core")
    tail_part = swapped(tail_mine, "core")

    token = np.arange(members * rows * cols).reshape(members, rows, 2, HALF)
    source = (np.arange(16)[None, :, None] * 2 + np.arange(2)[:, None, None]) * SHARD + np.arange(
        BLOCK
    )[None, None, :]
    source = np.where(np.arange(BLOCK)[None, None, :] < SHARD, source, -1).reshape(-1)
    pick_rows = one_hot(token.transpose(2, 0, 1, 3).reshape(-1), token.size)
    pick_cols = (jnp.arange(feats, dtype=jnp.int32)[:, None] == jnp.asarray(source, jnp.int32)[None, :]).astype(bf16)
    states = times(pick_rows, starting_ensemble.reshape(-1, feats)).astype(bf16)
    states = times(states, pick_cols).astype(bf16)
    table = packed_obs(
        sensor_gridpoint.reshape(-1),
        sensor_domain_index.reshape(-1),
        sensor_channel_list.reshape(-1),
        sensor_reading.reshape(-1),
        sensor_noise_deviation.reshape(-1),
        2 * SIDE,
    )
    count = token.size
    both = lax.all_gather(jnp.concatenate([states, table], axis=0), "zh", axis=0, tiled=False)
    own_x = both[:, :count].reshape(2, 2, count // 2, 2 * SIDE)
    west_x = passed_along(own_x[:, 1], TILE, 1)
    east_x = passed_along(own_x[:, 0], TILE, -1)
    obs = weighted_places(both[:, count:], sensor_gridpoint.size)

    def embed_rows(own, other):
        return jnp.concatenate(
            [own[:, :BLOCK].reshape(SIDE, -1), other[:, :BLOCK].reshape(SIDE, -1)], axis=0
        )

    def lifts(own, other):
        own, other = own[:, None, BLOCK:], other[:, None, BLOCK:]
        return in_order(zh, own, other, 1).reshape(-1, own.shape[-1])

    scale = jnp.repeat(cosine_logit_scale, HEAD)[None, :]
    hidden, context = attention(
        flags,
        own_x,
        west_x,
        east_x,
        embed_rows(own_front, other_front),
        embed_rows(own_front_p, other_front_p),
        lifts(own_front, other_front),
        lifts(own_front_p, other_front_p),
        scale,
    )

    size = 2 * count
    grid = np.arange(size).reshape(2, 2, members, rows, HALF)
    order = one_hot(grid.transpose(3, 1, 0, 2, 4).reshape(-1), size)
    latent = latent_rows(flags, context, hidden, order, tail_mine, tail_part)
    moved = exchanged(latent.reshape(16, size // 16, width)).reshape(size, width)

    grid = np.arange(size).reshape(16, 2, members, HALF)
    order = one_hot(grid.transpose(3, 1, 0, 2).reshape(-1), size)
    grid = np.arange(size // 2).reshape(HALF, 16, members)
    back_order = one_hot(grid.transpose(1, 2, 0).reshape(-1), size // 2)
    posterior = analysis(flags, moved, order, back_order, obs, tail_mine, tail_part)
    back = exchanged(posterior.reshape(16, size // 32, width)).reshape(size // 2, width)

    grid = np.arange(size // 2).reshape(rows, 2, members, HALF)
    order = one_hot(grid.transpose(2, 0, 1, 3).reshape(-1), size // 2)
    back = times(order, back).astype(bf16)

    def strip(tail):
        return tail.reshape(32, BLOCK, -1)[:, :SHARD].reshape(feats, -1)

    dec_part = swapped(dec_mine, "core")
    b_mine, b_part = halves(core, back)
    result = times_t(b_mine, strip(dec_mine)) + times_t(b_part, strip(dec_part))
    return result.astype(bf16).reshape(members, rows, cols, feats)


def solution(mesh):
    fine = Mesh(
        np.asarray(mesh.devices).reshape(4, 4, 2, 8, 2), ("x", "y", "zh", "zl", "core")
    )
    return jax.shard_map(
        per_device,
        mesh=fine,
        in_specs=(
            P(MEM, None, TILE, None),
            P(MEM, None),
            P(None, MEM),
            P(None, MEM),
            P(None, MEM),
            P(),
            P(),
            P(MEM, TILE, None),
            P(MEM, TILE, None),
            P(MEM, TILE, None),
            P(MEM, TILE, None),
            P(MEM, TILE, None),
        ),
        out_specs=P(MEM, None, TILE, None),
        check_vma=False,
    )
```

time: 227 us -> 201 us (0.89)
  the two profiles are of different devices: /device:TPU:8 before, /device:TPU:32 now
where the time goes in v2:
time: 201 us; the launch traced here: 200 us
  blocking collectives  75.9 us (38%)
  starting transfers between devices  54.6 us (27%)
  waiting for transfers between devices  25.1 us (12%)
  Pallas kernels  18.5 us (9%)
  local copies, waits for them, and re-layouts  15 us (7%)
  other arithmetic  7.83 us (4%)
  matrix products  2.91 us (1%)
    all_gather x1, blocking collectives, per_device(): lax.all_gather(jnp.concatenate([states, table], axis=0), 'zh', axis=0, ti...  43 us
    all_gather x1, blocking collectives, per_device(): dec_mine = lax.all_gather(decoder, PLANE, axis=0, tiled=True)  33 us
    all_to_all x5, starting transfers between devices, exchanged(): lax.all_to_all(blocks, PLANE, split_axis=0, concat_axis=0, tiled=True)  26.1 us
    all_to_all x5, waiting for transfers between devices, exchanged(): lax.all_to_all(blocks, PLANE, split_axis=0, concat_axis=0, tiled=True)  25 us
    ppermute x5, starting transfers between devices, swapped(): return lax.ppermute(value, axis, [(0, 1), (1, 0)])  23 us
    pallas_call x1, Pallas kernels, attention(): pl.pallas_call(attention_kernel, grid=(groups,), in_specs=[pl.BlockSpec(m...  10.9 us
    ppermute x2, starting transfers between devices, passed_along(): lax.ppermute(value, axis, [(i, (i + by) % devices) for i in range(devices)])  5.55 us
    pallas_call x1, Pallas kernels, analysis(): pl.pallas_call(analysis_kernel, in_specs=[pl.BlockSpec(memory_space=pltpu...  5.08 us
  transfers between devices with their start and end apart: 12, of which 3 were waited for; matrix products, arithmetic and copies ran while one was open for 11% of the time, Pallas kernels for 9%

profile of v2, /device:TPU:32, one launch (start us, length us, event | category | flops | bytes accessed | tf_op | source)
XLA Modules:
  0.0 200.4 jit_solution(2408698485464382374)
XLA Ops:
  0.0 1.0 fusion.11
  1.1 14.8 %collective-permute-start.2 = (bf16[176,384]{1,0:T(8,128)(2,1)S(1)}, bf16[176,384]{1,0:T(8,128)(2,1)S(1)}, u32[]{:S(2)}, u32[]{:S(2)}) collective-permute-start(bf16[176,384]{1,0:T(8,128)(2,1)S(1)} %slice_select_fusion), channel_id=1, source_target_pairs={{0,16},{16,0},{1,17},{17,1},{2,18},{18,2},{3,19},{19,3},{4,20},{20... | collective-permute-start | bytes 405512 | tf_op jit(solution)/shard_map/ppermute | solution.py:31
  16.0 1.2 broadcast_in_dim.9
  17.2 7.1 %all-to-all-start = ((bf16[16,112,384]{2,1,0:T(8,128)(2,1)}), bf16[16,112,384]{2,1,0:T(8,128)(2,1)}, u32[]{:S(2)}, u32[]{:S(2)}) async-start(bf16[16,112,384]{2,1,0:T(8,128)(2,1)} %broadcast_in_dim.9), calls=%async_computation | async-start | bytes 2752512 | tf_op jit(solution)/shard_map/all_to_all | solution.py:44
  24.5 1.3 fusion.3
  25.8 43.0 %all-gather = bf16[288,1280]{1,0:T(8,128)(2,1)S(1)} all-gather(bf16[144,1280]{1,0:T(8,128)(2,1)S(1)} %fusion.10), channel_id=2, replica_groups=mesh['x'=4,'y'=4,'zh'=2,'zl'=8,'core'=2] {'zh'}, dimensions={0}, use_global_device_ids=true | all-gather | bytes 1105920 | tf_op jit(solution)/shard_map/all_gather | solution.py:394
  68.8 1.2 broadcast_in_dim.8
  70.1 7.1 %all-to-all-start.1 = ((bf16[16,112,384]{2,1,0:T(8,128)(2,1)}), bf16[16,112,384]{2,1,0:T(8,128)(2,1)}, u32[]{:S(2)}, u32[]{:S(2)}) async-start(bf16[16,112,384]{2,1,0:T(8,128)(2,1)} %broadcast_in_dim.8), calls=%async_computation.1 | async-start | bytes 2752512 | tf_op jit(solution)/shard_map/all_to_all | solution.py:44
  77.1 0.8 slice_bitcast_fusion
  77.9 1.9 collective-permute-start
  79.8 3.6 %collective-permute-start.1 = (bf16[2,64,1280]{2,1,0:T(8,128)(2,1)S(1)}, bf16[2,64,1280]{2,1,0:T(8,128)(2,1)S(1)}, u32[]{:S(2)}, u32[]{:S(2)}) collective-permute-start(bf16[2,64,1280]{2,1,0:T(8,128)(2,1)S(1)} %get-tuple-element.21), channel_id=1, source_target_pairs={{0,15},{1,0},{2,1},{3,2},{4,3},{5,4},{6,5},{7,6},{8,7},{9,8},{10,9... | collective-permute-start | bytes 983048 | tf_op jit(solution)/shard_map/ppermute | solution.py:36
  83.5 0.1 reshape.219
  83.6 0.1 reshape.220
  83.9 0.1 convolution_convert_fusion.2
  84.0 1.0 broadcast_in_dim.10
  85.1 1.9 collective-permute-start.3
  87.0 10.4 %all-to-all-done.1 = bf16[16,112,384]{2,1,0:T(8,128)(2,1)} async-done(((bf16[16,112,384]{2,1,0:T(8,128)(2,1)}), bf16[16,112,384]{2,1,0:T(8,128)(2,1)}, u32[]{:S(2)}, u32[]{:S(2)}) %all-to-all-start.1) | async-done | bytes 1376288 | tf_op jit(solution)/shard_map/all_to_all | solution.py:44
  97.4 1.9 collective-permute-start.4
  99.4 0.5 copy.41
  99.9 0.6 copy.38
  100.5 3.6 %all-to-all-start.2 = ((bf16[16,64,384]{2,1,0:T(8,128)(2,1)}), bf16[16,64,384]{2,1,0:T(8,128)(2,1)S(1)}, u32[]{:S(2)}, u32[]{:S(2)}) async-start(bf16[16,64,384]{2,1,0:T(8,128)(2,1)} %broadcast_in_dim.10), calls=%async_computation.2 | async-start | bytes 1572864 | tf_op jit(solution)/shard_map/all_to_all | solution.py:44
  104.2 33.0 %all_gather.11 = bf16[1280,384]{1,0:T(8,128)(2,1)} all-gather(bf16[80,384]{1,0:T(8,128)(2,1)S(1)} %pad_maximum_fusion.4), channel_id=1, replica_groups=mesh['x'=4,'y'=4,'zh'=2,'zl'=8,'core'=2] {'x','y'}, dimensions={0}, use_global_device_ids=true | all-gather | bytes 1044480 | tf_op jit(solution)/shard_map/all_gather | solution.py:371
  137.2 1.9 slice.108
  139.1 2.9 %select_bitcast_fusion.3 = (bf16[16,1,72,384]{3,2,0,1:T(8,128)(2,1)}, bf16[16,1,72,384]{3,2,0,1:T(8,128)(2,1)}) fusion(pred[]{:T(512)S(6)} %eq.28, bf16[16,112,384]{2,1,0:T(8,128)(2,1)} %all-to-all-done.1, bf16[16,112,384]{2,1,0:T(8,128)(2,1)} %all-to-all-done), kind=kLoop, calls=%fused_computation.19 | loop fusion | flops 884736 | bytes 3538945 | tf_op jit(solution)/shard_map/jit(_where)/select_n | solution.py:62
  142.0 1.9 collective-permute-start.5
  143.9 1.6 pad_maximum_fusion
  145.5 1.1 slice.113
  146.6 0.2 copy.25
  146.8 2.4 %collective-permute-start.6 = (bf16[1280,384]{1,0:T(8,128)(2,1)}, bf16[1280,384]{1,0:T(8,128)(2,1)}, u32[]{:S(2)}, u32[]{:S(2)}) collective-permute-start(bf16[1280,384]{1,0:T(8,128)(2,1)} %all_gather.11), channel_id=1, source_target_pairs={{0,1},{1,0},{2,3},{3,2},{4,5},{5,4},{6,7},{7,6},{8,9},{9,8},{10,11... | collective-permute-start | bytes 2949128 | tf_op jit(solution)/shard_map/ppermute | solution.py:31
  149.2 1.1 slice.146
  150.3 1.6 select_bitcast_fusion.1
  152.0 0.2 pad_maximum_fusion.1
  152.2 1.1 slice.147
  153.3 0.2 pad_maximum_fusion.2
  153.5 10.9 %attention.1 = (bf16[256,768]{1,0:T(8,128)(2,1)S(1)}, bf16[256,768]{1,0:T(8,128)(2,1)S(1)}) custom-call(s32[2]{0:T(128)S(1)} %pad_add_fusion.flags, bf16[2,2,64,1280]{3,2,1,0:T(8,128)(2,1)S(1)} %bitcast.99, bf16[2,64,1280]{2,1,0:T(8,128)(2,1)S(1)} %collective-permute-done.west_x, bf16[2,64,1280]{2,1,0:T(8,128)(2,1)S(1)} %collective-permute-done.1.east_x, ...), custom_call_target="tpu_custom_call" | custom-call | tf_op jit(solution)/shard_map/attention/pallas_call | solution.py:167
  164.5 2.5 %latent.1 = bf16[256,768]{1,0:T(8,128)(2,1)} custom-call(s32[2]{0:T(128)S(1)} %pad_add_fusion.flags, bf16[256,768]{1,0:T(8,128)(2,1)S(1)} %get-tuple-element.14.context, bf16[256,768]{1,0:T(8,128)(2,1)S(1)} %get-tuple-element.15.hidden, bf16[256,256]{1,0:T(8,128)(2,1)S(1)} %copy-done.2, bf16[16,64,384]{2,1,0:T(8,128)(2,1)S(1)} %all-to-all-done.2.t_mine, ...), custom_call_target="tpu_custom_call" | custom-call | tf_op jit(solution)/shard_map/latent/pallas_call | solution.py:202
  167.0 4.6 %all-to-all-start.3 = ((bf16[16,16,768]{2,1,0:T(8,128)(2,1)}), bf16[16,16,768]{2,1,0:T(8,128)(2,1)S(1)}, u32[]{:S(2)}, u32[]{:S(2)}) async-start(bf16[16,16,768]{2,1,0:T(8,128)(2,1)} %bitcast.26), calls=%async_computation.3 | async-start | bytes 786432 | tf_op jit(solution)/shard_map/all_to_all | solution.py:44
  171.6 0.5 fusion.5.obs
  172.1 9.5 %all-to-all-done.3 = bf16[16,16,768]{2,1,0:T(8,128)(2,1)S(1)} async-done(((bf16[16,16,768]{2,1,0:T(8,128)(2,1)}), bf16[16,16,768]{2,1,0:T(8,128)(2,1)S(1)}, u32[]{:S(2)}, u32[]{:S(2)}) %all-to-all-start.3) | async-done | bytes 393248 | tf_op jit(solution)/shard_map/all_to_all | solution.py:44
  181.6 5.1 %analysis.1 = bf16[128,768]{1,0:T(8,128)(2,1)} custom-call(s32[2]{0:T(128)S(1)} %pad_add_fusion.flags, bf16[256,768]{1,0:T(8,128)(2,1)S(1)} %bitcast.100, bf16[256,256]{1,0:T(8,128)(2,1)S(1)} %copy-done.1, bf16[128,128]{1,0:T(8,128)(2,1)S(1)} %copy-done.3, f32[2,4,512]{2,1,0:T(4,128)S(1)} %fusion.5.obs, bf16[16,64,384]{2,1,0:T(8,128)(2,1)S(1)} %all-to-all-done.2.t_mine, ...), custom_call_target="tpu_custom_call" | custom-call | tf_op jit(solution)/shard_map/analysis/pallas_call | solution.py:289
  186.7 3.7 %all-to-all-start.4 = ((bf16[16,8,768]{2,1,0:T(8,128)(2,1)}), bf16[16,8,768]{2,1,0:T(8,128)(2,1)S(1)}, u32[]{:S(2)}, u32[]{:S(2)}) async-start(bf16[16,8,768]{2,1,0:T(8,128)(2,1)} %bitcast.28), calls=%async_computation.4 | async-start | bytes 393216 | tf_op jit(solution)/shard_map/all_to_all | solution.py:44
  190.4 1.5 reshape.231
  191.9 1.5 reshape.233
  193.3 5.1 %all-to-all-done.4 = bf16[16,8,768]{2,1,0:T(8,128)(2,1)S(1)} async-done(((bf16[16,8,768]{2,1,0:T(8,128)(2,1)}), bf16[16,8,768]{2,1,0:T(8,128)(2,1)S(1)}, u32[]{:S(2)}, u32[]{:S(2)}) %all-to-all-start.4) | async-done | bytes 196640 | tf_op jit(solution)/shard_map/all_to_all | solution.py:44
  198.5 0.2 fusion.4
  198.7 0.4 fusion.16
  199.1 0.4 fusion.2
  199.5 0.9 copy.27
  (65 shorter events, 0.6 us)
Async XLA Ops:
  0.0 24.4 %copy-start = (bf16[2,8,8,1120]{3,2,1,0:T(8,128)(2,1)S(1)}, bf16[2,8,8,1120]{3,2,1,0:T(8,128)(2,1)}, u32[]{:S(2)}) copy-start(bf16[2,8,8,1120]{3,2,1,0:T(8,128)(2,1)} %param.18) | copy-start | bytes 860164
  1.1 67.7 %collective-permute-start.2 = (bf16[176,384]{1,0:T(8,128)(2,1)S(1)}, bf16[176,384]{1,0:T(8,128)(2,1)S(1)}, u32[]{:S(2)}, u32[]{:S(2)}) collective-permute-start(bf16[176,384]{1,0:T(8,128)(2,1)S(1)} %slice_select_fusion), channel_id=1, source_target_pairs={{0,16},{16,0},{1,17},{17,1},{2,18},{18,2},{3,19},{19,3},{4,20},{20... | collective-permute-start | bytes 405512 | tf_op jit(solution)/shard_map/ppermute | solution.py:31
  15.9 8.4 %copy-start.8 = (f32[1,1,256]{2,1,0:T(1,128)S(1)}, f32[1,1,256]{2,1,0:T(1,128)}, u32[]{:S(2)}) copy-start(f32[1,1,256]{2,1,0:T(1,128)} %param.29) | copy-start | bytes 3076
  15.9 8.4 %copy-start.9 = (f32[1,1,256]{2,1,0:T(1,128)S(1)}, f32[1,1,256]{2,1,0:T(1,128)}, u32[]{:S(2)}) copy-start(f32[1,1,256]{2,1,0:T(1,128)} %param.28) | copy-start | bytes 3076
  15.9 8.4 %copy-start.11 = (s32[1,1,256]{2,1,0:T(1,128)S(1)}, s32[1,1,256]{2,1,0:T(1,128)}, u32[]{:S(2)}) copy-start(s32[1,1,256]{2,1,0:T(1,128)} %param.25) | copy-start | bytes 3076
  16.0 8.4 %copy-start.12 = (s32[1,1,256]{2,1,0:T(1,128)S(1)}, s32[1,1,256]{2,1,0:T(1,128)}, u32[]{:S(2)}) copy-start(s32[1,1,256]{2,1,0:T(1,128)} %param.27) | copy-start | bytes 3076
  16.0 8.4 %copy-start.13 = (s32[1,1,256]{2,1,0:T(1,128)S(1)}, s32[1,1,256]{2,1,0:T(1,128)}, u32[]{:S(2)}) copy-start(s32[1,1,256]{2,1,0:T(1,128)} %param.26) | copy-start | bytes 3076
  16.0 8.5 %copy-start.5 = (bf16[128,128]{1,0:T(8,128)(2,1)S(1)}, bf16[128,128]{1,0:T(8,128)(2,1)}, u32[]{:S(2)}) copy-start(bf16[128,128]{1,0:T(8,128)(2,1)} %constant.43.clone) | copy-start | bytes 98308
  16.0 8.5 %copy-start.15 = (s32[1280]{0:T(1024)S(1)}, s32[1280]{0:T(1024)}, u32[]{:S(2)}) copy-start(s32[1280]{0:T(1024)} %constant.44.clone) | copy-start | bytes 15364
  17.2 52.9 %all-to-all-start = ((bf16[16,112,384]{2,1,0:T(8,128)(2,1)}), bf16[16,112,384]{2,1,0:T(8,128)(2,1)}, u32[]{:S(2)}, u32[]{:S(2)}) async-start(bf16[16,112,384]{2,1,0:T(8,128)(2,1)} %broadcast_in_dim.9), calls=%async_computation | async-start | bytes 2752512 | tf_op jit(solution)/shard_map/all_to_all | solution.py:44
  70.1 13.4 %copy-start.7 = (bf16[16,70]{1,0:T(8,128)(2,1)S(1)}, bf16[16,70]{1,0:T(8,128)(2,1)}, u32[]{:S(2)}) copy-start(bf16[16,70]{1,0:T(8,128)(2,1)} %param.24) | copy-start | bytes 6724
  70.1 13.6 %copy-start.14 = (f32[12]{0:T(128)S(1)}, f32[12]{0:T(128)}, u32[]{:S(2)}) copy-start(f32[12]{0:T(128)} %param.23) | copy-start | bytes 148
  70.1 27.3 %all-to-all-start.1 = ((bf16[16,112,384]{2,1,0:T(8,128)(2,1)}), bf16[16,112,384]{2,1,0:T(8,128)(2,1)}, u32[]{:S(2)}, u32[]{:S(2)}) async-start(bf16[16,112,384]{2,1,0:T(8,128)(2,1)} %broadcast_in_dim.8), calls=%async_computation.1 | async-start | bytes 2752512 | tf_op jit(solution)/shard_map/all_to_all | solution.py:44
  77.9 75.6 %collective-permute-start = (bf16[2,64,1280]{2,1,0:T(8,128)(2,1)}, bf16[2,64,1280]{2,1,0:T(8,128)(2,1)S(1)}, u32[]{:S(2)}, u32[]{:S(2)}) collective-permute-start(bf16[2,64,1280]{2,1,0:T(8,128)(2,1)} %get-tuple-element.22), channel_id=1, source_target_pairs={{0,1},{1,2},{2,3},{3,4},{4,5},{5,6},{6,7},{7,8},{8,9},{9,10},{10,1... | collective-permute-start | bytes 983048 | tf_op jit(solution)/shard_map/ppermute | solution.py:36
  79.8 73.7 %collective-permute-start.1 = (bf16[2,64,1280]{2,1,0:T(8,128)(2,1)S(1)}, bf16[2,64,1280]{2,1,0:T(8,128)(2,1)S(1)}, u32[]{:S(2)}, u32[]{:S(2)}) collective-permute-start(bf16[2,64,1280]{2,1,0:T(8,128)(2,1)S(1)} %get-tuple-element.21), channel_id=1, source_target_pairs={{0,15},{1,0},{2,1},{3,2},{4,3},{5,4},{6,5},{7,6},{8,7},{9,8},{10,9... | collective-permute-start | bytes 983048 | tf_op jit(solution)/shard_map/ppermute | solution.py:36
  85.1 61.8 %collective-permute-start.3 = (bf16[16,112,384]{2,1,0:T(8,128)(2,1)}, bf16[16,112,384]{2,1,0:T(8,128)(2,1)}, u32[]{:S(2)}, u32[]{:S(2)}) collective-permute-start(bf16[16,112,384]{2,1,0:T(8,128)(2,1)} %all-to-all-done), channel_id=1, source_target_pairs={{0,1},{1,0},{2,3},{3,2},{4,5},{5,4},{6,7},{7,6},{8,9},{9,8},{10,11... | collective-permute-start | bytes 4128776 | tf_op jit(solution)/shard_map/ppermute | solution.py:31
  97.4 52.9 %collective-permute-start.4 = (bf16[16,112,384]{2,1,0:T(8,128)(2,1)}, bf16[16,112,384]{2,1,0:T(8,128)(2,1)}, u32[]{:S(2)}, u32[]{:S(2)}) collective-permute-start(bf16[16,112,384]{2,1,0:T(8,128)(2,1)} %all-to-all-done.1), channel_id=1, source_target_pairs={{0,1},{1,0},{2,3},{3,2},{4,5},{5,4},{6,7},{7,6},{8,9},{9,8},{10,11... | collective-permute-start | bytes 4128776 | tf_op jit(solution)/shard_map/ppermute | solution.py:31
  100.5 41.5 %all-to-all-start.2 = ((bf16[16,64,384]{2,1,0:T(8,128)(2,1)}), bf16[16,64,384]{2,1,0:T(8,128)(2,1)S(1)}, u32[]{:S(2)}, u32[]{:S(2)}) async-start(bf16[16,64,384]{2,1,0:T(8,128)(2,1)} %broadcast_in_dim.10), calls=%async_computation.2 | async-start | bytes 1572864 | tf_op jit(solution)/shard_map/all_to_all | solution.py:44
  142.0 22.5 %collective-permute-start.5 = (bf16[16,64,384]{2,1,0:T(8,128)(2,1)S(1)}, bf16[16,64,384]{2,1,0:T(8,128)(2,1)S(1)}, u32[]{:S(2)}, u32[]{:S(2)}) collective-permute-start(bf16[16,64,384]{2,1,0:T(8,128)(2,1)S(1)} %all-to-all-done.2.t_mine), channel_id=1, source_target_pairs={{0,1},{1,0},{2,3},{3,2},{4,5},{5,4},{6,7},{7,6},{8,9},{9,8},{10,11... | collective-permute-start | bytes 2359304 | tf_op jit(solution)/shard_map/ppermute | solution.py:31
  146.8 45.0 %collective-permute-start.6 = (bf16[1280,384]{1,0:T(8,128)(2,1)}, bf16[1280,384]{1,0:T(8,128)(2,1)}, u32[]{:S(2)}, u32[]{:S(2)}) collective-permute-start(bf16[1280,384]{1,0:T(8,128)(2,1)} %all_gather.11), channel_id=1, source_target_pairs={{0,1},{1,0},{2,3},{3,2},{4,5},{5,4},{6,7},{7,6},{8,9},{9,8},{10,11... | collective-permute-start | bytes 2949128 | tf_op jit(solution)/shard_map/ppermute | solution.py:31
  151.9 1.3 copy-start.4
  153.5 11.0 %copy-start.2 = (bf16[256,256]{1,0:T(8,128)(2,1)S(1)}, bf16[256,256]{1,0:T(8,128)(2,1)}, u32[]{:S(2)}) copy-start(bf16[256,256]{1,0:T(8,128)(2,1)} %constant.45.clone.order) | copy-start | bytes 393220
  164.5 7.1 %copy-start.6 = (s32[2,1,256]{2,0,1:T(2,128)S(1)}, s32[2,1,256]{2,0,1:T(2,128)}, u32[]{:S(2)}) copy-start(s32[2,1,256]{2,0,1:T(2,128)} %copy.41) | copy-start | bytes 6148
  164.5 7.1 %copy-start.10 = (s32[2,1,256]{2,0,1:T(2,128)S(1)}, s32[2,1,256]{2,0,1:T(2,128)}, u32[]{:S(2)}) copy-start(s32[2,1,256]{2,0,1:T(2,128)} %copy.38) | copy-start | bytes 6148
  164.5 17.1 %copy-start.1 = (bf16[256,256]{1,0:T(8,128)(2,1)S(1)}, bf16[256,256]{1,0:T(8,128)(2,1)}, u32[]{:S(2)}) copy-start(bf16[256,256]{1,0:T(8,128)(2,1)} %constant.46.clone.order) | copy-start | bytes 393220
  164.5 17.1 %copy-start.3 = (bf16[128,128]{1,0:T(8,128)(2,1)S(1)}, bf16[128,128]{1,0:T(8,128)(2,1)}, u32[]{:S(2)}) copy-start(bf16[128,128]{1,0:T(8,128)(2,1)} %constant.47.clone.back_order) | copy-start | bytes 98308
  167.0 14.6 %all-to-all-start.3 = ((bf16[16,16,768]{2,1,0:T(8,128)(2,1)}), bf16[16,16,768]{2,1,0:T(8,128)(2,1)S(1)}, u32[]{:S(2)}, u32[]{:S(2)}) async-start(bf16[16,16,768]{2,1,0:T(8,128)(2,1)} %bitcast.26), calls=%async_computation.3 | async-start | bytes 786432 | tf_op jit(solution)/shard_map/all_to_all | solution.py:44
  186.7 11.8 %all-to-all-start.4 = ((bf16[16,8,768]{2,1,0:T(8,128)(2,1)}), bf16[16,8,768]{2,1,0:T(8,128)(2,1)S(1)}, u32[]{:S(2)}, u32[]{:S(2)}) async-start(bf16[16,8,768]{2,1,0:T(8,128)(2,1)} %bitcast.28), calls=%async_computation.4 | async-start | bytes 393216 | tf_op jit(solution)/shard_map/all_to_all | solution.py:44

commit v3 on v2

v3 whole, which is shorter than its diff:
```python
import functools

import numpy as np
import jax
import jax.numpy as jnp
from jax import lax
from jax.experimental import pallas as pl
from jax.experimental.pallas import tpu as pltpu
from jax.sharding import Mesh, PartitionSpec as P

PANE_SIDE = 8
HALF = PANE_SIDE // 2
NS_ITERS = 5
PLANE = ("x", "y")
MEM = ("x", "y", "zh")
TILE = ("zl", "core")
BLOCK = 40
SHARD = 35
SIDE = 16 * BLOCK
HEAD = 64
GROUP = 4 * HEAD
OWN = PANE_SIDE * HALF

eps_norm = 1e-05
normalizing_guard = 1e-06
bf16 = jnp.bfloat16
f32 = jnp.float32


def swapped(value, axis):
    return lax.ppermute(value, axis, [(0, 1), (1, 0)])


def shifted(value, by):
    return lax.ppermute(value, ("zh", "zl"), [(z, (z + by) % 16) for z in range(16)])


def crossed(value):
    pairs = [(8 * h + z, 8 * (1 - h) + (z + 4) % 8) for h in range(2) for z in range(8)]
    return lax.ppermute(value, ("zh", "zl"), pairs)


def between_chips(value):
    pairs = [(2 * z, 2 * ((z - 1) % 8) + 1) for z in range(8)]
    return lax.ppermute(value, TILE, pairs + [(b, a) for a, b in pairs])


def copies_of(part):
    return lax.optimization_barrier(jnp.broadcast_to(part[None], (16,) + part.shape))


def exchanged(blocks):
    return lax.all_to_all(blocks, PLANE, split_axis=0, concat_axis=0, tiled=True)


def times(left, right):
    return jnp.dot(left, right, preferred_element_type=f32)


def times_t(left, right):
    return lax.dot_general(left, right, (((1,), (1,)), ((), ())), preferred_element_type=f32)


def normalized(values):
    center = values - jnp.mean(values, axis=-1, keepdims=True)
    spread = jnp.mean(center * center, axis=-1, keepdims=True)
    return center * lax.rsqrt(spread + eps_norm)


def in_order(flag, first, second, axis):
    low = jnp.where(flag == 0, first, second)
    high = jnp.where(flag == 0, second, first)
    return jnp.concatenate([low, high], axis=axis)


def halves(flag, value):
    width = value.shape[-1] // 2
    low, high = value[..., :width], value[..., width:]
    return jnp.where(flag == 0, low, high), jnp.where(flag == 0, high, low)


def two_parts(value):
    high = value.astype(bf16)
    return high, (value - high.astype(f32)).astype(bf16)


def three_parts(value):
    high = value.astype(bf16)
    rest = value - high.astype(f32)
    middle = rest.astype(bf16)
    return high, middle, (rest - middle.astype(f32)).astype(bf16)


def iota(shape, axis):
    return lax.broadcasted_iota(jnp.int32, shape, axis)


def one_hot(order, width):
    return jnp.asarray(np.asarray(order)[:, None] == np.arange(width)[None, :], bf16)


def front_kernel(
    flags,
    x_all,
    own_m,
    other_m,
    own_p,
    other_p,
    scale,
    order,
    latent_out,
    w_mine,
    w_part,
    latents,
):
    core, zh = flags[0], flags[1]
    members = x_all.shape[1] // (4 * OWN)
    lanes = own_m.shape[2]
    lifts, outs = 6 * lanes // 32, 2 * lanes // 32
    front = lifts + BLOCK
    width = 2 * lanes

    @pl.when(pl.program_id(0) == 0)
    def _():
        for target, own, other in ((w_mine, own_m, other_m), (w_part, own_p, other_p)):
            for place in range(16):
                target[2 * lifts * place : 2 * lifts * (place + 1), :] = in_order(
                    zh, own[place, :lifts, :], other[place, :lifts, :], 0
                )

    def embed(own, other):
        return times(x_own, own[:, lifts:front, :].reshape(SIDE, lanes)) + times(
            x_other, other[:, lifts:front, :].reshape(SIDE, lanes)
        )

    x = x_all[0]
    x_own, x_other = halves(zh, x)
    hidden = in_order(core, embed(own_m, other_m), embed(own_p, other_p), 1).astype(bf16)
    normed = normalized(hidden.astype(f32)).astype(bf16)
    n_mine, n_part = halves(core, normed)
    own_rows = 2 * members * OWN

    same = (iota((GROUP, GROUP), 0) // HEAD) == (iota((GROUP, GROUP), 1) // HEAD)
    ones = same.astype(bf16)
    lane_head = iota((PANE_SIDE * PANE_SIDE, GROUP), 1) // HEAD

    def projected(left, right, start):
        rows = pl.ds(start, GROUP)
        return (times_t(left, w_mine[rows, :]) + times_t(right, w_part[rows, :])).astype(bf16)

    def unit(values):
        values = values.astype(f32)
        high, low = two_parts(values * values)
        total = times(high, ones) + times(low, ones)
        return (values * lax.rsqrt(total + normalizing_guard)).astype(bf16)

    def diagonal(rows):
        zero = jnp.zeros_like(rows)
        return jnp.concatenate([jnp.where(lane_head == h, rows, zero) for h in range(4)], axis=0)

    def pane_rows(values, w, m):
        own = values[(w * members + m) * OWN : (w * members + m + 1) * OWN]
        start = own_rows + (w * members + m) * OWN
        return jnp.concatenate([own, values[start : start + OWN]], axis=0)

    panes = [(w, m) for w in range(2) for m in range(members)]
    context = []
    for g in range(width // GROUP):
        at = g * GROUP
        query = unit(projected(n_mine[:own_rows], n_part[:own_rows], at))
        key_rows = unit(projected(n_mine, n_part, width + at))
        value_rows = projected(n_mine, n_part, 2 * width + at)
        scores = [
            times_t(query[i * OWN : (i + 1) * OWN], diagonal(pane_rows(key_rows, w, m)))
            for i, (w, m) in enumerate(panes)
        ]
        weights = jnp.exp(jnp.concatenate(scores, axis=0) * scale[:, at : at + GROUP]).astype(bf16)
        total = times(weights, ones)
        mixed = [
            times(weights[i * OWN : (i + 1) * OWN], diagonal(pane_rows(value_rows, w, m)))
            for i, (w, m) in enumerate(panes)
        ]
        context.append((jnp.concatenate(mixed, axis=0) / total).astype(bf16))
    c_mine, c_part = halves(core, jnp.concatenate(context, axis=1))

    def combiner(own, other):
        rows = [
            in_order(
                zh, own[place, front : front + outs, :], other[place, front : front + outs, :], 0
            )
            for place in range(16)
        ]
        return jnp.concatenate(rows, axis=0)

    mixed = times_t(c_mine, combiner(own_m, other_m)) + times_t(c_part, combiner(own_p, other_p))
    latent = normalized(hidden[:own_rows].astype(f32) + mixed).astype(bf16)
    latents[pl.ds(pl.multiple_of(pl.program_id(0) * own_rows, own_rows), own_rows), :] = latent

    @pl.when(pl.program_id(0) == pl.num_programs(0) - 1)
    def _():
        latent_out[...] = times(order[...], latents[...]).astype(bf16)


def front_latents(flags, states, weights, scale, order):
    lanes = weights[0].shape[2]
    groups, count, wide = states.shape
    shape = (order.shape[0], 2 * lanes)

    def whole(array):
        return pl.BlockSpec(
            array.shape, lambda i: (0,) * array.ndim, pipeline_mode=pl.Buffered(1)
        )

    return pl.pallas_call(
        front_kernel,
        grid=(groups,),
        in_specs=[
            pl.BlockSpec(memory_space=pltpu.SMEM),
            pl.BlockSpec((1, count, wide), lambda i: (i, 0, 0)),
        ]
        + [whole(v) for v in (*weights, scale, order)],
        out_specs=pl.BlockSpec(shape, lambda i: (0, 0)),
        out_shape=jax.ShapeDtypeStruct(shape, bf16),
        scratch_shapes=[pltpu.VMEM((6 * lanes, lanes), bf16)] * 2 + [pltpu.VMEM(shape, bf16)],
        compiler_params=pltpu.CompilerParams(vmem_limit_bytes=32 * 1024 * 1024),
        name="front",
    )(flags, states, *weights, scale, order)


def prepare_kernel(x, order, grid, domain, channel, reading, noise, packed):
    count = x.shape[0]
    packed[:count, :] = times(order[...], x[...]).astype(bf16)
    table = [grid[...].astype(f32), domain[...].astype(f32), channel[...].astype(f32)]
    table = [t.astype(bf16) for t in table]
    table += list(three_parts(reading[...])) + list(three_parts(noise[...]))
    table = jnp.concatenate([t.astype(f32) for t in table], axis=0)
    packed[count:, :] = jnp.zeros((16, packed.shape[1]), bf16)
    table = jnp.concatenate([table, jnp.zeros((16 - table.shape[0], table.shape[1]), f32)], axis=0)
    packed[count:, : table.shape[1]] = table.astype(bf16)


def prepare(x, order, *obs):
    vmem = pl.BlockSpec(memory_space=pltpu.VMEM)
    count, feats = x.shape
    return pl.pallas_call(
        prepare_kernel,
        in_specs=[vmem] * (2 + len(obs)),
        out_specs=vmem,
        out_shape=jax.ShapeDtypeStruct((count + 16, feats), bf16),
        name="prepare",
    )(x, order, *obs)


def product(left, right):
    l_high, l_low = two_parts(left)
    r_high, r_low = two_parts(right)
    return times(
        jnp.concatenate([l_high, l_high, l_low], axis=1),
        jnp.concatenate([r_high, r_low, r_high], axis=0),
    )


def product_t(left, right):
    l_high, l_low = two_parts(left)
    r_high, r_low = two_parts(right)
    return times_t(
        jnp.concatenate([l_high, l_high, l_low], axis=1),
        jnp.concatenate([r_high, r_low, r_high], axis=1),
    )


def analysis_kernel(flags, moved, order, back_order, obs, t_mine, t_part, posterior_out):
    latent = times(order[...], moved[...]).astype(bf16)
    members = latent.shape[0] // HALF
    l_mine, l_part = halves(flags[0], latent)

    def readers(ref):
        return ref[:, ref.shape[1] - 16 :, :].reshape(16 * 16, ref.shape[2])

    seen = times_t(l_mine, readers(t_mine)) + times_t(l_part, readers(t_part))
    eye = (iota((members, members), 0) == iota((members, members), 1)).astype(f32)
    systems, drives = [], []
    for block in range(2):
        ens = [seen[(2 * block + t) * members : (2 * block + t + 1) * members] for t in range(2)]
        mean = [jnp.mean(e, axis=0, keepdims=True) for e in ens]
        pert = jnp.concatenate([e - m for e, m in zip(ens, mean)], axis=1)
        mean = jnp.concatenate(mean, axis=1)
        for r in range(2):
            weight = obs[block, r : r + 1, :]
            read = obs[block, 2 + r : 3 + r, :]
            gram = product_t(pert * weight, pert)
            drives.append(jnp.sum(pert * (read - weight * mean), axis=1, keepdims=True))
            systems.append(eye + gram / (members - 1.0))
    bounds = [
        jnp.max(jnp.sum(jnp.abs(s), axis=1, keepdims=True), axis=0, keepdims=True) for s in systems
    ]
    iterates = [s / b for s, b in zip(systems, bounds)]
    factors = [1.5 * eye - 0.5 * y for y in iterates]
    iterates = [product(y, f) for y, f in zip(iterates, factors)]
    roots = factors
    for step in range(1, NS_ITERS):
        factors = [1.5 * eye - 0.5 * product(z, y) for z, y in zip(roots, iterates)]
        if step + 1 < NS_ITERS:
            iterates = [product(y, f) for y, f in zip(iterates, factors)]
        roots = [product(f, z) for f, z in zip(factors, roots)]
    results = []
    for region in range(2 * 2):
        root = roots[region] * lax.rsqrt(bounds[region])
        inner = jnp.sum(root * drives[region], axis=0, keepdims=True)
        mean_weight = jnp.sum(root * inner, axis=1, keepdims=True) / (members - 1.0)
        transform = root + mean_weight
        own_t = transform[:, : members // 2].T
        values = latent[region * members : (region + 1) * members]
        center = jnp.mean(values.astype(f32), axis=0, keepdims=True)
        high, middle, low = three_parts(own_t)
        left = jnp.concatenate([high, middle, low], axis=1)
        moved_part = times(left, jnp.concatenate([values] * 3, axis=0))
        share = 1.0 - jnp.sum(own_t, axis=1, keepdims=True)
        results.append((moved_part + share * center).astype(bf16))
    posterior = jnp.concatenate(results, axis=0)
    posterior_out[...] = times(back_order[...], posterior).astype(bf16)


def analysis(flags, moved, order, back_order, obs, t_mine, t_part):
    vmem = pl.BlockSpec(memory_space=pltpu.VMEM)
    return pl.pallas_call(
        analysis_kernel,
        in_specs=[pl.BlockSpec(memory_space=pltpu.SMEM)] + [vmem] * 6,
        out_specs=vmem,
        out_shape=jax.ShapeDtypeStruct((back_order.shape[0], moved.shape[1]), bf16),
        compiler_params=pltpu.CompilerParams(vmem_limit_bytes=32 * 1024 * 1024),
        name="analysis",
    )(flags, moved, order, back_order, obs, t_mine, t_part)


def decode_kernel(flags, parts, order, d_mine, d_part, out):
    b_mine, b_part = halves(flags[0], times(order[...], parts[...]).astype(bf16))
    out[...] = (times_t(b_mine, d_mine[...]) + times_t(b_part, d_part[...])).astype(bf16)


def decode(flags, parts, order, d_mine, d_part):
    vmem = pl.BlockSpec(memory_space=pltpu.VMEM)
    return pl.pallas_call(
        decode_kernel,
        in_specs=[pl.BlockSpec(memory_space=pltpu.SMEM)] + [vmem] * 4,
        out_specs=vmem,
        out_shape=jax.ShapeDtypeStruct((order.shape[0], d_mine.shape[0]), bf16),
        compiler_params=pltpu.CompilerParams(vmem_limit_bytes=32 * 1024 * 1024),
        name="decode",
    )(flags, parts, order, d_mine, d_part)


def weighted_places(table, count):
    table = table[:, :, :count].astype(f32)
    grid = table[:, 0].astype(jnp.int32)
    domain = table[:, 1].astype(jnp.int32)
    channel = table[:, 2].astype(jnp.int32)
    reading = table[:, 3] + (table[:, 4] + table[:, 5])
    noise = table[:, 6] + (table[:, 7] + table[:, 8])
    token = grid // 16
    distance = (token - domain).astype(f32)
    weight = jnp.exp(-0.5 * distance * distance) / (noise * noise)
    region = (domain[:, None, :] == jnp.arange(2, dtype=jnp.int32)[None, :, None]).astype(f32)
    weight = region * weight[:, None, :]
    left = jnp.concatenate([weight, weight * reading[:, None, :]], axis=1)
    place = grid * 16 + channel
    pick = (place[:, :, None] == jnp.arange(512, dtype=jnp.int32)[None, None, :]).astype(f32)
    return jnp.einsum("bcj,bjp->bcp", left, pick, precision=lax.Precision.HIGHEST)


def per_device(
    starting_ensemble,
    patch_lifting,
    query_keyvalue_lift,
    output_combiner,
    decoder_linear_map,
    cosine_logit_scale,
    sensor_variable_loadings,
    sensor_gridpoint,
    sensor_domain_index,
    sensor_channel_list,
    sensor_reading,
    sensor_noise_deviation,
):
    members, rows, cols, feats = starting_ensemble.shape
    width = patch_lifting.shape[1]
    core = lax.axis_index("core")
    zh = lax.axis_index("zh")
    flags = jnp.stack([core, zh]).astype(jnp.int32)

    fill = ((0, BLOCK - SHARD), (0, 0))
    packed = jnp.concatenate(
        [
            query_keyvalue_lift.T,
            jnp.pad(patch_lifting, fill),
            output_combiner.T,
            jnp.pad(decoder_linear_map.T, fill),
        ],
        axis=0,
    )
    mine, _ = halves(core, packed)
    lanes = mine.shape[1]
    front = query_keyvalue_lift.shape[1] + BLOCK
    o_end = front + output_combiner.shape[1]
    own_all = exchanged(copies_of(mine))

    count = members * rows * cols
    grid = np.arange(count).reshape(members, rows, 2, HALF)
    pick_rows = one_hot(grid.transpose(2, 0, 1, 3).reshape(-1), count)
    obs = (
        sensor_gridpoint,
        sensor_domain_index,
        sensor_channel_list,
        sensor_reading,
        sensor_noise_deviation,
    )
    sent = prepare(
        starting_ensemble.reshape(count, feats), pick_rows, *(o.reshape(1, -1) for o in obs)
    )
    sent, outgoing = lax.optimization_barrier((sent, mine))
    theirs = crossed(outgoing)
    middle = (count + 16) // 2
    up, down = shifted(sent[:middle], 4), shifted(sent[middle:], -4)

    decoder = in_order(zh, mine[o_end:], theirs[o_end:], 0)
    loadings = jnp.pad(
        sensor_variable_loadings.reshape(16, 2, SHARD), ((0, 0), (0, 0), (0, BLOCK - SHARD))
    ).reshape(16, 2 * BLOCK)
    readers = times(loadings, decoder).astype(bf16)
    copies, own_all, up, down = lax.optimization_barrier(
        (copies_of(jnp.concatenate([theirs, readers], axis=0)), own_all, up, down)
    )
    partner = jnp.concatenate([shifted(up, 4), shifted(down, -4)], axis=0)
    other_main = exchanged(copies)
    inside = np.arange(BLOCK)[None, None, :]
    place = np.arange(16)[None, :, None] * 2 + np.arange(2)[:, None, None]
    source = np.where(inside < SHARD, place * SHARD + inside, -1).reshape(-1)
    pick_cols = jnp.asarray(np.arange(feats)[:, None] == source[None, :], bf16)

    both = jnp.stack([sent, partner])
    low, high = both[:, : count // 2], both[:, count // 2 : count]
    core_x = swapped(jnp.where(core == 0, high, low), "core")
    chip_x = between_chips(jnp.where(core == 0, low, high))

    states = jnp.concatenate([both[:, :count], in_order(core, chip_x, core_x, 1)], axis=1)
    states = times(states.reshape(4 * count, feats), pick_cols).astype(bf16)
    states = states.reshape(2, 2 * count, 2 * SIDE)

    own_all_p = swapped(own_all, "core")
    other_main, own_all_p, _ = lax.optimization_barrier((other_main, own_all_p, partner))
    other_main_p = swapped(other_main, "core")
    scale = jnp.repeat(cosine_logit_scale, HEAD)[None, :]
    weights = (own_all, other_main, own_all_p, other_main_p)
    size = 2 * count
    grid = np.arange(size).reshape(2, 2, members, rows, HALF)
    order = one_hot(grid.transpose(3, 1, 0, 2, 4).reshape(-1), size)
    latent = front_latents(flags, states, weights, scale, order)
    tables, latent, own_all, own_all_p = lax.optimization_barrier(
        (both[:, count:], latent, own_all, own_all_p)
    )
    obs = weighted_places(in_order(zh, tables[:1], tables[1:], 0), sensor_gridpoint.size)
    moved = exchanged(latent.reshape(16, size // 16, width)).reshape(size, width)

    grid = np.arange(size).reshape(16, 2, members, HALF)
    order = one_hot(grid.transpose(3, 1, 0, 2).reshape(-1), size)
    grid = np.arange(count).reshape(HALF, 16, members)
    back_order = one_hot(grid.transpose(1, 2, 0).reshape(-1), count)
    posterior = analysis(flags, moved, order, back_order, obs, other_main, other_main_p)
    back = exchanged(posterior.reshape(16, count // 16, width)).reshape(count, width)

    def strip(own, other):
        own, other = own[:, None, o_end : o_end + SHARD], other[:, None, o_end : o_end + SHARD]
        return in_order(zh, own, other, 1).reshape(feats, -1)

    grid = np.arange(count).reshape(rows, 2, members, HALF)
    order = one_hot(grid.transpose(2, 0, 1, 3).reshape(-1), count)
    result = decode(
        flags,
        back,
        order,
        strip(own_all, other_main),
        strip(own_all_p, other_main_p),
    )
    return result.reshape(members, rows, cols, feats)


def solution(mesh):
    fine = Mesh(
        np.asarray(mesh.devices).reshape(4, 4, 2, 8, 2), ("x", "y", "zh", "zl", "core")
    )
    return jax.shard_map(
        per_device,
        mesh=fine,
        in_specs=(
            P(MEM, None, TILE, None),
            P(MEM, None),
            P(None, MEM),
            P(None, MEM),
            P(None, MEM),
            P(),
            P(),
            P(MEM, TILE, None),
            P(MEM, TILE, None),
            P(MEM, TILE, None),
            P(MEM, TILE, None),
            P(MEM, TILE, None),
        ),
        out_specs=P(MEM, None, TILE, None),
        check_vma=False,
    )
```

time: 201 us -> 160 us (0.80)
  the two profiles are of different devices: /device:TPU:32 before, /device:TPU:8 now
where the time goes in v3:
time: 160 us; the launch traced here: 159 us
  starting transfers between devices  75.9 us (47%)
  waiting for transfers between devices  40.9 us (26%)
  Pallas kernels  24.9 us (16%)
  local copies, waits for them, and re-layouts  9.23 us (6%)
  other arithmetic  5.65 us (4%)
  matrix products  2.47 us (2%)
    all_to_all x4, starting transfers between devices, exchanged(): lax.all_to_all(blocks, PLANE, split_axis=0, concat_axis=0, tiled=True)  29.2 us
    ppermute x4, starting transfers between devices, shifted(): lax.ppermute(value, ('zh', 'zl'), [(z, (z + by) % 16) for z in range(16)])  19.9 us
    ppermute x4, waiting for transfers between devices, shifted(): lax.ppermute(value, ('zh', 'zl'), [(z, (z + by) % 16) for z in range(16)])  16.6 us
    pallas_call x1, Pallas kernels, front_latents(): pl.pallas_call(front_kernel, grid=(groups,), in_specs=[pl.BlockSpec(memor...  14.7 us
    all_to_all x4, waiting for transfers between devices, exchanged(): lax.all_to_all(blocks, PLANE, split_axis=0, concat_axis=0, tiled=True)  10.9 us
    ppermute x1, starting transfers between devices, crossed(): return lax.ppermute(value, ('zh', 'zl'), pairs)  10.8 us
    ppermute x1, starting transfers between devices, between_chips(): return lax.ppermute(value, TILE, pairs + [(b, a) for a, b in pairs])  10.3 us
    ppermute x1, waiting for transfers between devices, crossed(): return lax.ppermute(value, ('zh', 'zl'), pairs)  8.04 us
  transfers between devices with their start and end apart: 13, of which 8 were waited for; matrix products, arithmetic and copies ran while one was open for 7% of the time, Pallas kernels for 1%

profile of v3, /device:TPU:8, one launch (start us, length us, event | category | flops | bytes accessed | tf_op | source)
XLA Modules:
  0.0 159.4 jit_solution(8003942175170059912)
XLA Ops:
  0.0 1.0 fusion.9
  1.0 1.6 broadcast_in_dim.7
  2.6 9.5 %all-to-all-start = ((bf16[16,176,384]{2,1,0:T(8,128)(2,1)}), bf16[16,176,384]{2,1,0:T(8,128)(2,1)S(1)}, u32[]{:S(2)}, u32[]{:S(2)}) async-start(bf16[16,176,384]{2,1,0:T(8,128)(2,1)} %broadcast_in_dim.7), calls=%async_computation | async-start | bytes 4325376 | tf_op jit(solution)/shard_map/all_to_all | solution.py:53
  12.1 2.0 %prepare.1 = bf16[144,1120]{1,0:T(8,128)(2,1)} custom-call(bf16[128,1120]{1,0:T(8,128)(2,1)} %bitcast.51, bf16[128,128]{1,0:T(8,128)(2,1)} %constant.43.clone.order, s32[1,256]{1,0:T(1,128)} %bitcast.57, s32[1,256]{1,0:T(1,128)} %bitcast.58, s32[1,256]{1,0:T(1,128)} %bitcast.59, f32[1,256]{1,0:T(1,128)} %bitcast.60, f32[1,256]{1,0:T(1,128)} %bitcast.61), custom_call_target="tpu_custom_call" | custom-call | tf_op jit(solution)/shard_map/prepare/pallas_call | solution.py:245
  14.0 10.8 %collective-permute-start = (bf16[176,384]{1,0:T(8,128)(2,1)S(1)}, bf16[176,384]{1,0:T(8,128)(2,1)S(1)}, u32[]{:S(2)}, u32[]{:S(2)}) collective-permute-start(bf16[176,384]{1,0:T(8,128)(2,1)S(1)} %slice_select_fusion), channel_id=1, source_target_pairs={{0,24},{2,26},{4,28},{6,30},{8,16},{10,18},{12,20},{14,22},{16,8},... | collective-permute-start | bytes 405512 | tf_op jit(solution)/shard_map/ppermute | solution.py:40
  24.8 1.0 fusion.28
  25.9 5.5 %collective-permute-start.1 = (bf16[72,1120]{1,0:T(8,128)(2,1)S(1)}, bf16[72,1120]{1,0:T(8,128)(2,1)S(1)}, u32[]{:S(2)}, u32[]{:S(2)}) collective-permute-start(bf16[72,1120]{1,0:T(8,128)(2,1)S(1)} %get-tuple-element.38), channel_id=1, source_target_pairs={{0,8},{2,10},{4,12},{6,14},{8,16},{10,18},{12,20},{14,22},{16,24},... | collective-permute-start | bytes 483848 | tf_op jit(solution)/shard_map/ppermute | solution.py:35
  31.3 4.3 %collective-permute-start.2 = (bf16[72,1120]{1,0:T(8,128)(2,1)S(1)}, bf16[72,1120]{1,0:T(8,128)(2,1)S(1)}, u32[]{:S(2)}, u32[]{:S(2)}) collective-permute-start(bf16[72,1120]{1,0:T(8,128)(2,1)S(1)} %get-tuple-element.37), channel_id=1, source_target_pairs={{0,24},{2,26},{4,28},{6,30},{8,0},{10,2},{12,4},{14,6},{16,8},{18,... | collective-permute-start | bytes 483848 | tf_op jit(solution)/shard_map/ppermute | solution.py:35
  35.6 0.1 reshape.80
  35.7 0.1 reshape.81
  35.8 8.0 %collective-permute-done = bf16[176,384]{1,0:T(8,128)(2,1)S(1)} collective-permute-done((bf16[176,384]{1,0:T(8,128)(2,1)S(1)}, bf16[176,384]{1,0:T(8,128)(2,1)S(1)}, u32[]{:S(2)}, u32[]{:S(2)}) %collective-permute-start) | collective-permute-done | bytes 135200 | tf_op jit(solution)/shard_map/ppermute | solution.py:40
  43.9 0.1 convolution_convert_fusion.1
  44.0 1.7 %broadcast_in_dim.6 = bf16[16,192,384]{2,1,0:T(8,128)(2,1)} broadcast(bf16[192,384]{1,0:T(8,128)(2,1)S(1)} %pad_maximum_fusion.4), dimensions={1,2} | broadcast | bytes 2506752 | tf_op jit(solution)/shard_map/broadcast_in_dim | solution.py:49
  45.8 4.5 %collective-permute-done.2 = bf16[72,1120]{1,0:T(8,128)(2,1)S(1)} collective-permute-done((bf16[72,1120]{1,0:T(8,128)(2,1)S(1)}, bf16[72,1120]{1,0:T(8,128)(2,1)S(1)}, u32[]{:S(2)}, u32[]{:S(2)}) %collective-permute-start.2) | collective-permute-done | bytes 161312 | tf_op jit(solution)/shard_map/ppermute | solution.py:35
  50.3 1.4 copy-done
  51.7 7.2 %all-to-all-start.1 = ((bf16[16,192,384]{2,1,0:T(8,128)(2,1)}), bf16[16,192,384]{2,1,0:T(8,128)(2,1)S(1)}, u32[]{:S(2)}, u32[]{:S(2)}) async-start(bf16[16,192,384]{2,1,0:T(8,128)(2,1)} %broadcast_in_dim.6), calls=%async_computation.1 | async-start | bytes 4718592 | tf_op jit(solution)/shard_map/all_to_all | solution.py:53
  58.9 1.9 %collective-permute-start.7 = (bf16[16,176,384]{2,1,0:T(8,128)(2,1)}, bf16[16,176,384]{2,1,0:T(8,128)(2,1)S(1)}, u32[]{:S(2)}, u32[]{:S(2)}) collective-permute-start(bf16[16,176,384]{2,1,0:T(8,128)(2,1)} %copy-done), channel_id=1, source_target_pairs={{0,1},{1,0},{2,3},{3,2},{4,5},{5,4},{6,7},{7,6},{8,9},{9,8},{10,11... | collective-permute-start | bytes 6488072 | tf_op jit(solution)/shard_map/ppermute | solution.py:31
  60.8 6.5 %collective-permute-start.3 = (bf16[72,1120]{1,0:T(8,128)(2,1)S(1)}, bf16[72,1120]{1,0:T(8,128)(2,1)S(1)}, u32[]{:S(2)}, u32[]{:S(2)}) collective-permute-start(bf16[72,1120]{1,0:T(8,128)(2,1)S(1)} %collective-permute-done.1), channel_id=1, source_target_pairs={{0,8},{2,10},{4,12},{6,14},{8,16},{10,18},{12,20},{14,22},{16,24},... | collective-permute-start | bytes 483848 | tf_op jit(solution)/shard_map/ppermute | solution.py:35
  67.4 3.6 %collective-permute-start.4 = (bf16[72,1120]{1,0:T(8,128)(2,1)S(1)}, bf16[72,1120]{1,0:T(8,128)(2,1)S(1)}, u32[]{:S(2)}, u32[]{:S(2)}) collective-permute-start(bf16[72,1120]{1,0:T(8,128)(2,1)S(1)} %collective-permute-done.2), channel_id=1, source_target_pairs={{0,24},{2,26},{4,28},{6,30},{8,0},{10,2},{12,4},{14,6},{16,8},{18,... | collective-permute-start | bytes 483848 | tf_op jit(solution)/shard_map/ppermute | solution.py:35
  71.0 11.2 %collective-permute-done.3 = bf16[72,1120]{1,0:T(8,128)(2,1)S(1)} collective-permute-done((bf16[72,1120]{1,0:T(8,128)(2,1)S(1)}, bf16[72,1120]{1,0:T(8,128)(2,1)S(1)}, u32[]{:S(2)}, u32[]{:S(2)}) %collective-permute-start.3) | collective-permute-done | bytes 161312 | tf_op jit(solution)/shard_map/ppermute | solution.py:35
  82.2 0.9 collective-permute-done.4
  83.2 1.4 copy-done.2
  84.5 2.8 %all-to-all-done.1.other_m.t_mine = bf16[16,192,384]{2,1,0:T(8,128)(2,1)S(1)} async-done(((bf16[16,192,384]{2,1,0:T(8,128)(2,1)}), bf16[16,192,384]{2,1,0:T(8,128)(2,1)S(1)}, u32[]{:S(2)}, u32[]{:S(2)}) %all-to-all-start.1) | async-done | bytes 2359328 | tf_op jit(solution)/shard_map/all_to_all | solution.py:53
  87.3 1.9 %collective-permute-start.8 = (bf16[16,192,384]{2,1,0:T(8,128)(2,1)S(1)}, bf16[16,192,384]{2,1,0:T(8,128)(2,1)}, u32[]{:S(2)}, u32[]{:S(2)}) collective-permute-start(bf16[16,192,384]{2,1,0:T(8,128)(2,1)S(1)} %all-to-all-done.1.other_m.t_mine), channel_id=1, source_target_pairs={{0,1},{1,0},{2,3},{3,2},{4,5},{5,4},{6,7},{7,6},{8,9},{9,8},{10,11... | collective-permute-start | bytes 7077896 | tf_op jit(solution)/shard_map/ppermute | solution.py:31
  89.3 0.1 broadcast_in_dim_reshape.3.scale
  89.5 0.1 broadcast_select_fusion.3
  89.6 10.3 %collective-permute-start.5 = (bf16[2,64,1120]{2,1,0:T(8,128)(2,1)S(1)}, bf16[2,64,1120]{2,1,0:T(8,128)(2,1)S(1)}, u32[]{:S(2)}, u32[]{:S(2)}) collective-permute-start(bf16[2,64,1120]{2,1,0:T(8,128)(2,1)S(1)} %get-tuple-element.33), channel_id=1, source_target_pairs={{0,15},{2,1},{4,3},{6,5},{8,7},{10,9},{12,11},{14,13},{15,0},{1,2}... | collective-permute-start | bytes 860168 | tf_op jit(solution)/shard_map/ppermute | solution.py:45
  99.9 1.9 %collective-permute-start.6 = (bf16[2,64,1120]{2,1,0:T(8,128)(2,1)S(1)}, bf16[2,64,1120]{2,1,0:T(8,128)(2,1)S(1)}, u32[]{:S(2)}, u32[]{:S(2)}) collective-permute-start(bf16[2,64,1120]{2,1,0:T(8,128)(2,1)S(1)} %get-tuple-element.34), channel_id=1, source_target_pairs={{0,1},{1,0},{2,3},{3,2},{4,5},{5,4},{6,7},{7,6},{8,9},{9,8},{10,11... | collective-permute-start | bytes 860168 | tf_op jit(solution)/shard_map/ppermute | solution.py:31
  101.9 5.3 %collective-permute-done.5 = bf16[2,64,1120]{2,1,0:T(8,128)(2,1)S(1)} collective-permute-done((bf16[2,64,1120]{2,1,0:T(8,128)(2,1)S(1)}, bf16[2,64,1120]{2,1,0:T(8,128)(2,1)S(1)}, u32[]{:S(2)}, u32[]{:S(2)}) %collective-permute-start.5) | collective-permute-done | bytes 286752 | tf_op jit(solution)/shard_map/ppermute | solution.py:45
  107.3 0.1 pad_maximum_fusion
  107.4 1.9 %convolution_convert_fusion = bf16[512,1280]{1,0:T(8,128)(2,1)S(1)} fusion(bf16[512,1120]{1,0:T(8,128)(2,1)S(1)} %bitcast.50, bf16[1120,1280]{1,0:T(8,128)(2,1)S(1)} %copy-done.12), kind=kOutput, calls=%fused_computation | convolution fusion | flops 1468661760 | bytes 5324800 | tf_op jit(solution)/shard_map/dot_general | solution.py:57
  109.3 0.3 copy-done.3
  109.7 14.7 %front.1 = bf16[256,768]{1,0:T(8,128)(2,1)} custom-call(s32[2]{0:T(128)S(1)} %pad_add_fusion.flags, bf16[2,256,1280]{2,1,0:T(8,128)(2,1)S(1)} %bitcast.42, bf16[16,176,384]{2,1,0:T(8,128)(2,1)S(1)} %copy-done.1, bf16[16,192,384]{2,1,0:T(8,128)(2,1)S(1)} %all-to-all-done.1.other_m.t_mine, bf16[16,176,384]{2,1,0:T(8,128)(2,1)S(1)} %copy-done.3, ...), custom_call_target="tpu_custom_call" | custom-call | tf_op jit(solution)/shard_map/front/pallas_call | solution.py:214
  124.5 7.2 %all-to-all-start.2 = ((bf16[16,16,768]{2,1,0:T(8,128)(2,1)}), bf16[16,16,768]{2,1,0:T(8,128)(2,1)S(1)}, u32[]{:S(2)}, u32[]{:S(2)}) async-start(bf16[16,16,768]{2,1,0:T(8,128)(2,1)} %bitcast.15), calls=%async_computation.2 | async-start | bytes 786432 | tf_op jit(solution)/shard_map/all_to_all | solution.py:53
  131.7 0.5 fusion.obs
  132.2 2.6 %select_bitcast_fusion.1 = (bf16[16,1,35,384]{3,2,0,1:T(8,128)(2,1)S(1)}, bf16[16,1,35,384]{3,2,0,1:T(8,128)(2,1)}, bf16[16,1,35,384]{3,2,0,1:T(8,128)(2,1)}, bf16[16,1,35,384]{3,2,0,1:T(8,128)(2,1)}) fusion(pred[]{:T(512)S(6)} %eq.19, bf16[16,192,384]{2,1,0:T(8,128)(2,1)} %collective-permute-done.8.other_p.t_part, bf16[16,176,384]{2,1,0:T(8,128)(2,1)} %copy-done.2, ...), kind=kLoop, calls=%fused_computation.20 | loop fusion | flops 860160 | bytes 3440641 | tf_op jit(solution)/shard_map/jit(_where)/select_n | solution.py:71
  134.8 4.4 %all-to-all-done.2 = bf16[16,16,768]{2,1,0:T(8,128)(2,1)S(1)} async-done(((bf16[16,16,768]{2,1,0:T(8,128)(2,1)}), bf16[16,16,768]{2,1,0:T(8,128)(2,1)S(1)}, u32[]{:S(2)}, u32[]{:S(2)}) %all-to-all-start.2) | async-done | bytes 393248 | tf_op jit(solution)/shard_map/all_to_all | solution.py:53
  139.2 6.1 %analysis.1 = bf16[128,768]{1,0:T(8,128)(2,1)} custom-call(s32[2]{0:T(128)S(1)} %pad_add_fusion.flags, bf16[256,768]{1,0:T(8,128)(2,1)S(1)} %bitcast.41, bf16[256,256]{1,0:T(8,128)(2,1)S(1)} %copy-done.6, bf16[128,128]{1,0:T(8,128)(2,1)S(1)} %copy-done.7, f32[2,4,512]{2,1,0:T(4,128)S(1)} %fusion.obs, ...), custom_call_target="tpu_custom_call" | custom-call | tf_op jit(solution)/shard_map/analysis/pallas_call | solution.py:326
  145.3 5.3 %all-to-all-start.3 = ((bf16[16,8,768]{2,1,0:T(8,128)(2,1)}), bf16[16,8,768]{2,1,0:T(8,128)(2,1)S(1)}, u32[]{:S(2)}, u32[]{:S(2)}) async-start(bf16[16,8,768]{2,1,0:T(8,128)(2,1)} %bitcast.17), calls=%async_computation.3 | async-start | bytes 393216 | tf_op jit(solution)/shard_map/all_to_all | solution.py:53
  150.6 1.3 pad_maximum_fusion.1
  151.9 0.1 copy.21
  152.1 0.3 reshape.88.d_mine
  152.3 0.6 copy-done.9
  153.0 0.1 pad_maximum_fusion.2
  153.1 0.1 copy.22
  153.2 0.3 reshape.89.d_part
  153.5 3.8 %all-to-all-done.3 = bf16[16,8,768]{2,1,0:T(8,128)(2,1)S(1)} async-done(((bf16[16,8,768]{2,1,0:T(8,128)(2,1)}), bf16[16,8,768]{2,1,0:T(8,128)(2,1)S(1)}, u32[]{:S(2)}, u32[]{:S(2)}) %all-to-all-start.3) | async-done | bytes 196640 | tf_op jit(solution)/shard_map/all_to_all | solution.py:53
  157.3 2.1 %decode.1 = bf16[128,1120]{1,0:T(8,128)(2,1)} custom-call(s32[2]{0:T(128)S(1)} %pad_add_fusion.flags, bf16[128,768]{1,0:T(8,128)(2,1)S(1)} %bitcast.43, bf16[128,128]{1,0:T(8,128)(2,1)S(1)} %copy-done.5, bf16[1120,384]{1,0:T(8,128)(2,1)S(1)} %reshape.88.d_mine, bf16[1120,384]{1,0:T(8,128)(2,1)S(1)} %reshape.89.d_part), custom_call_target="tpu_custom_call" | custom-call | tf_op jit(solution)/shard_map/decode/pallas_call | solution.py:343
  (46 shorter events, 0.5 us)
Async XLA Ops:
  2.6 33.0 %copy-start.10 = (bf16[16,70]{1,0:T(8,128)(2,1)S(1)}, bf16[16,70]{1,0:T(8,128)(2,1)}, u32[]{:S(2)}) copy-start(bf16[16,70]{1,0:T(8,128)(2,1)} %param.24) | copy-start | bytes 6724
  2.6 47.7 %all-to-all-start = ((bf16[16,176,384]{2,1,0:T(8,128)(2,1)}), bf16[16,176,384]{2,1,0:T(8,128)(2,1)S(1)}, u32[]{:S(2)}, u32[]{:S(2)}) async-start(bf16[16,176,384]{2,1,0:T(8,128)(2,1)} %broadcast_in_dim.7), calls=%async_computation | async-start | bytes 4325376 | tf_op jit(solution)/shard_map/all_to_all | solution.py:53
  14.0 29.8 %collective-permute-start = (bf16[176,384]{1,0:T(8,128)(2,1)S(1)}, bf16[176,384]{1,0:T(8,128)(2,1)S(1)}, u32[]{:S(2)}, u32[]{:S(2)}) collective-permute-start(bf16[176,384]{1,0:T(8,128)(2,1)S(1)} %slice_select_fusion), channel_id=1, source_target_pairs={{0,24},{2,26},{4,28},{6,30},{8,16},{10,18},{12,20},{14,22},{16,8},... | collective-permute-start | bytes 405512 | tf_op jit(solution)/shard_map/ppermute | solution.py:40
  25.9 19.9 %collective-permute-start.1 = (bf16[72,1120]{1,0:T(8,128)(2,1)S(1)}, bf16[72,1120]{1,0:T(8,128)(2,1)S(1)}, u32[]{:S(2)}, u32[]{:S(2)}) collective-permute-start(bf16[72,1120]{1,0:T(8,128)(2,1)S(1)} %get-tuple-element.38), channel_id=1, source_target_pairs={{0,8},{2,10},{4,12},{6,14},{8,16},{10,18},{12,20},{14,22},{16,24},... | collective-permute-start | bytes 483848 | tf_op jit(solution)/shard_map/ppermute | solution.py:35
  31.3 19.0 %collective-permute-start.2 = (bf16[72,1120]{1,0:T(8,128)(2,1)S(1)}, bf16[72,1120]{1,0:T(8,128)(2,1)S(1)}, u32[]{:S(2)}, u32[]{:S(2)}) collective-permute-start(bf16[72,1120]{1,0:T(8,128)(2,1)S(1)} %get-tuple-element.37), channel_id=1, source_target_pairs={{0,24},{2,26},{4,28},{6,30},{8,0},{10,2},{12,4},{14,6},{16,8},{18,... | collective-permute-start | bytes 483848 | tf_op jit(solution)/shard_map/ppermute | solution.py:35
  45.8 43.5 %copy-start.11 = (f32[12]{0:T(128)S(1)}, f32[12]{0:T(128)}, u32[]{:S(2)}) copy-start(f32[12]{0:T(128)} %param.23) | copy-start | bytes 148
  45.8 43.7 %copy-start.8 = (bf16[144,1120]{1,0:T(8,128)(2,1)S(1)}, bf16[144,1120]{1,0:T(8,128)(2,1)}, u32[]{:S(2)}) copy-start(bf16[144,1120]{1,0:T(8,128)(2,1)} %prepare.1) | copy-start | bytes 967684
  50.3 1.4 copy-start
  51.7 35.6 %all-to-all-start.1 = ((bf16[16,192,384]{2,1,0:T(8,128)(2,1)}), bf16[16,192,384]{2,1,0:T(8,128)(2,1)S(1)}, u32[]{:S(2)}, u32[]{:S(2)}) async-start(bf16[16,192,384]{2,1,0:T(8,128)(2,1)} %broadcast_in_dim.6), calls=%async_computation.1 | async-start | bytes 4718592 | tf_op jit(solution)/shard_map/all_to_all | solution.py:53
  58.9 24.2 %collective-permute-start.7 = (bf16[16,176,384]{2,1,0:T(8,128)(2,1)}, bf16[16,176,384]{2,1,0:T(8,128)(2,1)S(1)}, u32[]{:S(2)}, u32[]{:S(2)}) collective-permute-start(bf16[16,176,384]{2,1,0:T(8,128)(2,1)} %copy-done), channel_id=1, source_target_pairs={{0,1},{1,0},{2,3},{3,2},{4,5},{5,4},{6,7},{7,6},{8,9},{9,8},{10,11... | collective-permute-start | bytes 6488072 | tf_op jit(solution)/shard_map/ppermute | solution.py:31
  60.8 21.4 %collective-permute-start.3 = (bf16[72,1120]{1,0:T(8,128)(2,1)S(1)}, bf16[72,1120]{1,0:T(8,128)(2,1)S(1)}, u32[]{:S(2)}, u32[]{:S(2)}) collective-permute-start(bf16[72,1120]{1,0:T(8,128)(2,1)S(1)} %collective-permute-done.1), channel_id=1, source_target_pairs={{0,8},{2,10},{4,12},{6,14},{8,16},{10,18},{12,20},{14,22},{16,24},... | collective-permute-start | bytes 483848 | tf_op jit(solution)/shard_map/ppermute | solution.py:35
  67.4 15.8 %collective-permute-start.4 = (bf16[72,1120]{1,0:T(8,128)(2,1)S(1)}, bf16[72,1120]{1,0:T(8,128)(2,1)S(1)}, u32[]{:S(2)}, u32[]{:S(2)}) collective-permute-start(bf16[72,1120]{1,0:T(8,128)(2,1)S(1)} %collective-permute-done.2), channel_id=1, source_target_pairs={{0,24},{2,26},{4,28},{6,30},{8,0},{10,2},{12,4},{14,6},{16,8},{18,... | collective-permute-start | bytes 483848 | tf_op jit(solution)/shard_map/ppermute | solution.py:35
  83.2 1.4 copy-start.2
  87.3 22.0 %collective-permute-start.8 = (bf16[16,192,384]{2,1,0:T(8,128)(2,1)S(1)}, bf16[16,192,384]{2,1,0:T(8,128)(2,1)}, u32[]{:S(2)}, u32[]{:S(2)}) collective-permute-start(bf16[16,192,384]{2,1,0:T(8,128)(2,1)S(1)} %all-to-all-done.1.other_m.t_mine), channel_id=1, source_target_pairs={{0,1},{1,0},{2,3},{3,2},{4,5},{5,4},{6,7},{7,6},{8,9},{9,8},{10,11... | collective-permute-start | bytes 7077896 | tf_op jit(solution)/shard_map/ppermute | solution.py:31
  89.6 17.7 %collective-permute-start.5 = (bf16[2,64,1120]{2,1,0:T(8,128)(2,1)S(1)}, bf16[2,64,1120]{2,1,0:T(8,128)(2,1)S(1)}, u32[]{:S(2)}, u32[]{:S(2)}) collective-permute-start(bf16[2,64,1120]{2,1,0:T(8,128)(2,1)S(1)} %get-tuple-element.33), channel_id=1, source_target_pairs={{0,15},{2,1},{4,3},{6,5},{8,7},{10,9},{12,11},{14,13},{15,0},{1,2}... | collective-permute-start | bytes 860168 | tf_op jit(solution)/shard_map/ppermute | solution.py:45
  99.9 7.4 %collective-permute-start.6 = (bf16[2,64,1120]{2,1,0:T(8,128)(2,1)S(1)}, bf16[2,64,1120]{2,1,0:T(8,128)(2,1)S(1)}, u32[]{:S(2)}, u32[]{:S(2)}) collective-permute-start(bf16[2,64,1120]{2,1,0:T(8,128)(2,1)S(1)} %get-tuple-element.34), channel_id=1, source_target_pairs={{0,1},{1,0},{2,3},{3,2},{4,5},{5,4},{6,7},{7,6},{8,9},{9,8},{10,11... | collective-permute-start | bytes 860168 | tf_op jit(solution)/shard_map/ppermute | solution.py:31
  101.8 5.6 %copy-start.12 = (bf16[1120,1280]{1,0:T(8,128)(2,1)S(1)}, bf16[1120,1280]{1,0:T(8,128)(2,1)}, u32[]{:S(2)}) copy-start(bf16[1120,1280]{1,0:T(8,128)(2,1)} %constant.44.clone) | copy-start | bytes 8601604
  107.4 1.9 %copy-start.1 = (bf16[16,176,384]{2,1,0:T(8,128)(2,1)S(1)}, bf16[16,176,384]{2,1,0:T(8,128)(2,1)}, u32[]{:S(2)}) copy-start(bf16[16,176,384]{2,1,0:T(8,128)(2,1)} %copy-done) | copy-start | bytes 6488068
  107.4 2.3 %copy-start.3 = (bf16[16,176,384]{2,1,0:T(8,128)(2,1)S(1)}, bf16[16,176,384]{2,1,0:T(8,128)(2,1)}, u32[]{:S(2)}) copy-start(bf16[16,176,384]{2,1,0:T(8,128)(2,1)} %copy-done.2) | copy-start | bytes 6488068
  107.4 2.2 %copy-start.4 = (bf16[256,256]{1,0:T(8,128)(2,1)S(1)}, bf16[256,256]{1,0:T(8,128)(2,1)}, u32[]{:S(2)}) copy-start(bf16[256,256]{1,0:T(8,128)(2,1)} %constant.45.clone.order) | copy-start | bytes 393220
  124.5 14.7 %copy-start.6 = (bf16[256,256]{1,0:T(8,128)(2,1)S(1)}, bf16[256,256]{1,0:T(8,128)(2,1)}, u32[]{:S(2)}) copy-start(bf16[256,256]{1,0:T(8,128)(2,1)} %constant.46.clone.order) | copy-start | bytes 393220
  124.5 14.7 %copy-start.7 = (bf16[128,128]{1,0:T(8,128)(2,1)S(1)}, bf16[128,128]{1,0:T(8,128)(2,1)}, u32[]{:S(2)}) copy-start(bf16[128,128]{1,0:T(8,128)(2,1)} %constant.47.clone.back_order) | copy-start | bytes 98308
  124.5 14.7 %all-to-all-start.2 = ((bf16[16,16,768]{2,1,0:T(8,128)(2,1)}), bf16[16,16,768]{2,1,0:T(8,128)(2,1)S(1)}, u32[]{:S(2)}, u32[]{:S(2)}) async-start(bf16[16,16,768]{2,1,0:T(8,128)(2,1)} %bitcast.15), calls=%async_computation.2 | async-start | bytes 786432 | tf_op jit(solution)/shard_map/all_to_all | solution.py:53
  145.3 12.0 %all-to-all-start.3 = ((bf16[16,8,768]{2,1,0:T(8,128)(2,1)}), bf16[16,8,768]{2,1,0:T(8,128)(2,1)S(1)}, u32[]{:S(2)}, u32[]{:S(2)}) async-start(bf16[16,8,768]{2,1,0:T(8,128)(2,1)} %bitcast.17), calls=%async_computation.3 | async-start | bytes 393216 | tf_op jit(solution)/shard_map/all_to_all | solution.py:53
  151.9 1.0 copy-start.9
  153.1 4.2 %copy-start.5 = (bf16[128,128]{1,0:T(8,128)(2,1)S(1)}, bf16[128,128]{1,0:T(8,128)(2,1)}, u32[]{:S(2)}) copy-start(bf16[128,128]{1,0:T(8,128)(2,1)} %constant.43.clone.order) | copy-start | bytes 98308

commit v4 on v3

--- a/solution.py
+++ b/solution.py
@@ -111,34 +111,33 @@
     latent_out,
     w_mine,
     w_part,
-    latents,
 ):
     core, zh = flags[0], flags[1]
-    members = x_all.shape[1] // (4 * OWN)
     lanes = own_m.shape[2]
     lifts, outs = 6 * lanes // 32, 2 * lanes // 32
     front = lifts + BLOCK
     width = 2 * lanes
 
-    @pl.when(pl.program_id(0) == 0)
-    def _():
-        for target, own, other in ((w_mine, own_m, other_m), (w_part, own_p, other_p)):
-            for place in range(16):
-                target[2 * lifts * place : 2 * lifts * (place + 1), :] = in_order(
-                    zh, own[place, :lifts, :], other[place, :lifts, :], 0
-                )
+    for target, own, other in ((w_mine, own_m, other_m), (w_part, own_p, other_p)):
+        for place in range(16):
+            target[2 * lifts * place : 2 * lifts * (place + 1), :] = in_order(
+                zh, own[place, :lifts, :], other[place, :lifts, :], 0
+            )
 
     def embed(own, other):
         return times(x_own, own[:, lifts:front, :].reshape(SIDE, lanes)) + times(
             x_other, other[:, lifts:front, :].reshape(SIDE, lanes)
         )
 
-    x = x_all[0]
+    groups, count = x_all.shape[0], x_all.shape[1] // 2
+    x = jnp.concatenate(
+        [x_all[g, i * count : (i + 1) * count, :] for i in range(2) for g in range(groups)], axis=0
+    )
     x_own, x_other = halves(zh, x)
     hidden = in_order(core, embed(own_m, other_m), embed(own_p, other_p), 1).astype(bf16)
     normed = normalized(hidden.astype(f32)).astype(bf16)
     n_mine, n_part = halves(core, normed)
-    own_rows = 2 * members * OWN
+    own_rows = groups * count
 
     same = (iota((GROUP, GROUP), 0) // HEAD) == (iota((GROUP, GROUP), 1) // HEAD)
     ones = same.astype(bf16)
@@ -149,21 +148,20 @@
         return (times_t(left, w_mine[rows, :]) + times_t(right, w_part[rows, :])).astype(bf16)
 
     def unit(values):
+        total = times(values * values, ones)
         values = values.astype(f32)
-        high, low = two_parts(values * values)
-        total = times(high, ones) + times(low, ones)
         return (values * lax.rsqrt(total + normalizing_guard)).astype(bf16)
 
     def diagonal(rows):
         zero = jnp.zeros_like(rows)
         return jnp.concatenate([jnp.where(lane_head == h, rows, zero) for h in range(4)], axis=0)
 
-    def pane_rows(values, w, m):
-        own = values[(w * members + m) * OWN : (w * members + m + 1) * OWN]
-        start = own_rows + (w * members + m) * OWN
-        return jnp.concatenate([own, values[start : start + OWN]], axis=0)
-
-    panes = [(w, m) for w in range(2) for m in range(members)]
+    def pane_rows(values, i):
+        return jnp.concatenate(
+            [values[i * OWN : (i + 1) * OWN], values[own_rows + i * OWN :][:OWN]], axis=0
+        )
+
+    panes = own_rows // OWN
     context = []
     for g in range(width // GROUP):
         at = g * GROUP
@@ -171,14 +169,14 @@
         key_rows = unit(projected(n_mine, n_part, width + at))
         value_rows = projected(n_mine, n_part, 2 * width + at)
         scores = [
-            times_t(query[i * OWN : (i + 1) * OWN], diagonal(pane_rows(key_rows, w, m)))
-            for i, (w, m) in enumerate(panes)
+            times_t(query[i * OWN : (i + 1) * OWN], diagonal(pane_rows(key_rows, i)))
+            for i in range(panes)
         ]
         weights = jnp.exp(jnp.concatenate(scores, axis=0) * scale[:, at : at + GROUP]).astype(bf16)
         total = times(weights, ones)
         mixed = [
-            times(weights[i * OWN : (i + 1) * OWN], diagonal(pane_rows(value_rows, w, m)))
-            for i, (w, m) in enumerate(panes)
+            times(weights[i * OWN : (i + 1) * OWN], diagonal(pane_rows(value_rows, i)))
+            for i in range(panes)
         ]
         context.append((jnp.concatenate(mixed, axis=0) / total).astype(bf16))
     c_mine, c_part = halves(core, jnp.concatenate(context, axis=1))
@@ -194,35 +192,19 @@
 
     mixed = times_t(c_mine, combiner(own_m, other_m)) + times_t(c_part, combiner(own_p, other_p))
     latent = normalized(hidden[:own_rows].astype(f32) + mixed).astype(bf16)
-    latents[pl.ds(pl.multiple_of(pl.program_id(0) * own_rows, own_rows), own_rows), :] = latent
-
-    @pl.when(pl.program_id(0) == pl.num_programs(0) - 1)
-    def _():
-        latent_out[...] = times(order[...], latents[...]).astype(bf16)
+    latent_out[...] = times(order[...], latent).astype(bf16)
 
 
 def front_latents(flags, states, weights, scale, order):
     lanes = weights[0].shape[2]
-    groups, count, wide = states.shape
-    shape = (order.shape[0], 2 * lanes)
-
-    def whole(array):
-        return pl.BlockSpec(
-            array.shape, lambda i: (0,) * array.ndim, pipeline_mode=pl.Buffered(1)
-        )
-
+    vmem = pl.BlockSpec(memory_space=pltpu.VMEM)
     return pl.pallas_call(
         front_kernel,
-        grid=(groups,),
-        in_specs=[
-            pl.BlockSpec(memory_space=pltpu.SMEM),
-            pl.BlockSpec((1, count, wide), lambda i: (i, 0, 0)),
-        ]
-        + [whole(v) for v in (*weights, scale, order)],
-        out_specs=pl.BlockSpec(shape, lambda i: (0, 0)),
-        out_shape=jax.ShapeDtypeStruct(shape, bf16),
-        scratch_shapes=[pltpu.VMEM((6 * lanes, lanes), bf16)] * 2 + [pltpu.VMEM(shape, bf16)],
-        compiler_params=pltpu.CompilerParams(vmem_limit_bytes=32 * 1024 * 1024),
+        in_specs=[pl.BlockSpec(memory_space=pltpu.SMEM)] + [vmem] * (3 + len(weights)),
+        out_specs=vmem,
+        out_shape=jax.ShapeDtypeStruct((order.shape[0], 2 * lanes), bf16),
+        scratch_shapes=[pltpu.VMEM((6 * lanes, lanes), bf16)] * 2,
+        compiler_params=pltpu.CompilerParams(vmem_limit_bytes=16 * 1024 * 1024),
         name="front",
     )(flags, states, *weights, scale, order)
 
@@ -328,7 +310,7 @@
         in_specs=[pl.BlockSpec(memory_space=pltpu.SMEM)] + [vmem] * 6,
         out_specs=vmem,
         out_shape=jax.ShapeDtypeStruct((back_order.shape[0], moved.shape[1]), bf16),
-        compiler_params=pltpu.CompilerParams(vmem_limit_bytes=32 * 1024 * 1024),
+        compiler_params=pltpu.CompilerParams(vmem_limit_bytes=12 * 1024 * 1024),
         name="analysis",
     )(flags, moved, order, back_order, obs, t_mine, t_part)
 
@@ -345,7 +327,7 @@
         in_specs=[pl.BlockSpec(memory_space=pltpu.SMEM)] + [vmem] * 4,
         out_specs=vmem,
         out_shape=jax.ShapeDtypeStruct((order.shape[0], d_mine.shape[0]), bf16),
-        compiler_params=pltpu.CompilerParams(vmem_limit_bytes=32 * 1024 * 1024),
+        compiler_params=pltpu.CompilerParams(vmem_limit_bytes=12 * 1024 * 1024),
         name="decode",
     )(flags, parts, order, d_mine, d_part)
 
@@ -427,9 +409,10 @@
         sensor_variable_loadings.reshape(16, 2, SHARD), ((0, 0), (0, 0), (0, BLOCK - SHARD))
     ).reshape(16, 2 * BLOCK)
     readers = times(loadings, decoder).astype(bf16)
-    copies, own_all, up, down = lax.optimization_barrier(
-        (copies_of(jnp.concatenate([theirs, readers], axis=0)), own_all, up, down)
-    )
+    copies, own_all = lax.optimization_barrier(
+        (copies_of(jnp.concatenate([theirs, readers], axis=0)), own_all)
+    )
+    up, down, own_sent = lax.optimization_barrier((up, down, own_all))
     partner = jnp.concatenate([shifted(up, 4), shifted(down, -4)], axis=0)
     other_main = exchanged(copies)
     inside = np.arange(BLOCK)[None, None, :]
@@ -446,7 +429,7 @@
     states = times(states.reshape(4 * count, feats), pick_cols).astype(bf16)
     states = states.reshape(2, 2 * count, 2 * SIDE)
 
-    own_all_p = swapped(own_all, "core")
+    own_all_p = swapped(own_sent, "core")
     other_main, own_all_p, _ = lax.optimization_barrier((other_main, own_all_p, partner))
     other_main_p = swapped(other_main, "core")
     scale = jnp.repeat(cosine_logit_scale, HEAD)[None, :]

time: 160 us -> 153 us (0.956)
  waiting for transfers between devices: 40.9 us -> 35.1 us
  Pallas kernels: 24.9 us -> 21.5 us
    pallas_call x1, Pallas kernels: 14.7 us -> 11.4 us  [front_latents(): pl.pallas_call(front_kernel, in_specs=[pl.BlockSpec(memory_space=pltpu.SM...]
    ppermute x4, waiting for transfers between devices: 16.6 us -> 13.6 us  [shifted(): lax.ppermute(value, ('zh', 'zl'), [(z, (z + by) % 16) for z in range(16)])]
    all_to_all x4, waiting for transfers between devices: 10.9 us -> 8.17 us  [exchanged(): lax.all_to_all(blocks, PLANE, split_axis=0, concat_axis=0, tiled=True)]
  transfers between devices with their start and end apart: 13 -> 13, of which waited for: 8 -> 5; matrix products, arithmetic and copies ran while one was open for 7% -> 7% of each run, Pallas kernels for 1% -> 1%
where the time goes in v4:
time: 153 us; the launch traced here: 152 us
  starting transfers between devices  77.5 us (51%)
  waiting for transfers between devices  35.1 us (23%)
  Pallas kernels  21.5 us (14%)
  local copies, waits for them, and re-layouts  9.2 us (6%)
  other arithmetic  5.61 us (4%)
  matrix products  2.5 us (2%)
    all_to_all x4, starting transfers between devices, exchanged(): lax.all_to_all(blocks, PLANE, split_axis=0, concat_axis=0, tiled=True)  29.5 us
    ppermute x4, starting transfers between devices, shifted(): lax.ppermute(value, ('zh', 'zl'), [(z, (z + by) % 16) for z in range(16)])  20.3 us
    ppermute x4, waiting for transfers between devices, shifted(): lax.ppermute(value, ('zh', 'zl'), [(z, (z + by) % 16) for z in range(16)])  13.6 us
    pallas_call x1, Pallas kernels, front_latents(): pl.pallas_call(front_kernel, in_specs=[pl.BlockSpec(memory_space=pltpu.SM...  11.4 us
    ppermute x1, starting transfers between devices, between_chips(): return lax.ppermute(value, TILE, pairs + [(b, a) for a, b in pairs])  11.2 us
    ppermute x1, starting transfers between devices, crossed(): return lax.ppermute(value, ('zh', 'zl'), pairs)  10.8 us
    all_to_all x4, waiting for transfers between devices, exchanged(): lax.all_to_all(blocks, PLANE, split_axis=0, concat_axis=0, tiled=True)  8.17 us
    ppermute x1, waiting for transfers between devices, crossed(): return lax.ppermute(value, ('zh', 'zl'), pairs)  7.94 us
  transfers between devices with their start and end apart: 13, of which 5 were waited for; matrix products, arithmetic and copies ran while one was open for 7% of the time, Pallas kernels for 1%

profile of v4, /device:TPU:8, one launch (start us, length us, event | category | flops | bytes accessed | tf_op | source)
XLA Modules:
  0.0 151.8 jit_solution(886621966335555532)
XLA Ops:
  0.0 1.0 fusion.9
  1.0 1.6 %broadcast_in_dim.7 = bf16[16,176,384]{2,1,0:T(8,128)(2,1)} broadcast(bf16[176,384]{1,0:T(8,128)(2,1)S(1)} %slice_select_fusion), dimensions={1,2} | broadcast | bytes 2297856 | tf_op jit(solution)/shard_map/broadcast_in_dim | solution.py:49
  2.6 9.5 %all-to-all-start = ((bf16[16,176,384]{2,1,0:T(8,128)(2,1)}), bf16[16,176,384]{2,1,0:T(8,128)(2,1)S(1)}, u32[]{:S(2)}, u32[]{:S(2)}) async-start(bf16[16,176,384]{2,1,0:T(8,128)(2,1)} %broadcast_in_dim.7), calls=%async_computation | async-start | bytes 4325376 | tf_op jit(solution)/shard_map/all_to_all | solution.py:53
  12.1 2.0 %prepare.1 = bf16[144,1120]{1,0:T(8,128)(2,1)} custom-call(bf16[128,1120]{1,0:T(8,128)(2,1)} %bitcast.51, bf16[128,128]{1,0:T(8,128)(2,1)} %constant.43.clone.order, s32[1,256]{1,0:T(1,128)} %bitcast.57, s32[1,256]{1,0:T(1,128)} %bitcast.58, s32[1,256]{1,0:T(1,128)} %bitcast.59, f32[1,256]{1,0:T(1,128)} %bitcast.60, f32[1,256]{1,0:T(1,128)} %bitcast.61), custom_call_target="tpu_custom_call" | custom-call | tf_op jit(solution)/shard_map/prepare/pallas_call | solution.py:227
  14.0 10.8 %collective-permute-start.2 = (bf16[176,384]{1,0:T(8,128)(2,1)S(1)}, bf16[176,384]{1,0:T(8,128)(2,1)S(1)}, u32[]{:S(2)}, u32[]{:S(2)}) collective-permute-start(bf16[176,384]{1,0:T(8,128)(2,1)S(1)} %slice_select_fusion), channel_id=1, source_target_pairs={{0,24},{2,26},{4,28},{6,30},{8,16},{10,18},{12,20},{14,22},{16,8},... | collective-permute-start | bytes 405512 | tf_op jit(solution)/shard_map/ppermute | solution.py:40
  24.8 1.0 fusion.28
  25.9 5.5 %collective-permute-start = (bf16[72,1120]{1,0:T(8,128)(2,1)S(1)}, bf16[72,1120]{1,0:T(8,128)(2,1)S(1)}, u32[]{:S(2)}, u32[]{:S(2)}) collective-permute-start(bf16[72,1120]{1,0:T(8,128)(2,1)S(1)} %get-tuple-element.40), channel_id=1, source_target_pairs={{0,8},{2,10},{4,12},{6,14},{8,16},{10,18},{12,20},{14,22},{16,24},... | collective-permute-start | bytes 483848 | tf_op jit(solution)/shard_map/ppermute | solution.py:35
  31.3 4.3 %collective-permute-start.1 = (bf16[72,1120]{1,0:T(8,128)(2,1)S(1)}, bf16[72,1120]{1,0:T(8,128)(2,1)S(1)}, u32[]{:S(2)}, u32[]{:S(2)}) collective-permute-start(bf16[72,1120]{1,0:T(8,128)(2,1)S(1)} %get-tuple-element.39), channel_id=1, source_target_pairs={{0,24},{2,26},{4,28},{6,30},{8,0},{10,2},{12,4},{14,6},{16,8},{18,... | collective-permute-start | bytes 483848 | tf_op jit(solution)/shard_map/ppermute | solution.py:35
  35.6 0.1 reshape.80
  35.7 0.1 reshape.81
  35.8 7.9 %collective-permute-done.2 = bf16[176,384]{1,0:T(8,128)(2,1)S(1)} collective-permute-done((bf16[176,384]{1,0:T(8,128)(2,1)S(1)}, bf16[176,384]{1,0:T(8,128)(2,1)S(1)}, u32[]{:S(2)}, u32[]{:S(2)}) %collective-permute-start.2) | collective-permute-done | bytes 135200 | tf_op jit(solution)/shard_map/ppermute | solution.py:40
  43.8 0.1 convolution_convert_fusion.1
  43.9 1.7 %broadcast_in_dim.6 = bf16[16,192,384]{2,1,0:T(8,128)(2,1)} broadcast(bf16[192,384]{1,0:T(8,128)(2,1)S(1)} %pad_maximum_fusion.4), dimensions={1,2} | broadcast | bytes 2506752 | tf_op jit(solution)/shard_map/broadcast_in_dim | solution.py:49
  45.7 1.4 copy-done
  47.1 7.3 %all-to-all-start.1 = ((bf16[16,192,384]{2,1,0:T(8,128)(2,1)}), bf16[16,192,384]{2,1,0:T(8,128)(2,1)S(1)}, u32[]{:S(2)}, u32[]{:S(2)}) async-start(bf16[16,192,384]{2,1,0:T(8,128)(2,1)} %broadcast_in_dim.6), calls=%async_computation.1 | async-start | bytes 4718592 | tf_op jit(solution)/shard_map/all_to_all | solution.py:53
  54.4 1.9 %collective-permute-start.7 = (bf16[16,176,384]{2,1,0:T(8,128)(2,1)}, bf16[16,176,384]{2,1,0:T(8,128)(2,1)S(1)}, u32[]{:S(2)}, u32[]{:S(2)}) collective-permute-start(bf16[16,176,384]{2,1,0:T(8,128)(2,1)} %copy-done), channel_id=1, source_target_pairs={{0,1},{1,0},{2,3},{3,2},{4,5},{5,4},{6,7},{7,6},{8,9},{9,8},{10,11... | collective-permute-start | bytes 6488072 | tf_op jit(solution)/shard_map/ppermute | solution.py:31
  56.3 4.2 %collective-permute-start.3 = (bf16[72,1120]{1,0:T(8,128)(2,1)S(1)}, bf16[72,1120]{1,0:T(8,128)(2,1)S(1)}, u32[]{:S(2)}, u32[]{:S(2)}) collective-permute-start(bf16[72,1120]{1,0:T(8,128)(2,1)S(1)} %collective-permute-done), channel_id=1, source_target_pairs={{0,8},{2,10},{4,12},{6,14},{8,16},{10,18},{12,20},{14,22},{16,24},... | collective-permute-start | bytes 483848 | tf_op jit(solution)/shard_map/ppermute | solution.py:35
  60.5 6.3 %collective-permute-start.4 = (bf16[72,1120]{1,0:T(8,128)(2,1)S(1)}, bf16[72,1120]{1,0:T(8,128)(2,1)S(1)}, u32[]{:S(2)}, u32[]{:S(2)}) collective-permute-start(bf16[72,1120]{1,0:T(8,128)(2,1)S(1)} %collective-permute-done.1), channel_id=1, source_target_pairs={{0,24},{2,26},{4,28},{6,30},{8,0},{10,2},{12,4},{14,6},{16,8},{18,... | collective-permute-start | bytes 483848 | tf_op jit(solution)/shard_map/ppermute | solution.py:35
  66.9 13.6 %collective-permute-done.3 = bf16[72,1120]{1,0:T(8,128)(2,1)S(1)} collective-permute-done((bf16[72,1120]{1,0:T(8,128)(2,1)S(1)}, bf16[72,1120]{1,0:T(8,128)(2,1)S(1)}, u32[]{:S(2)}, u32[]{:S(2)}) %collective-permute-start.3) | collective-permute-done | bytes 161312 | tf_op jit(solution)/shard_map/ppermute | solution.py:35
  80.6 1.4 copy-done.2
  81.9 1.9 %collective-permute-start.8 = (bf16[16,192,384]{2,1,0:T(8,128)(2,1)S(1)}, bf16[16,192,384]{2,1,0:T(8,128)(2,1)}, u32[]{:S(2)}, u32[]{:S(2)}) collective-permute-start(bf16[16,192,384]{2,1,0:T(8,128)(2,1)S(1)} %all-to-all-done.1.other_m.t_mine), channel_id=1, source_target_pairs={{0,1},{1,0},{2,3},{3,2},{4,5},{5,4},{6,7},{7,6},{8,9},{9,8},{10,11... | collective-permute-start | bytes 7077896 | tf_op jit(solution)/shard_map/ppermute | solution.py:31
  83.9 0.1 broadcast_in_dim.8
  83.9 0.1 broadcast_in_dim_reshape.3.scale
  84.0 0.1 pad_add_fusion.flags
  84.1 0.1 broadcast_select_fusion.3
  84.2 11.2 %collective-permute-start.5 = (bf16[2,64,1120]{2,1,0:T(8,128)(2,1)S(1)}, bf16[2,64,1120]{2,1,0:T(8,128)(2,1)S(1)}, u32[]{:S(2)}, u32[]{:S(2)}) collective-permute-start(bf16[2,64,1120]{2,1,0:T(8,128)(2,1)S(1)} %get-tuple-element.35), channel_id=1, source_target_pairs={{0,15},{2,1},{4,3},{6,5},{8,7},{10,9},{12,11},{14,13},{15,0},{1,2}... | collective-permute-start | bytes 860168 | tf_op jit(solution)/shard_map/ppermute | solution.py:45
  95.4 1.9 %collective-permute-start.6 = (bf16[2,64,1120]{2,1,0:T(8,128)(2,1)S(1)}, bf16[2,64,1120]{2,1,0:T(8,128)(2,1)S(1)}, u32[]{:S(2)}, u32[]{:S(2)}) collective-permute-start(bf16[2,64,1120]{2,1,0:T(8,128)(2,1)S(1)} %get-tuple-element.36), channel_id=1, source_target_pairs={{0,1},{1,0},{2,3},{3,2},{4,5},{5,4},{6,7},{7,6},{8,9},{9,8},{10,11... | collective-permute-start | bytes 860168 | tf_op jit(solution)/shard_map/ppermute | solution.py:31
  97.4 0.1 fusion.1
  97.5 5.3 %collective-permute-done.5 = bf16[2,64,1120]{2,1,0:T(8,128)(2,1)S(1)} collective-permute-done((bf16[2,64,1120]{2,1,0:T(8,128)(2,1)S(1)}, bf16[2,64,1120]{2,1,0:T(8,128)(2,1)S(1)}, u32[]{:S(2)}, u32[]{:S(2)}) %collective-permute-start.5) | collective-permute-done | bytes 286752 | tf_op jit(solution)/shard_map/ppermute | solution.py:45
  102.8 0.1 pad_maximum_fusion
  103.0 1.9 %convolution_convert_fusion = bf16[512,1280]{1,0:T(8,128)(2,1)S(1)} fusion(bf16[512,1120]{1,0:T(8,128)(2,1)S(1)} %bitcast.50, bf16[1120,1280]{1,0:T(8,128)(2,1)S(1)} %copy-done.12), kind=kOutput, calls=%fused_computation | convolution fusion | flops 1468661760 | bytes 5324800 | tf_op jit(solution)/shard_map/dot_general | solution.py:57
  104.9 0.3 copy-done.3
  105.2 11.4 %front.1 = bf16[256,768]{1,0:T(8,128)(2,1)} custom-call(s32[2]{0:T(128)S(1)} %pad_add_fusion.flags, bf16[2,256,1280]{2,1,0:T(8,128)(2,1)S(1)} %bitcast.42, bf16[16,176,384]{2,1,0:T(8,128)(2,1)S(1)} %copy-done.1, bf16[16,192,384]{2,1,0:T(8,128)(2,1)S(1)} %all-to-all-done.1.other_m.t_mine, bf16[16,176,384]{2,1,0:T(8,128)(2,1)S(1)} %copy-done.3, ...), custom_call_target="tpu_custom_call" | custom-call | tf_op jit(solution)/shard_map/front/pallas_call | solution.py:201
  116.7 7.4 %all-to-all-start.2 = ((bf16[16,16,768]{2,1,0:T(8,128)(2,1)}), bf16[16,16,768]{2,1,0:T(8,128)(2,1)S(1)}, u32[]{:S(2)}, u32[]{:S(2)}) async-start(bf16[16,16,768]{2,1,0:T(8,128)(2,1)} %bitcast.15), calls=%async_computation.2 | async-start | bytes 786432 | tf_op jit(solution)/shard_map/all_to_all | solution.py:53
  124.2 0.5 fusion.obs
  124.7 2.6 %select_bitcast_fusion.1 = (bf16[16,1,35,384]{3,2,0,1:T(8,128)(2,1)S(1)}, bf16[16,1,35,384]{3,2,0,1:T(8,128)(2,1)}, bf16[16,1,35,384]{3,2,0,1:T(8,128)(2,1)}, bf16[16,1,35,384]{3,2,0,1:T(8,128)(2,1)}) fusion(pred[]{:T(512)S(6)} %eq.19, bf16[16,192,384]{2,1,0:T(8,128)(2,1)} %collective-permute-done.8.other_p.t_part, bf16[16,176,384]{2,1,0:T(8,128)(2,1)} %copy-done.2, ...), kind=kLoop, calls=%fused_computation.20 | loop fusion | flops 860160 | bytes 3440641 | tf_op jit(solution)/shard_map/jit(_where)/select_n | solution.py:71
  127.3 4.4 %all-to-all-done.2 = bf16[16,16,768]{2,1,0:T(8,128)(2,1)S(1)} async-done(((bf16[16,16,768]{2,1,0:T(8,128)(2,1)}), bf16[16,16,768]{2,1,0:T(8,128)(2,1)S(1)}, u32[]{:S(2)}, u32[]{:S(2)}) %all-to-all-start.2) | async-done | bytes 393248 | tf_op jit(solution)/shard_map/all_to_all | solution.py:53
  131.7 6.1 %analysis.1 = bf16[128,768]{1,0:T(8,128)(2,1)} custom-call(s32[2]{0:T(128)S(1)} %pad_add_fusion.flags, bf16[256,768]{1,0:T(8,128)(2,1)S(1)} %bitcast.41, bf16[256,256]{1,0:T(8,128)(2,1)S(1)} %copy-done.6, bf16[128,128]{1,0:T(8,128)(2,1)S(1)} %copy-done.7, f32[2,4,512]{2,1,0:T(4,128)S(1)} %fusion.obs, ...), custom_call_target="tpu_custom_call" | custom-call | tf_op jit(solution)/shard_map/analysis/pallas_call | solution.py:308
  137.8 5.3 %all-to-all-start.3 = ((bf16[16,8,768]{2,1,0:T(8,128)(2,1)}), bf16[16,8,768]{2,1,0:T(8,128)(2,1)S(1)}, u32[]{:S(2)}, u32[]{:S(2)}) async-start(bf16[16,8,768]{2,1,0:T(8,128)(2,1)} %bitcast.17), calls=%async_computation.3 | async-start | bytes 393216 | tf_op jit(solution)/shard_map/all_to_all | solution.py:53
  143.1 1.3 pad_maximum_fusion.1
  144.4 0.1 copy.21
  144.5 0.3 reshape.88.d_mine
  144.8 0.6 copy-done.9
  145.4 0.1 pad_maximum_fusion.2
  145.6 0.1 copy.22
  145.7 0.3 reshape.89.d_part
  146.0 3.8 %all-to-all-done.3 = bf16[16,8,768]{2,1,0:T(8,128)(2,1)S(1)} async-done(((bf16[16,8,768]{2,1,0:T(8,128)(2,1)}), bf16[16,8,768]{2,1,0:T(8,128)(2,1)S(1)}, u32[]{:S(2)}, u32[]{:S(2)}) %all-to-all-start.3) | async-done | bytes 196640 | tf_op jit(solution)/shard_map/all_to_all | solution.py:53
  149.8 2.1 %decode.1 = bf16[128,1120]{1,0:T(8,128)(2,1)} custom-call(s32[2]{0:T(128)S(1)} %pad_add_fusion.flags, bf16[128,768]{1,0:T(8,128)(2,1)S(1)} %bitcast.43, bf16[128,128]{1,0:T(8,128)(2,1)S(1)} %copy-done.5, bf16[1120,384]{1,0:T(8,128)(2,1)S(1)} %reshape.88.d_mine, bf16[1120,384]{1,0:T(8,128)(2,1)S(1)} %reshape.89.d_part), custom_call_target="tpu_custom_call" | custom-call | tf_op jit(solution)/shard_map/decode/pallas_call | solution.py:325
  (46 shorter events, 0.3 us)
Async XLA Ops:
  2.6 33.0 %copy-start.10 = (bf16[16,70]{1,0:T(8,128)(2,1)S(1)}, bf16[16,70]{1,0:T(8,128)(2,1)}, u32[]{:S(2)}) copy-start(bf16[16,70]{1,0:T(8,128)(2,1)} %param.24) | copy-start | bytes 6724
  2.6 43.1 %all-to-all-start = ((bf16[16,176,384]{2,1,0:T(8,128)(2,1)}), bf16[16,176,384]{2,1,0:T(8,128)(2,1)S(1)}, u32[]{:S(2)}, u32[]{:S(2)}) async-start(bf16[16,176,384]{2,1,0:T(8,128)(2,1)} %broadcast_in_dim.7), calls=%async_computation | async-start | bytes 4325376 | tf_op jit(solution)/shard_map/all_to_all | solution.py:53
  14.0 29.7 %collective-permute-start.2 = (bf16[176,384]{1,0:T(8,128)(2,1)S(1)}, bf16[176,384]{1,0:T(8,128)(2,1)S(1)}, u32[]{:S(2)}, u32[]{:S(2)}) collective-permute-start(bf16[176,384]{1,0:T(8,128)(2,1)S(1)} %slice_select_fusion), channel_id=1, source_target_pairs={{0,24},{2,26},{4,28},{6,30},{8,16},{10,18},{12,20},{14,22},{16,8},... | collective-permute-start | bytes 405512 | tf_op jit(solution)/shard_map/ppermute | solution.py:40
  25.9 28.5 %collective-permute-start = (bf16[72,1120]{1,0:T(8,128)(2,1)S(1)}, bf16[72,1120]{1,0:T(8,128)(2,1)S(1)}, u32[]{:S(2)}, u32[]{:S(2)}) collective-permute-start(bf16[72,1120]{1,0:T(8,128)(2,1)S(1)} %get-tuple-element.40), channel_id=1, source_target_pairs={{0,8},{2,10},{4,12},{6,14},{8,16},{10,18},{12,20},{14,22},{16,24},... | collective-permute-start | bytes 483848 | tf_op jit(solution)/shard_map/ppermute | solution.py:35
  31.3 23.1 %collective-permute-start.1 = (bf16[72,1120]{1,0:T(8,128)(2,1)S(1)}, bf16[72,1120]{1,0:T(8,128)(2,1)S(1)}, u32[]{:S(2)}, u32[]{:S(2)}) collective-permute-start(bf16[72,1120]{1,0:T(8,128)(2,1)S(1)} %get-tuple-element.39), channel_id=1, source_target_pairs={{0,24},{2,26},{4,28},{6,30},{8,0},{10,2},{12,4},{14,6},{16,8},{18,... | collective-permute-start | bytes 483848 | tf_op jit(solution)/shard_map/ppermute | solution.py:35
  45.7 38.2 %copy-start.11 = (f32[12]{0:T(128)S(1)}, f32[12]{0:T(128)}, u32[]{:S(2)}) copy-start(f32[12]{0:T(128)} %param.23) | copy-start | bytes 148
  45.7 38.4 %copy-start.8 = (bf16[144,1120]{1,0:T(8,128)(2,1)S(1)}, bf16[144,1120]{1,0:T(8,128)(2,1)}, u32[]{:S(2)}) copy-start(bf16[144,1120]{1,0:T(8,128)(2,1)} %prepare.1) | copy-start | bytes 967684
  45.7 1.4 copy-start
  47.1 34.9 %all-to-all-start.1 = ((bf16[16,192,384]{2,1,0:T(8,128)(2,1)}), bf16[16,192,384]{2,1,0:T(8,128)(2,1)S(1)}, u32[]{:S(2)}, u32[]{:S(2)}) async-start(bf16[16,192,384]{2,1,0:T(8,128)(2,1)} %broadcast_in_dim.6), calls=%async_computation.1 | async-start | bytes 4718592 | tf_op jit(solution)/shard_map/all_to_all | solution.py:53
  54.4 26.1 %collective-permute-start.7 = (bf16[16,176,384]{2,1,0:T(8,128)(2,1)}, bf16[16,176,384]{2,1,0:T(8,128)(2,1)S(1)}, u32[]{:S(2)}, u32[]{:S(2)}) collective-permute-start(bf16[16,176,384]{2,1,0:T(8,128)(2,1)} %copy-done), channel_id=1, source_target_pairs={{0,1},{1,0},{2,3},{3,2},{4,5},{5,4},{6,7},{7,6},{8,9},{9,8},{10,11... | collective-permute-start | bytes 6488072 | tf_op jit(solution)/shard_map/ppermute | solution.py:31
  56.3 24.2 %collective-permute-start.3 = (bf16[72,1120]{1,0:T(8,128)(2,1)S(1)}, bf16[72,1120]{1,0:T(8,128)(2,1)S(1)}, u32[]{:S(2)}, u32[]{:S(2)}) collective-permute-start(bf16[72,1120]{1,0:T(8,128)(2,1)S(1)} %collective-permute-done), channel_id=1, source_target_pairs={{0,8},{2,10},{4,12},{6,14},{8,16},{10,18},{12,20},{14,22},{16,24},... | collective-permute-start | bytes 483848 | tf_op jit(solution)/shard_map/ppermute | solution.py:35
  60.5 20.0 %collective-permute-start.4 = (bf16[72,1120]{1,0:T(8,128)(2,1)S(1)}, bf16[72,1120]{1,0:T(8,128)(2,1)S(1)}, u32[]{:S(2)}, u32[]{:S(2)}) collective-permute-start(bf16[72,1120]{1,0:T(8,128)(2,1)S(1)} %collective-permute-done.1), channel_id=1, source_target_pairs={{0,24},{2,26},{4,28},{6,30},{8,0},{10,2},{12,4},{14,6},{16,8},{18,... | collective-permute-start | bytes 483848 | tf_op jit(solution)/shard_map/ppermute | solution.py:35
  80.5 1.4 copy-start.2
  81.9 23.0 %collective-permute-start.8 = (bf16[16,192,384]{2,1,0:T(8,128)(2,1)S(1)}, bf16[16,192,384]{2,1,0:T(8,128)(2,1)}, u32[]{:S(2)}, u32[]{:S(2)}) collective-permute-start(bf16[16,192,384]{2,1,0:T(8,128)(2,1)S(1)} %all-to-all-done.1.other_m.t_mine), channel_id=1, source_target_pairs={{0,1},{1,0},{2,3},{3,2},{4,5},{5,4},{6,7},{7,6},{8,9},{9,8},{10,11... | collective-permute-start | bytes 7077896 | tf_op jit(solution)/shard_map/ppermute | solution.py:31
  84.2 18.6 %collective-permute-start.5 = (bf16[2,64,1120]{2,1,0:T(8,128)(2,1)S(1)}, bf16[2,64,1120]{2,1,0:T(8,128)(2,1)S(1)}, u32[]{:S(2)}, u32[]{:S(2)}) collective-permute-start(bf16[2,64,1120]{2,1,0:T(8,128)(2,1)S(1)} %get-tuple-element.35), channel_id=1, source_target_pairs={{0,15},{2,1},{4,3},{6,5},{8,7},{10,9},{12,11},{14,13},{15,0},{1,2}... | collective-permute-start | bytes 860168 | tf_op jit(solution)/shard_map/ppermute | solution.py:45
  95.4 7.4 %collective-permute-start.6 = (bf16[2,64,1120]{2,1,0:T(8,128)(2,1)S(1)}, bf16[2,64,1120]{2,1,0:T(8,128)(2,1)S(1)}, u32[]{:S(2)}, u32[]{:S(2)}) collective-permute-start(bf16[2,64,1120]{2,1,0:T(8,128)(2,1)S(1)} %get-tuple-element.36), channel_id=1, source_target_pairs={{0,1},{1,0},{2,3},{3,2},{4,5},{5,4},{6,7},{7,6},{8,9},{9,8},{10,11... | collective-permute-start | bytes 860168 | tf_op jit(solution)/shard_map/ppermute | solution.py:31
  97.4 5.6 %copy-start.12 = (bf16[1120,1280]{1,0:T(8,128)(2,1)S(1)}, bf16[1120,1280]{1,0:T(8,128)(2,1)}, u32[]{:S(2)}) copy-start(bf16[1120,1280]{1,0:T(8,128)(2,1)} %constant.44.clone) | copy-start | bytes 8601604
  103.0 1.9 %copy-start.1 = (bf16[16,176,384]{2,1,0:T(8,128)(2,1)S(1)}, bf16[16,176,384]{2,1,0:T(8,128)(2,1)}, u32[]{:S(2)}) copy-start(bf16[16,176,384]{2,1,0:T(8,128)(2,1)} %copy-done) | copy-start | bytes 6488068
  103.0 2.3 %copy-start.3 = (bf16[16,176,384]{2,1,0:T(8,128)(2,1)S(1)}, bf16[16,176,384]{2,1,0:T(8,128)(2,1)}, u32[]{:S(2)}) copy-start(bf16[16,176,384]{2,1,0:T(8,128)(2,1)} %copy-done.2) | copy-start | bytes 6488068
  103.0 2.2 %copy-start.4 = (bf16[256,256]{1,0:T(8,128)(2,1)S(1)}, bf16[256,256]{1,0:T(8,128)(2,1)}, u32[]{:S(2)}) copy-start(bf16[256,256]{1,0:T(8,128)(2,1)} %constant.45.clone.order) | copy-start | bytes 393220
  116.7 15.0 %copy-start.6 = (bf16[256,256]{1,0:T(8,128)(2,1)S(1)}, bf16[256,256]{1,0:T(8,128)(2,1)}, u32[]{:S(2)}) copy-start(bf16[256,256]{1,0:T(8,128)(2,1)} %constant.46.clone.order) | copy-start | bytes 393220
  116.7 15.0 %copy-start.7 = (bf16[128,128]{1,0:T(8,128)(2,1)S(1)}, bf16[128,128]{1,0:T(8,128)(2,1)}, u32[]{:S(2)}) copy-start(bf16[128,128]{1,0:T(8,128)(2,1)} %constant.47.clone.back_order) | copy-start | bytes 98308
  116.7 15.0 %all-to-all-start.2 = ((bf16[16,16,768]{2,1,0:T(8,128)(2,1)}), bf16[16,16,768]{2,1,0:T(8,128)(2,1)S(1)}, u32[]{:S(2)}, u32[]{:S(2)}) async-start(bf16[16,16,768]{2,1,0:T(8,128)(2,1)} %bitcast.15), calls=%async_computation.2 | async-start | bytes 786432 | tf_op jit(solution)/shard_map/all_to_all | solution.py:53
  137.8 12.0 %all-to-all-start.3 = ((bf16[16,8,768]{2,1,0:T(8,128)(2,1)}), bf16[16,8,768]{2,1,0:T(8,128)(2,1)S(1)}, u32[]{:S(2)}, u32[]{:S(2)}) async-start(bf16[16,8,768]{2,1,0:T(8,128)(2,1)} %bitcast.17), calls=%async_computation.3 | async-start | bytes 393216 | tf_op jit(solution)/shard_map/all_to_all | solution.py:53
  144.4 1.0 copy-start.9
  145.6 4.2 %copy-start.5 = (bf16[128,128]{1,0:T(8,128)(2,1)S(1)}, bf16[128,128]{1,0:T(8,128)(2,1)}, u32[]{:S(2)}) copy-start(bf16[128,128]{1,0:T(8,128)(2,1)} %constant.43.clone.order) | copy-start | bytes 98308

commit v5 on v4

--- a/solution.py
+++ b/solution.py
@@ -36,7 +36,7 @@
 
 
 def crossed(value):
-    pairs = [(8 * h + z, 8 * (1 - h) + (z + 4) % 8) for h in range(2) for z in range(8)]
+    pairs = [(z, 15 - z) for z in range(16)]
     return lax.ppermute(value, ("zh", "zl"), pairs)
 
 
@@ -251,15 +251,12 @@
     )
 
 
-def analysis_kernel(flags, moved, order, back_order, obs, t_mine, t_part, posterior_out):
+def analysis_kernel(flags, moved, order, back_order, obs, r_mine, r_part, posterior_out):
     latent = times(order[...], moved[...]).astype(bf16)
     members = latent.shape[0] // HALF
     l_mine, l_part = halves(flags[0], latent)
 
-    def readers(ref):
-        return ref[:, ref.shape[1] - 16 :, :].reshape(16 * 16, ref.shape[2])
-
-    seen = times_t(l_mine, readers(t_mine)) + times_t(l_part, readers(t_part))
+    seen = times_t(l_mine, r_mine[...]) + times_t(l_part, r_part[...])
     eye = (iota((members, members), 0) == iota((members, members), 1)).astype(f32)
     systems, drives = [], []
     for block in range(2):
@@ -303,7 +300,7 @@
     posterior_out[...] = times(back_order[...], posterior).astype(bf16)
 
 
-def analysis(flags, moved, order, back_order, obs, t_mine, t_part):
+def analysis(flags, moved, order, back_order, obs, r_mine, r_part):
     vmem = pl.BlockSpec(memory_space=pltpu.VMEM)
     return pl.pallas_call(
         analysis_kernel,
@@ -312,7 +309,7 @@
         out_shape=jax.ShapeDtypeStruct((back_order.shape[0], moved.shape[1]), bf16),
         compiler_params=pltpu.CompilerParams(vmem_limit_bytes=12 * 1024 * 1024),
         name="analysis",
-    )(flags, moved, order, back_order, obs, t_mine, t_part)
+    )(flags, moved, order, back_order, obs, r_mine, r_part)
 
 
 def decode_kernel(flags, parts, order, d_mine, d_part, out):
@@ -438,9 +435,10 @@
     grid = np.arange(size).reshape(2, 2, members, rows, HALF)
     order = one_hot(grid.transpose(3, 1, 0, 2, 4).reshape(-1), size)
     latent = front_latents(flags, states, weights, scale, order)
-    tables, latent, own_all, own_all_p = lax.optimization_barrier(
-        (both[:, count:], latent, own_all, own_all_p)
-    )
+    tables, latent, own_all, own_all_p, other_main, other_main_p = lax.optimization_barrier(
+        (both[:, count:], latent, own_all, own_all_p, other_main, other_main_p)
+    )
+    readers = [array[:, -16:].reshape(16 * 16, lanes) for array in (other_main, other_main_p)]
     obs = weighted_places(in_order(zh, tables[:1], tables[1:], 0), sensor_gridpoint.size)
     moved = exchanged(latent.reshape(16, size // 16, width)).reshape(size, width)
 
@@ -448,7 +446,7 @@
     order = one_hot(grid.transpose(3, 1, 0, 2).reshape(-1), size)
     grid = np.arange(count).reshape(HALF, 16, members)
     back_order = one_hot(grid.transpose(1, 2, 0).reshape(-1), count)
-    posterior = analysis(flags, moved, order, back_order, obs, other_main, other_main_p)
+    posterior = analysis(flags, moved, order, back_order, obs, *readers)
     back = exchanged(posterior.reshape(16, count // 16, width)).reshape(count, width)
 
     def strip(own, other):

time: 153 us -> 151 us (0.987)
  starting transfers between devices: 77.5 us -> 67.5 us
  waiting for transfers between devices: 35.1 us -> 43.7 us
    ppermute x4, waiting for transfers between devices: 13.6 us -> 21.8 us  [shifted(): lax.ppermute(value, ('zh', 'zl'), [(z, (z + by) % 16) for z in range(16)])]
    ppermute x1, starting transfers between devices: 11.2 us -> 3.09 us  [between_chips(): return lax.ppermute(value, TILE, pairs + [(b, a) for a, b in pairs])]
    ppermute x1, waiting for transfers between devices: 5.31 us -> 9.62 us  [between_chips(): return lax.ppermute(value, TILE, pairs + [(b, a) for a, b in pairs])]
    ppermute x1, waiting for transfers between devices: 7.94 us -> 5.41 us  [crossed(): return lax.ppermute(value, ('zh', 'zl'), pairs)]
    unnamed x30 -> x32, local copies, waits for them, and re-layouts: 3.77 us -> 3.9 us
  transfers between devices with their start and end apart: 13 -> 13, of which waited for: 5 -> 7; matrix products, arithmetic and copies ran while one was open for 7% -> 8% of each run, Pallas kernels for 1% -> 1%
where the time goes in v5:
time: 151 us
  starting transfers between devices  67.5 us (45%)
  waiting for transfers between devices  43.7 us (29%)
  Pallas kernels  20.4 us (14%)
  local copies, waits for them, and re-layouts  10.4 us (7%)
  other arithmetic  5.77 us (4%)
  matrix products  2.5 us (2%)
    all_to_all x4, starting transfers between devices, exchanged(): lax.all_to_all(blocks, PLANE, split_axis=0, concat_axis=0, tiled=True)  29.3 us
    ppermute x4, waiting for transfers between devices, shifted(): lax.ppermute(value, ('zh', 'zl'), [(z, (z + by) % 16) for z in range(16)])  21.8 us
    ppermute x4, starting transfers between devices, shifted(): lax.ppermute(value, ('zh', 'zl'), [(z, (z + by) % 16) for z in range(16)])  19.8 us
    pallas_call x1, Pallas kernels, front_latents(): pl.pallas_call(front_kernel, in_specs=[pl.BlockSpec(memory_space=pltpu.SM...  11.4 us
    ppermute x1, waiting for transfers between devices, between_chips(): return lax.ppermute(value, TILE, pairs + [(b, a) for a, b in pairs])  9.62 us
    ppermute x1, starting transfers between devices, crossed(): return lax.ppermute(value, ('zh', 'zl'), pairs)  9.45 us
    all_to_all x4, waiting for transfers between devices, exchanged(): lax.all_to_all(blocks, PLANE, split_axis=0, concat_axis=0, tiled=True)  6.83 us
    ppermute x3, starting transfers between devices, swapped(): return lax.ppermute(value, axis, [(0, 1), (1, 0)])  5.8 us
  transfers between devices with their start and end apart: 13, of which 7 were waited for; matrix products, arithmetic and copies ran while one was open for 8% of the time, Pallas kernels for 1%

profile of v5, /device:TPU:8, one launch (start us, length us, event | category | flops | bytes accessed | tf_op | source)
XLA Modules:
  0.0 150.5 jit_solution(15743719403090680147)
XLA Ops:
  0.0 1.0 fusion.9
  1.0 1.6 %broadcast_in_dim.7 = bf16[16,176,384]{2,1,0:T(8,128)(2,1)} broadcast(bf16[176,384]{1,0:T(8,128)(2,1)S(1)} %slice_select_fusion), dimensions={1,2} | broadcast | bytes 2297856 | tf_op jit(solution)/shard_map/broadcast_in_dim | solution.py:49
  2.6 9.5 %all-to-all-start = ((bf16[16,176,384]{2,1,0:T(8,128)(2,1)}), bf16[16,176,384]{2,1,0:T(8,128)(2,1)S(1)}, u32[]{:S(2)}, u32[]{:S(2)}) async-start(bf16[16,176,384]{2,1,0:T(8,128)(2,1)} %broadcast_in_dim.7), calls=%async_computation | async-start | bytes 4325376 | tf_op jit(solution)/shard_map/all_to_all | solution.py:53
  12.1 2.0 %prepare.1 = bf16[144,1120]{1,0:T(8,128)(2,1)} custom-call(bf16[128,1120]{1,0:T(8,128)(2,1)} %bitcast.55, bf16[128,128]{1,0:T(8,128)(2,1)} %constant.43.clone.order, s32[1,256]{1,0:T(1,128)} %bitcast.61, s32[1,256]{1,0:T(1,128)} %bitcast.62, s32[1,256]{1,0:T(1,128)} %bitcast.63, f32[1,256]{1,0:T(1,128)} %bitcast.64, f32[1,256]{1,0:T(1,128)} %bitcast.65), custom_call_target="tpu_custom_call" | custom-call | tf_op jit(solution)/shard_map/prepare/pallas_call | solution.py:227
  14.0 9.5 %collective-permute-start.2 = (bf16[176,384]{1,0:T(8,128)(2,1)S(1)}, bf16[176,384]{1,0:T(8,128)(2,1)S(1)}, u32[]{:S(2)}, u32[]{:S(2)}) collective-permute-start(bf16[176,384]{1,0:T(8,128)(2,1)S(1)} %slice_select_fusion), channel_id=1, source_target_pairs={{0,30},{2,28},{4,26},{6,24},{8,22},{10,20},{12,18},{14,16},{16,14}... | collective-permute-start | bytes 405512 | tf_op jit(solution)/shard_map/ppermute | solution.py:40
  23.5 1.0 fusion.28
  24.5 8.2 %collective-permute-start = (bf16[72,1120]{1,0:T(8,128)(2,1)S(1)}, bf16[72,1120]{1,0:T(8,128)(2,1)S(1)}, u32[]{:S(2)}, u32[]{:S(2)}) collective-permute-start(bf16[72,1120]{1,0:T(8,128)(2,1)S(1)} %get-tuple-element.44), channel_id=1, source_target_pairs={{0,8},{2,10},{4,12},{6,14},{8,16},{10,18},{12,20},{14,22},{16,24},... | collective-permute-start | bytes 483848 | tf_op jit(solution)/shard_map/ppermute | solution.py:35
  32.7 1.9 %collective-permute-start.1 = (bf16[72,1120]{1,0:T(8,128)(2,1)S(1)}, bf16[72,1120]{1,0:T(8,128)(2,1)S(1)}, u32[]{:S(2)}, u32[]{:S(2)}) collective-permute-start(bf16[72,1120]{1,0:T(8,128)(2,1)S(1)} %get-tuple-element.43), channel_id=1, source_target_pairs={{0,24},{2,26},{4,28},{6,30},{8,0},{10,2},{12,4},{14,6},{16,8},{18,... | collective-permute-start | bytes 483848 | tf_op jit(solution)/shard_map/ppermute | solution.py:35
  34.6 0.1 reshape.86
  34.7 0.1 reshape.87
  34.8 5.4 %collective-permute-done.2 = bf16[176,384]{1,0:T(8,128)(2,1)S(1)} collective-permute-done((bf16[176,384]{1,0:T(8,128)(2,1)S(1)}, bf16[176,384]{1,0:T(8,128)(2,1)S(1)}, u32[]{:S(2)}, u32[]{:S(2)}) %collective-permute-start.2) | collective-permute-done | bytes 135200 | tf_op jit(solution)/shard_map/ppermute | solution.py:40
  40.2 0.1 convolution_convert_fusion.1
  40.4 1.7 %broadcast_in_dim.6 = bf16[16,192,384]{2,1,0:T(8,128)(2,1)} broadcast(bf16[192,384]{1,0:T(8,128)(2,1)S(1)} %pad_maximum_fusion.4), dimensions={1,2} | broadcast | bytes 2506752 | tf_op jit(solution)/shard_map/broadcast_in_dim | solution.py:49
  42.1 1.4 copy-done
  43.5 7.2 %all-to-all-start.1 = ((bf16[16,192,384]{2,1,0:T(8,128)(2,1)}), bf16[16,192,384]{2,1,0:T(8,128)(2,1)S(1)}, u32[]{:S(2)}, u32[]{:S(2)}) async-start(bf16[16,192,384]{2,1,0:T(8,128)(2,1)} %broadcast_in_dim.6), calls=%async_computation.1 | async-start | bytes 4718592 | tf_op jit(solution)/shard_map/all_to_all | solution.py:53
  50.7 1.9 %collective-permute-done.1 = bf16[72,1120]{1,0:T(8,128)(2,1)S(1)} collective-permute-done((bf16[72,1120]{1,0:T(8,128)(2,1)S(1)}, bf16[72,1120]{1,0:T(8,128)(2,1)S(1)}, u32[]{:S(2)}, u32[]{:S(2)}) %collective-permute-start.1) | collective-permute-done | bytes 161312 | tf_op jit(solution)/shard_map/ppermute | solution.py:35
  52.7 1.9 %collective-permute-start.7 = (bf16[16,176,384]{2,1,0:T(8,128)(2,1)}, bf16[16,176,384]{2,1,0:T(8,128)(2,1)S(1)}, u32[]{:S(2)}, u32[]{:S(2)}) collective-permute-start(bf16[16,176,384]{2,1,0:T(8,128)(2,1)} %copy-done), channel_id=1, source_target_pairs={{0,1},{1,0},{2,3},{3,2},{4,5},{5,4},{6,7},{7,6},{8,9},{9,8},{10,11... | collective-permute-start | bytes 6488072 | tf_op jit(solution)/shard_map/ppermute | solution.py:31
  54.6 3.5 %collective-permute-start.3 = (bf16[72,1120]{1,0:T(8,128)(2,1)S(1)}, bf16[72,1120]{1,0:T(8,128)(2,1)S(1)}, u32[]{:S(2)}, u32[]{:S(2)}) collective-permute-start(bf16[72,1120]{1,0:T(8,128)(2,1)S(1)} %collective-permute-done), channel_id=1, source_target_pairs={{0,8},{2,10},{4,12},{6,14},{8,16},{10,18},{12,20},{14,22},{16,24},... | collective-permute-start | bytes 483848 | tf_op jit(solution)/shard_map/ppermute | solution.py:35
  58.1 6.2 %collective-permute-start.4 = (bf16[72,1120]{1,0:T(8,128)(2,1)S(1)}, bf16[72,1120]{1,0:T(8,128)(2,1)S(1)}, u32[]{:S(2)}, u32[]{:S(2)}) collective-permute-start(bf16[72,1120]{1,0:T(8,128)(2,1)S(1)} %collective-permute-done.1), channel_id=1, source_target_pairs={{0,24},{2,26},{4,28},{6,30},{8,0},{10,2},{12,4},{14,6},{16,8},{18,... | collective-permute-start | bytes 483848 | tf_op jit(solution)/shard_map/ppermute | solution.py:35
  64.3 5.0 %collective-permute-done.3 = bf16[72,1120]{1,0:T(8,128)(2,1)S(1)} collective-permute-done((bf16[72,1120]{1,0:T(8,128)(2,1)S(1)}, bf16[72,1120]{1,0:T(8,128)(2,1)S(1)}, u32[]{:S(2)}, u32[]{:S(2)}) %collective-permute-start.3) | collective-permute-done | bytes 161312 | tf_op jit(solution)/shard_map/ppermute | solution.py:35
  69.3 14.9 %collective-permute-done.4 = bf16[72,1120]{1,0:T(8,128)(2,1)S(1)} collective-permute-done((bf16[72,1120]{1,0:T(8,128)(2,1)S(1)}, bf16[72,1120]{1,0:T(8,128)(2,1)S(1)}, u32[]{:S(2)}, u32[]{:S(2)}) %collective-permute-start.4) | collective-permute-done | bytes 161312 | tf_op jit(solution)/shard_map/ppermute | solution.py:35
  84.3 1.4 copy-done.2
  85.7 2.0 %collective-permute-start.8 = (bf16[16,192,384]{2,1,0:T(8,128)(2,1)S(1)}, bf16[16,192,384]{2,1,0:T(8,128)(2,1)}, u32[]{:S(2)}, u32[]{:S(2)}) collective-permute-start(bf16[16,192,384]{2,1,0:T(8,128)(2,1)S(1)} %all-to-all-done.1.other_m), channel_id=1, source_target_pairs={{0,1},{1,0},{2,3},{3,2},{4,5},{5,4},{6,7},{7,6},{8,9},{9,8},{10,11... | collective-permute-start | bytes 7077896 | tf_op jit(solution)/shard_map/ppermute | solution.py:31
  87.9 0.1 broadcast_select_fusion.3
  88.0 3.1 %collective-permute-start.5 = (bf16[2,64,1120]{2,1,0:T(8,128)(2,1)S(1)}, bf16[2,64,1120]{2,1,0:T(8,128)(2,1)S(1)}, u32[]{:S(2)}, u32[]{:S(2)}) collective-permute-start(bf16[2,64,1120]{2,1,0:T(8,128)(2,1)S(1)} %get-tuple-element.39), channel_id=1, source_target_pairs={{0,15},{2,1},{4,3},{6,5},{8,7},{10,9},{12,11},{14,13},{15,0},{1,2}... | collective-permute-start | bytes 860168 | tf_op jit(solution)/shard_map/ppermute | solution.py:45
  91.1 1.9 %collective-permute-start.6 = (bf16[2,64,1120]{2,1,0:T(8,128)(2,1)S(1)}, bf16[2,64,1120]{2,1,0:T(8,128)(2,1)S(1)}, u32[]{:S(2)}, u32[]{:S(2)}) collective-permute-start(bf16[2,64,1120]{2,1,0:T(8,128)(2,1)S(1)} %get-tuple-element.40), channel_id=1, source_target_pairs={{0,1},{1,0},{2,3},{3,2},{4,5},{5,4},{6,7},{7,6},{8,9},{9,8},{10,11... | collective-permute-start | bytes 860168 | tf_op jit(solution)/shard_map/ppermute | solution.py:31
  93.1 9.6 %collective-permute-done.5 = bf16[2,64,1120]{2,1,0:T(8,128)(2,1)S(1)} collective-permute-done((bf16[2,64,1120]{2,1,0:T(8,128)(2,1)S(1)}, bf16[2,64,1120]{2,1,0:T(8,128)(2,1)S(1)}, u32[]{:S(2)}, u32[]{:S(2)}) %collective-permute-start.5) | collective-permute-done | bytes 286752 | tf_op jit(solution)/shard_map/ppermute | solution.py:45
  102.8 0.1 pad_maximum_fusion
  103.0 1.9 %convolution_convert_fusion = bf16[512,1280]{1,0:T(8,128)(2,1)S(1)} fusion(bf16[512,1120]{1,0:T(8,128)(2,1)S(1)} %bitcast.54, bf16[1120,1280]{1,0:T(8,128)(2,1)S(1)} %copy-done.13), kind=kOutput, calls=%fused_computation | convolution fusion | flops 1468661760 | bytes 5324800 | tf_op jit(solution)/shard_map/dot_general | solution.py:57
  104.9 0.3 copy-done.3
  105.2 11.4 %front.1 = bf16[256,768]{1,0:T(8,128)(2,1)} custom-call(s32[2]{0:T(128)S(1)} %pad_add_fusion.flags, bf16[2,256,1280]{2,1,0:T(8,128)(2,1)S(1)} %bitcast.44, bf16[16,176,384]{2,1,0:T(8,128)(2,1)S(1)} %copy-done.1, bf16[16,192,384]{2,1,0:T(8,128)(2,1)S(1)} %all-to-all-done.1.other_m, bf16[16,176,384]{2,1,0:T(8,128)(2,1)S(1)} %copy-done.3, ...), custom_call_target="tpu_custom_call" | custom-call | tf_op jit(solution)/shard_map/front/pallas_call | solution.py:201
  116.7 7.3 %all-to-all-start.2 = ((bf16[16,16,768]{2,1,0:T(8,128)(2,1)}), bf16[16,16,768]{2,1,0:T(8,128)(2,1)S(1)}, u32[]{:S(2)}, u32[]{:S(2)}) async-start(bf16[16,16,768]{2,1,0:T(8,128)(2,1)} %bitcast.15), calls=%async_computation.2 | async-start | bytes 786432 | tf_op jit(solution)/shard_map/all_to_all | solution.py:53
  124.0 0.5 fusion.obs
  124.6 1.0 slice.107
  125.6 2.8 %select_bitcast_fusion.1 = (bf16[16,1,35,384]{3,2,0,1:T(8,128)(2,1)}, bf16[16,1,35,384]{3,2,0,1:T(8,128)(2,1)}, bf16[16,1,35,384]{3,2,0,1:T(8,128)(2,1)}, bf16[16,1,35,384]{3,2,0,1:T(8,128)(2,1)}) fusion(pred[]{:T(512)S(6)} %eq.19, bf16[16,192,384]{2,1,0:T(8,128)(2,1)} %collective-permute-done.8.other_p, bf16[16,176,384]{2,1,0:T(8,128)(2,1)} %copy-done.2, ...), kind=kLoop, calls=%fused_computation.20 | loop fusion | flops 860160 | bytes 3440641 | tf_op jit(solution)/shard_map/jit(_where)/select_n | solution.py:71
  128.3 3.2 %all-to-all-done.2 = bf16[16,16,768]{2,1,0:T(8,128)(2,1)S(1)} async-done(((bf16[16,16,768]{2,1,0:T(8,128)(2,1)}), bf16[16,16,768]{2,1,0:T(8,128)(2,1)S(1)}, u32[]{:S(2)}, u32[]{:S(2)}) %all-to-all-start.2) | async-done | bytes 393248 | tf_op jit(solution)/shard_map/all_to_all | solution.py:53
  131.5 5.0 %analysis.1 = bf16[128,768]{1,0:T(8,128)(2,1)} custom-call(s32[2]{0:T(128)S(1)} %pad_add_fusion.flags, bf16[256,768]{1,0:T(8,128)(2,1)S(1)} %bitcast.43, bf16[256,256]{1,0:T(8,128)(2,1)S(1)} %copy-done.6, bf16[128,128]{1,0:T(8,128)(2,1)S(1)} %copy-done.7, f32[2,4,512]{2,1,0:T(4,128)S(1)} %fusion.obs, bf16[256,384]{1,0:T(8,128)(2,1)S(1)} %bitcast.46, ...), custom_call_target="tpu_custom_call" | custom-call | tf_op jit(solution)/shard_map/analysis/pallas_call | solution.py:305
  136.5 5.3 %all-to-all-start.3 = ((bf16[16,8,768]{2,1,0:T(8,128)(2,1)}), bf16[16,8,768]{2,1,0:T(8,128)(2,1)S(1)}, u32[]{:S(2)}, u32[]{:S(2)}) async-start(bf16[16,8,768]{2,1,0:T(8,128)(2,1)} %bitcast.19), calls=%async_computation.3 | async-start | bytes 393216 | tf_op jit(solution)/shard_map/all_to_all | solution.py:53
  141.8 1.3 pad_maximum_fusion.1
  143.1 0.1 copy.21
  143.2 0.3 reshape.96.d_mine
  143.5 0.6 copy-done.9
  144.1 0.1 copy-done.10
  144.3 0.1 pad_maximum_fusion.2
  144.4 0.1 copy.22
  144.5 0.3 reshape.97.d_part
  144.8 3.6 %all-to-all-done.3 = bf16[16,8,768]{2,1,0:T(8,128)(2,1)S(1)} async-done(((bf16[16,8,768]{2,1,0:T(8,128)(2,1)}), bf16[16,8,768]{2,1,0:T(8,128)(2,1)S(1)}, u32[]{:S(2)}, u32[]{:S(2)}) %all-to-all-start.3) | async-done | bytes 196640 | tf_op jit(solution)/shard_map/all_to_all | solution.py:53
  148.5 2.1 %decode.1 = bf16[128,1120]{1,0:T(8,128)(2,1)} custom-call(s32[2]{0:T(128)S(1)} %pad_add_fusion.flags, bf16[128,768]{1,0:T(8,128)(2,1)S(1)} %bitcast.45, bf16[128,128]{1,0:T(8,128)(2,1)S(1)} %copy-done.5, bf16[1120,384]{1,0:T(8,128)(2,1)S(1)} %reshape.96.d_mine, bf16[1120,384]{1,0:T(8,128)(2,1)S(1)} %reshape.97.d_part), custom_call_target="tpu_custom_call" | custom-call | tf_op jit(solution)/shard_map/decode/pallas_call | solution.py:322
  (50 shorter events, 0.7 us)
Async XLA Ops:
  2.6 32.0 %copy-start.11 = (bf16[16,70]{1,0:T(8,128)(2,1)S(1)}, bf16[16,70]{1,0:T(8,128)(2,1)}, u32[]{:S(2)}) copy-start(bf16[16,70]{1,0:T(8,128)(2,1)} %param.24) | copy-start | bytes 6724
  2.6 39.5 %all-to-all-start = ((bf16[16,176,384]{2,1,0:T(8,128)(2,1)}), bf16[16,176,384]{2,1,0:T(8,128)(2,1)S(1)}, u32[]{:S(2)}, u32[]{:S(2)}) async-start(bf16[16,176,384]{2,1,0:T(8,128)(2,1)} %broadcast_in_dim.7), calls=%async_computation | async-start | bytes 4325376 | tf_op jit(solution)/shard_map/all_to_all | solution.py:53
  14.0 26.2 %collective-permute-start.2 = (bf16[176,384]{1,0:T(8,128)(2,1)S(1)}, bf16[176,384]{1,0:T(8,128)(2,1)S(1)}, u32[]{:S(2)}, u32[]{:S(2)}) collective-permute-start(bf16[176,384]{1,0:T(8,128)(2,1)S(1)} %slice_select_fusion), channel_id=1, source_target_pairs={{0,30},{2,28},{4,26},{6,24},{8,22},{10,20},{12,18},{14,16},{16,14}... | collective-permute-start | bytes 405512 | tf_op jit(solution)/shard_map/ppermute | solution.py:40
  24.5 26.2 %collective-permute-start = (bf16[72,1120]{1,0:T(8,128)(2,1)S(1)}, bf16[72,1120]{1,0:T(8,128)(2,1)S(1)}, u32[]{:S(2)}, u32[]{:S(2)}) collective-permute-start(bf16[72,1120]{1,0:T(8,128)(2,1)S(1)} %get-tuple-element.44), channel_id=1, source_target_pairs={{0,8},{2,10},{4,12},{6,14},{8,16},{10,18},{12,20},{14,22},{16,24},... | collective-permute-start | bytes 483848 | tf_op jit(solution)/shard_map/ppermute | solution.py:35
  32.7 20.0 %collective-permute-start.1 = (bf16[72,1120]{1,0:T(8,128)(2,1)S(1)}, bf16[72,1120]{1,0:T(8,128)(2,1)S(1)}, u32[]{:S(2)}, u32[]{:S(2)}) collective-permute-start(bf16[72,1120]{1,0:T(8,128)(2,1)S(1)} %get-tuple-element.43), channel_id=1, source_target_pairs={{0,24},{2,26},{4,28},{6,30},{8,0},{10,2},{12,4},{14,6},{16,8},{18,... | collective-permute-start | bytes 483848 | tf_op jit(solution)/shard_map/ppermute | solution.py:35
  42.1 45.5 %copy-start.12 = (f32[12]{0:T(128)S(1)}, f32[12]{0:T(128)}, u32[]{:S(2)}) copy-start(f32[12]{0:T(128)} %param.23) | copy-start | bytes 148
  42.1 45.8 %copy-start.8 = (bf16[144,1120]{1,0:T(8,128)(2,1)S(1)}, bf16[144,1120]{1,0:T(8,128)(2,1)}, u32[]{:S(2)}) copy-start(bf16[144,1120]{1,0:T(8,128)(2,1)} %prepare.1) | copy-start | bytes 967684
  42.1 1.4 copy-start
  43.5 42.2 %all-to-all-start.1 = ((bf16[16,192,384]{2,1,0:T(8,128)(2,1)}), bf16[16,192,384]{2,1,0:T(8,128)(2,1)S(1)}, u32[]{:S(2)}, u32[]{:S(2)}) async-start(bf16[16,192,384]{2,1,0:T(8,128)(2,1)} %broadcast_in_dim.6), calls=%async_computation.1 | async-start | bytes 4718592 | tf_op jit(solution)/shard_map/all_to_all | solution.py:53
  52.7 31.6 %collective-permute-start.7 = (bf16[16,176,384]{2,1,0:T(8,128)(2,1)}, bf16[16,176,384]{2,1,0:T(8,128)(2,1)S(1)}, u32[]{:S(2)}, u32[]{:S(2)}) collective-permute-start(bf16[16,176,384]{2,1,0:T(8,128)(2,1)} %copy-done), channel_id=1, source_target_pairs={{0,1},{1,0},{2,3},{3,2},{4,5},{5,4},{6,7},{7,6},{8,9},{9,8},{10,11... | collective-permute-start | bytes 6488072 | tf_op jit(solution)/shard_map/ppermute | solution.py:31
  54.6 14.7 %collective-permute-start.3 = (bf16[72,1120]{1,0:T(8,128)(2,1)S(1)}, bf16[72,1120]{1,0:T(8,128)(2,1)S(1)}, u32[]{:S(2)}, u32[]{:S(2)}) collective-permute-start(bf16[72,1120]{1,0:T(8,128)(2,1)S(1)} %collective-permute-done), channel_id=1, source_target_pairs={{0,8},{2,10},{4,12},{6,14},{8,16},{10,18},{12,20},{14,22},{16,24},... | collective-permute-start | bytes 483848 | tf_op jit(solution)/shard_map/ppermute | solution.py:35
  58.1 26.1 %collective-permute-start.4 = (bf16[72,1120]{1,0:T(8,128)(2,1)S(1)}, bf16[72,1120]{1,0:T(8,128)(2,1)S(1)}, u32[]{:S(2)}, u32[]{:S(2)}) collective-permute-start(bf16[72,1120]{1,0:T(8,128)(2,1)S(1)} %collective-permute-done.1), channel_id=1, source_target_pairs={{0,24},{2,26},{4,28},{6,30},{8,0},{10,2},{12,4},{14,6},{16,8},{18,... | collective-permute-start | bytes 483848 | tf_op jit(solution)/shard_map/ppermute | solution.py:35
  84.3 1.4 copy-start.2
  85.7 19.2 %collective-permute-start.8 = (bf16[16,192,384]{2,1,0:T(8,128)(2,1)S(1)}, bf16[16,192,384]{2,1,0:T(8,128)(2,1)}, u32[]{:S(2)}, u32[]{:S(2)}) collective-permute-start(bf16[16,192,384]{2,1,0:T(8,128)(2,1)S(1)} %all-to-all-done.1.other_m), channel_id=1, source_target_pairs={{0,1},{1,0},{2,3},{3,2},{4,5},{5,4},{6,7},{7,6},{8,9},{9,8},{10,11... | collective-permute-start | bytes 7077896 | tf_op jit(solution)/shard_map/ppermute | solution.py:31
  88.0 14.8 %collective-permute-start.5 = (bf16[2,64,1120]{2,1,0:T(8,128)(2,1)S(1)}, bf16[2,64,1120]{2,1,0:T(8,128)(2,1)S(1)}, u32[]{:S(2)}, u32[]{:S(2)}) collective-permute-start(bf16[2,64,1120]{2,1,0:T(8,128)(2,1)S(1)} %get-tuple-element.39), channel_id=1, source_target_pairs={{0,15},{2,1},{4,3},{6,5},{8,7},{10,9},{12,11},{14,13},{15,0},{1,2}... | collective-permute-start | bytes 860168 | tf_op jit(solution)/shard_map/ppermute | solution.py:45
  91.1 11.7 %collective-permute-start.6 = (bf16[2,64,1120]{2,1,0:T(8,128)(2,1)S(1)}, bf16[2,64,1120]{2,1,0:T(8,128)(2,1)S(1)}, u32[]{:S(2)}, u32[]{:S(2)}) collective-permute-start(bf16[2,64,1120]{2,1,0:T(8,128)(2,1)S(1)} %get-tuple-element.40), channel_id=1, source_target_pairs={{0,1},{1,0},{2,3},{3,2},{4,5},{5,4},{6,7},{7,6},{8,9},{9,8},{10,11... | collective-permute-start | bytes 860168 | tf_op jit(solution)/shard_map/ppermute | solution.py:31
  93.1 9.9 %copy-start.13 = (bf16[1120,1280]{1,0:T(8,128)(2,1)S(1)}, bf16[1120,1280]{1,0:T(8,128)(2,1)}, u32[]{:S(2)}) copy-start(bf16[1120,1280]{1,0:T(8,128)(2,1)} %constant.44.clone) | copy-start | bytes 8601604
  102.9 1.9 %copy-start.1 = (bf16[16,176,384]{2,1,0:T(8,128)(2,1)S(1)}, bf16[16,176,384]{2,1,0:T(8,128)(2,1)}, u32[]{:S(2)}) copy-start(bf16[16,176,384]{2,1,0:T(8,128)(2,1)} %copy-done) | copy-start | bytes 6488068
  103.0 2.3 %copy-start.3 = (bf16[16,176,384]{2,1,0:T(8,128)(2,1)S(1)}, bf16[16,176,384]{2,1,0:T(8,128)(2,1)}, u32[]{:S(2)}) copy-start(bf16[16,176,384]{2,1,0:T(8,128)(2,1)} %copy-done.2) | copy-start | bytes 6488068
  103.0 2.2 %copy-start.4 = (bf16[256,256]{1,0:T(8,128)(2,1)S(1)}, bf16[256,256]{1,0:T(8,128)(2,1)}, u32[]{:S(2)}) copy-start(bf16[256,256]{1,0:T(8,128)(2,1)} %constant.45.clone.order) | copy-start | bytes 393220
  116.7 14.8 %all-to-all-start.2 = ((bf16[16,16,768]{2,1,0:T(8,128)(2,1)}), bf16[16,16,768]{2,1,0:T(8,128)(2,1)S(1)}, u32[]{:S(2)}, u32[]{:S(2)}) async-start(bf16[16,16,768]{2,1,0:T(8,128)(2,1)} %bitcast.15), calls=%async_computation.2 | async-start | bytes 786432 | tf_op jit(solution)/shard_map/all_to_all | solution.py:53
  124.5 7.0 %copy-start.6 = (bf16[256,256]{1,0:T(8,128)(2,1)S(1)}, bf16[256,256]{1,0:T(8,128)(2,1)}, u32[]{:S(2)}) copy-start(bf16[256,256]{1,0:T(8,128)(2,1)} %constant.46.clone.order) | copy-start | bytes 393220
  124.5 7.0 %copy-start.7 = (bf16[128,128]{1,0:T(8,128)(2,1)S(1)}, bf16[128,128]{1,0:T(8,128)(2,1)}, u32[]{:S(2)}) copy-start(bf16[128,128]{1,0:T(8,128)(2,1)} %constant.47.clone.back_order) | copy-start | bytes 98308
  136.5 12.0 %all-to-all-start.3 = ((bf16[16,8,768]{2,1,0:T(8,128)(2,1)}), bf16[16,8,768]{2,1,0:T(8,128)(2,1)S(1)}, u32[]{:S(2)}, u32[]{:S(2)}) async-start(bf16[16,8,768]{2,1,0:T(8,128)(2,1)} %bitcast.19), calls=%async_computation.3 | async-start | bytes 393216 | tf_op jit(solution)/shard_map/all_to_all | solution.py:53
  143.1 1.0 copy-start.9
  143.1 1.2 copy-start.10
  144.4 4.0 %copy-start.5 = (bf16[128,128]{1,0:T(8,128)(2,1)S(1)}, bf16[128,128]{1,0:T(8,128)(2,1)}, u32[]{:S(2)}) copy-start(bf16[128,128]{1,0:T(8,128)(2,1)} %constant.43.clone.order) | copy-start | bytes 98308

commit v6 on v5

--- a/solution.py
+++ b/solution.py
@@ -215,10 +215,11 @@
     table = [grid[...].astype(f32), domain[...].astype(f32), channel[...].astype(f32)]
     table = [t.astype(bf16) for t in table]
     table += list(three_parts(reading[...])) + list(three_parts(noise[...]))
-    table = jnp.concatenate([t.astype(f32) for t in table], axis=0)
-    packed[count:, :] = jnp.zeros((16, packed.shape[1]), bf16)
-    table = jnp.concatenate([table, jnp.zeros((16 - table.shape[0], table.shape[1]), f32)], axis=0)
-    packed[count:, : table.shape[1]] = table.astype(bf16)
+    table = [t.astype(f32) for t in table]
+    rest = jnp.zeros((1, packed.shape[1] - 3 * table[0].shape[1]), f32)
+    table = [jnp.concatenate(table[3 * i : 3 * i + 3] + [rest], axis=1) for i in range(3)]
+    table.append(jnp.zeros((5, packed.shape[1]), f32))
+    packed[count:, :] = jnp.concatenate(table, axis=0).astype(bf16)
 
 
 def prepare(x, order, *obs):
@@ -228,7 +229,7 @@
         prepare_kernel,
         in_specs=[vmem] * (2 + len(obs)),
         out_specs=vmem,
-        out_shape=jax.ShapeDtypeStruct((count + 16, feats), bf16),
+        out_shape=jax.ShapeDtypeStruct((count + 8, feats), bf16),
         name="prepare",
     )(x, order, *obs)
 
@@ -330,7 +331,7 @@
 
 
 def weighted_places(table, count):
-    table = table[:, :, :count].astype(f32)
+    table = table[:, :3, : 3 * count].astype(f32).reshape(2, 9, count)
     grid = table[:, 0].astype(jnp.int32)
     domain = table[:, 1].astype(jnp.int32)
     channel = table[:, 2].astype(jnp.int32)
@@ -398,7 +399,7 @@
     )
     sent, outgoing = lax.optimization_barrier((sent, mine))
     theirs = crossed(outgoing)
-    middle = (count + 16) // 2
+    middle = (count + 8) // 2
     up, down = shifted(sent[:middle], 4), shifted(sent[middle:], -4)
 
     decoder = in_order(zh, mine[o_end:], theirs[o_end:], 0)

time: 151 us -> 148 us (0.980)
  waiting for transfers between devices: 43.7 us -> 34.4 us
  starting transfers between devices: 67.5 us -> 73.6 us
    ppermute x1, starting transfers between devices: 3.09 us -> 9.31 us  [between_chips(): return lax.ppermute(value, TILE, pairs + [(b, a) for a, b in pairs])]
    ppermute x4, waiting for transfers between devices: 21.8 us -> 16.4 us  [shifted(): lax.ppermute(value, ('zh', 'zl'), [(z, (z + by) % 16) for z in range(16)])]
    ppermute x1, waiting for transfers between devices: 9.62 us -> 5.87 us  [between_chips(): return lax.ppermute(value, TILE, pairs + [(b, a) for a, b in pairs])]
    unnamed x32 -> x31, local copies, waits for them, and re-layouts: 3.9 us -> 3.91 us
where the time goes in v6:
time: 148 us; the launch traced here: 147 us
  starting transfers between devices  73.6 us (50%)
  waiting for transfers between devices  34.4 us (23%)
  Pallas kernels  20.4 us (14%)
  local copies, waits for them, and re-layouts  10.4 us (7%)
  other arithmetic  5.81 us (4%)
  matrix products  2.49 us (2%)
    all_to_all x4, starting transfers between devices, exchanged(): lax.all_to_all(blocks, PLANE, split_axis=0, concat_axis=0, tiled=True)  29.3 us
    ppermute x4, starting transfers between devices, shifted(): lax.ppermute(value, ('zh', 'zl'), [(z, (z + by) % 16) for z in range(16)])  19.8 us
    ppermute x4, waiting for transfers between devices, shifted(): lax.ppermute(value, ('zh', 'zl'), [(z, (z + by) % 16) for z in range(16)])  16.4 us
    pallas_call x1, Pallas kernels, front_latents(): pl.pallas_call(front_kernel, in_specs=[pl.BlockSpec(memory_space=pltpu.SM...  11.4 us
    ppermute x1, starting transfers between devices, crossed(): return lax.ppermute(value, ('zh', 'zl'), pairs)  9.45 us
    ppermute x1, starting transfers between devices, between_chips(): return lax.ppermute(value, TILE, pairs + [(b, a) for a, b in pairs])  9.31 us
    all_to_all x4, waiting for transfers between devices, exchanged(): lax.all_to_all(blocks, PLANE, split_axis=0, concat_axis=0, tiled=True)  6.83 us
    ppermute x1, waiting for transfers between devices, between_chips(): return lax.ppermute(value, TILE, pairs + [(b, a) for a, b in pairs])  5.87 us
  transfers between devices with their start and end apart: 13, of which 7 were waited for; matrix products, arithmetic and copies ran while one was open for 8% of the time, Pallas kernels for 1%

profile of v6, /device:TPU:8, one launch (start us, length us, event | category | flops | bytes accessed | tf_op | source)
XLA Modules:
  0.0 147.5 jit_solution(13817231146403683708)
XLA Ops:
  0.0 1.0 fusion.9
  1.0 1.6 %broadcast_in_dim.7 = bf16[16,176,384]{2,1,0:T(8,128)(2,1)} broadcast(bf16[176,384]{1,0:T(8,128)(2,1)S(1)} %slice_select_fusion), dimensions={1,2} | broadcast | bytes 2297856 | tf_op jit(solution)/shard_map/broadcast_in_dim | solution.py:49
  2.6 9.5 %all-to-all-start = ((bf16[16,176,384]{2,1,0:T(8,128)(2,1)}), bf16[16,176,384]{2,1,0:T(8,128)(2,1)S(1)}, u32[]{:S(2)}, u32[]{:S(2)}) async-start(bf16[16,176,384]{2,1,0:T(8,128)(2,1)} %broadcast_in_dim.7), calls=%async_computation | async-start | bytes 4325376 | tf_op jit(solution)/shard_map/all_to_all | solution.py:53
  12.1 2.0 %prepare.1 = bf16[136,1120]{1,0:T(8,128)(2,1)} custom-call(bf16[128,1120]{1,0:T(8,128)(2,1)} %bitcast.53, bf16[128,128]{1,0:T(8,128)(2,1)} %constant.43.clone.order, s32[1,256]{1,0:T(1,128)} %bitcast.59, s32[1,256]{1,0:T(1,128)} %bitcast.60, s32[1,256]{1,0:T(1,128)} %bitcast.61, f32[1,256]{1,0:T(1,128)} %bitcast.62, f32[1,256]{1,0:T(1,128)} %bitcast.63), custom_call_target="tpu_custom_call" | custom-call | tf_op jit(solution)/shard_map/prepare/pallas_call | solution.py:228
  14.0 9.5 %collective-permute-start.2 = (bf16[176,384]{1,0:T(8,128)(2,1)S(1)}, bf16[176,384]{1,0:T(8,128)(2,1)S(1)}, u32[]{:S(2)}, u32[]{:S(2)}) collective-permute-start(bf16[176,384]{1,0:T(8,128)(2,1)S(1)} %slice_select_fusion), channel_id=1, source_target_pairs={{0,30},{2,28},{4,26},{6,24},{8,22},{10,20},{12,18},{14,16},{16,14}... | collective-permute-start | bytes 405512 | tf_op jit(solution)/shard_map/ppermute | solution.py:40
  23.5 1.0 fusion.25
  24.5 8.2 %collective-permute-start = (bf16[68,1120]{1,0:T(8,128)(2,1)S(1)}, bf16[68,1120]{1,0:T(8,128)(2,1)S(1)}, u32[]{:S(2)}, u32[]{:S(2)}) collective-permute-start(bf16[68,1120]{1,0:T(8,128)(2,1)S(1)} %get-tuple-element.44), channel_id=1, source_target_pairs={{0,8},{2,10},{4,12},{6,14},{8,16},{10,18},{12,20},{14,22},{16,24},... | collective-permute-start | bytes 456968 | tf_op jit(solution)/shard_map/ppermute | solution.py:35
  32.7 1.9 %collective-permute-start.1 = (bf16[68,1120]{1,0:T(8,128)(2,1)S(1)}, bf16[68,1120]{1,0:T(8,128)(2,1)S(1)}, u32[]{:S(2)}, u32[]{:S(2)}) collective-permute-start(bf16[68,1120]{1,0:T(8,128)(2,1)S(1)} %get-tuple-element.43), channel_id=1, source_target_pairs={{0,24},{2,26},{4,28},{6,30},{8,0},{10,2},{12,4},{14,6},{16,8},{18,... | collective-permute-start | bytes 456968 | tf_op jit(solution)/shard_map/ppermute | solution.py:35
  34.6 0.1 reshape.92
  34.7 0.1 reshape.93
  34.8 5.3 %collective-permute-done.2 = bf16[176,384]{1,0:T(8,128)(2,1)S(1)} collective-permute-done((bf16[176,384]{1,0:T(8,128)(2,1)S(1)}, bf16[176,384]{1,0:T(8,128)(2,1)S(1)}, u32[]{:S(2)}, u32[]{:S(2)}) %collective-permute-start.2) | collective-permute-done | bytes 135200 | tf_op jit(solution)/shard_map/ppermute | solution.py:40
  40.2 0.1 convolution_convert_fusion.1
  40.3 1.7 %broadcast_in_dim.6 = bf16[16,192,384]{2,1,0:T(8,128)(2,1)} broadcast(bf16[192,384]{1,0:T(8,128)(2,1)S(1)} %pad_maximum_fusion.5), dimensions={1,2} | broadcast | bytes 2506752 | tf_op jit(solution)/shard_map/broadcast_in_dim | solution.py:49
  42.1 1.4 copy-done
  43.4 7.2 %all-to-all-start.1 = ((bf16[16,192,384]{2,1,0:T(8,128)(2,1)}), bf16[16,192,384]{2,1,0:T(8,128)(2,1)S(1)}, u32[]{:S(2)}, u32[]{:S(2)}) async-start(bf16[16,192,384]{2,1,0:T(8,128)(2,1)} %broadcast_in_dim.6), calls=%async_computation.1 | async-start | bytes 4718592 | tf_op jit(solution)/shard_map/all_to_all | solution.py:53
  50.7 2.0 %collective-permute-done.1 = bf16[68,1120]{1,0:T(8,128)(2,1)S(1)} collective-permute-done((bf16[68,1120]{1,0:T(8,128)(2,1)S(1)}, bf16[68,1120]{1,0:T(8,128)(2,1)S(1)}, u32[]{:S(2)}, u32[]{:S(2)}) %collective-permute-start.1) | collective-permute-done | bytes 152352 | tf_op jit(solution)/shard_map/ppermute | solution.py:35
  52.7 1.9 %collective-permute-start.7 = (bf16[16,176,384]{2,1,0:T(8,128)(2,1)}, bf16[16,176,384]{2,1,0:T(8,128)(2,1)S(1)}, u32[]{:S(2)}, u32[]{:S(2)}) collective-permute-start(bf16[16,176,384]{2,1,0:T(8,128)(2,1)} %copy-done), channel_id=1, source_target_pairs={{0,1},{1,0},{2,3},{3,2},{4,5},{5,4},{6,7},{7,6},{8,9},{9,8},{10,11... | collective-permute-start | bytes 6488072 | tf_op jit(solution)/shard_map/ppermute | solution.py:31
  54.6 6.4 %collective-permute-start.4 = (bf16[68,1120]{1,0:T(8,128)(2,1)S(1)}, bf16[68,1120]{1,0:T(8,128)(2,1)S(1)}, u32[]{:S(2)}, u32[]{:S(2)}) collective-permute-start(bf16[68,1120]{1,0:T(8,128)(2,1)S(1)} %collective-permute-done.1), channel_id=1, source_target_pairs={{0,24},{2,26},{4,28},{6,30},{8,0},{10,2},{12,4},{14,6},{16,8},{18,... | collective-permute-start | bytes 456968 | tf_op jit(solution)/shard_map/ppermute | solution.py:35
  61.0 3.3 %collective-permute-start.3 = (bf16[68,1120]{1,0:T(8,128)(2,1)S(1)}, bf16[68,1120]{1,0:T(8,128)(2,1)S(1)}, u32[]{:S(2)}, u32[]{:S(2)}) collective-permute-start(bf16[68,1120]{1,0:T(8,128)(2,1)S(1)} %collective-permute-done), channel_id=1, source_target_pairs={{0,8},{2,10},{4,12},{6,14},{8,16},{10,18},{12,20},{14,22},{16,24},... | collective-permute-start | bytes 456968 | tf_op jit(solution)/shard_map/ppermute | solution.py:35
  64.4 10.7 %collective-permute-done.4 = bf16[68,1120]{1,0:T(8,128)(2,1)S(1)} collective-permute-done((bf16[68,1120]{1,0:T(8,128)(2,1)S(1)}, bf16[68,1120]{1,0:T(8,128)(2,1)S(1)}, u32[]{:S(2)}, u32[]{:S(2)}) %collective-permute-start.4) | collective-permute-done | bytes 152352 | tf_op jit(solution)/shard_map/ppermute | solution.py:35
  75.0 3.7 %collective-permute-done.3 = bf16[68,1120]{1,0:T(8,128)(2,1)S(1)} collective-permute-done((bf16[68,1120]{1,0:T(8,128)(2,1)S(1)}, bf16[68,1120]{1,0:T(8,128)(2,1)S(1)}, u32[]{:S(2)}, u32[]{:S(2)}) %collective-permute-start.3) | collective-permute-done | bytes 152352 | tf_op jit(solution)/shard_map/ppermute | solution.py:35
  78.7 1.4 copy-done.2
  80.1 1.9 %collective-permute-start.8 = (bf16[16,192,384]{2,1,0:T(8,128)(2,1)S(1)}, bf16[16,192,384]{2,1,0:T(8,128)(2,1)}, u32[]{:S(2)}, u32[]{:S(2)}) collective-permute-start(bf16[16,192,384]{2,1,0:T(8,128)(2,1)S(1)} %all-to-all-done.1.other_m), channel_id=1, source_target_pairs={{0,1},{1,0},{2,3},{3,2},{4,5},{5,4},{6,7},{7,6},{8,9},{9,8},{10,11... | collective-permute-start | bytes 7077896 | tf_op jit(solution)/shard_map/ppermute | solution.py:31
  82.4 0.1 broadcast_select_fusion.3
  82.5 9.3 %collective-permute-start.5 = (bf16[2,64,1120]{2,1,0:T(8,128)(2,1)S(1)}, bf16[2,64,1120]{2,1,0:T(8,128)(2,1)S(1)}, u32[]{:S(2)}, u32[]{:S(2)}) collective-permute-start(bf16[2,64,1120]{2,1,0:T(8,128)(2,1)S(1)} %get-tuple-element.39), channel_id=1, source_target_pairs={{0,15},{2,1},{4,3},{6,5},{8,7},{10,9},{12,11},{14,13},{15,0},{1,2}... | collective-permute-start | bytes 860168 | tf_op jit(solution)/shard_map/ppermute | solution.py:45
  91.8 1.9 %collective-permute-start.6 = (bf16[2,64,1120]{2,1,0:T(8,128)(2,1)S(1)}, bf16[2,64,1120]{2,1,0:T(8,128)(2,1)S(1)}, u32[]{:S(2)}, u32[]{:S(2)}) collective-permute-start(bf16[2,64,1120]{2,1,0:T(8,128)(2,1)S(1)} %get-tuple-element.40), channel_id=1, source_target_pairs={{0,1},{1,0},{2,3},{3,2},{4,5},{5,4},{6,7},{7,6},{8,9},{9,8},{10,11... | collective-permute-start | bytes 860168 | tf_op jit(solution)/shard_map/ppermute | solution.py:31
  93.8 5.9 %collective-permute-done.5 = bf16[2,64,1120]{2,1,0:T(8,128)(2,1)S(1)} collective-permute-done((bf16[2,64,1120]{2,1,0:T(8,128)(2,1)S(1)}, bf16[2,64,1120]{2,1,0:T(8,128)(2,1)S(1)}, u32[]{:S(2)}, u32[]{:S(2)}) %collective-permute-start.5) | collective-permute-done | bytes 286752 | tf_op jit(solution)/shard_map/ppermute | solution.py:45
  99.8 0.1 pad_maximum_fusion
  99.9 1.9 %convolution_convert_fusion = bf16[512,1280]{1,0:T(8,128)(2,1)S(1)} fusion(bf16[512,1120]{1,0:T(8,128)(2,1)S(1)} %bitcast.52, bf16[1120,1280]{1,0:T(8,128)(2,1)S(1)} %copy-done.13), kind=kOutput, calls=%fused_computation | convolution fusion | flops 1468661760 | bytes 5324800 | tf_op jit(solution)/shard_map/dot_general | solution.py:57
  101.8 0.3 copy-done.3
  102.1 11.4 %front.1 = bf16[256,768]{1,0:T(8,128)(2,1)} custom-call(s32[2]{0:T(128)S(1)} %pad_add_fusion.flags, bf16[2,256,1280]{2,1,0:T(8,128)(2,1)S(1)} %bitcast.45, bf16[16,176,384]{2,1,0:T(8,128)(2,1)S(1)} %copy-done.1, bf16[16,192,384]{2,1,0:T(8,128)(2,1)S(1)} %all-to-all-done.1.other_m, bf16[16,176,384]{2,1,0:T(8,128)(2,1)S(1)} %copy-done.3, ...), custom_call_target="tpu_custom_call" | custom-call | tf_op jit(solution)/shard_map/front/pallas_call | solution.py:201
  113.6 7.3 %all-to-all-start.2 = ((bf16[16,16,768]{2,1,0:T(8,128)(2,1)}), bf16[16,16,768]{2,1,0:T(8,128)(2,1)S(1)}, u32[]{:S(2)}, u32[]{:S(2)}) async-start(bf16[16,16,768]{2,1,0:T(8,128)(2,1)} %bitcast.15), calls=%async_computation.2 | async-start | bytes 786432 | tf_op jit(solution)/shard_map/all_to_all | solution.py:53
  121.0 0.5 fusion.obs
  121.5 1.0 slice.107
  122.5 2.8 %select_bitcast_fusion.1 = (bf16[16,1,35,384]{3,2,0,1:T(8,128)(2,1)}, bf16[16,1,35,384]{3,2,0,1:T(8,128)(2,1)}, bf16[16,1,35,384]{3,2,0,1:T(8,128)(2,1)}, bf16[16,1,35,384]{3,2,0,1:T(8,128)(2,1)}) fusion(pred[]{:T(512)S(6)} %eq.19, bf16[16,192,384]{2,1,0:T(8,128)(2,1)} %collective-permute-done.8.other_p, bf16[16,176,384]{2,1,0:T(8,128)(2,1)} %copy-done.2, ...), kind=kLoop, calls=%fused_computation.20 | loop fusion | flops 860160 | bytes 3440641 | tf_op jit(solution)/shard_map/jit(_where)/select_n | solution.py:71
  125.3 3.2 %all-to-all-done.2 = bf16[16,16,768]{2,1,0:T(8,128)(2,1)S(1)} async-done(((bf16[16,16,768]{2,1,0:T(8,128)(2,1)}), bf16[16,16,768]{2,1,0:T(8,128)(2,1)S(1)}, u32[]{:S(2)}, u32[]{:S(2)}) %all-to-all-start.2) | async-done | bytes 393248 | tf_op jit(solution)/shard_map/all_to_all | solution.py:53
  128.5 5.0 %analysis.1 = bf16[128,768]{1,0:T(8,128)(2,1)} custom-call(s32[2]{0:T(128)S(1)} %pad_add_fusion.flags, bf16[256,768]{1,0:T(8,128)(2,1)S(1)} %bitcast.44, bf16[256,256]{1,0:T(8,128)(2,1)S(1)} %copy-done.6, bf16[128,128]{1,0:T(8,128)(2,1)S(1)} %copy-done.7, f32[2,4,512]{2,1,0:T(4,128)S(1)} %fusion.obs, bf16[256,384]{1,0:T(8,128)(2,1)S(1)} %bitcast.47, ...), custom_call_target="tpu_custom_call" | custom-call | tf_op jit(solution)/shard_map/analysis/pallas_call | solution.py:306
  133.4 5.3 %all-to-all-start.3 = ((bf16[16,8,768]{2,1,0:T(8,128)(2,1)}), bf16[16,8,768]{2,1,0:T(8,128)(2,1)S(1)}, u32[]{:S(2)}, u32[]{:S(2)}) async-start(bf16[16,8,768]{2,1,0:T(8,128)(2,1)} %bitcast.19), calls=%async_computation.3 | async-start | bytes 393216 | tf_op jit(solution)/shard_map/all_to_all | solution.py:53
  138.7 1.3 pad_maximum_fusion.1
  140.1 0.1 copy.21
  140.2 0.3 reshape.104.d_mine
  140.5 0.6 copy-done.9
  141.1 0.1 copy-done.10
  141.2 0.1 pad_maximum_fusion.2
  141.4 0.1 copy.22
  141.5 0.3 reshape.105.d_part
  141.8 3.6 %all-to-all-done.3 = bf16[16,8,768]{2,1,0:T(8,128)(2,1)S(1)} async-done(((bf16[16,8,768]{2,1,0:T(8,128)(2,1)}), bf16[16,8,768]{2,1,0:T(8,128)(2,1)S(1)}, u32[]{:S(2)}, u32[]{:S(2)}) %all-to-all-start.3) | async-done | bytes 196640 | tf_op jit(solution)/shard_map/all_to_all | solution.py:53
  145.4 2.1 %decode.1 = bf16[128,1120]{1,0:T(8,128)(2,1)} custom-call(s32[2]{0:T(128)S(1)} %pad_add_fusion.flags, bf16[128,768]{1,0:T(8,128)(2,1)S(1)} %bitcast.46, bf16[128,128]{1,0:T(8,128)(2,1)S(1)} %copy-done.5, bf16[1120,384]{1,0:T(8,128)(2,1)S(1)} %reshape.104.d_mine, bf16[1120,384]{1,0:T(8,128)(2,1)S(1)} %reshape.105.d_part), custom_call_target="tpu_custom_call" | custom-call | tf_op jit(solution)/shard_map/decode/pallas_call | solution.py:323
  (50 shorter events, 0.7 us)
Async XLA Ops:
  2.6 32.0 %copy-start.11 = (bf16[16,70]{1,0:T(8,128)(2,1)S(1)}, bf16[16,70]{1,0:T(8,128)(2,1)}, u32[]{:S(2)}) copy-start(bf16[16,70]{1,0:T(8,128)(2,1)} %param.24) | copy-start | bytes 6724
  2.6 39.5 %all-to-all-start = ((bf16[16,176,384]{2,1,0:T(8,128)(2,1)}), bf16[16,176,384]{2,1,0:T(8,128)(2,1)S(1)}, u32[]{:S(2)}, u32[]{:S(2)}) async-start(bf16[16,176,384]{2,1,0:T(8,128)(2,1)} %broadcast_in_dim.7), calls=%async_computation | async-start | bytes 4325376 | tf_op jit(solution)/shard_map/all_to_all | solution.py:53
  14.0 26.1 %collective-permute-start.2 = (bf16[176,384]{1,0:T(8,128)(2,1)S(1)}, bf16[176,384]{1,0:T(8,128)(2,1)S(1)}, u32[]{:S(2)}, u32[]{:S(2)}) collective-permute-start(bf16[176,384]{1,0:T(8,128)(2,1)S(1)} %slice_select_fusion), channel_id=1, source_target_pairs={{0,30},{2,28},{4,26},{6,24},{8,22},{10,20},{12,18},{14,16},{16,14}... | collective-permute-start | bytes 405512 | tf_op jit(solution)/shard_map/ppermute | solution.py:40
  24.5 26.2 %collective-permute-start = (bf16[68,1120]{1,0:T(8,128)(2,1)S(1)}, bf16[68,1120]{1,0:T(8,128)(2,1)S(1)}, u32[]{:S(2)}, u32[]{:S(2)}) collective-permute-start(bf16[68,1120]{1,0:T(8,128)(2,1)S(1)} %get-tuple-element.44), channel_id=1, source_target_pairs={{0,8},{2,10},{4,12},{6,14},{8,16},{10,18},{12,20},{14,22},{16,24},... | collective-permute-start | bytes 456968 | tf_op jit(solution)/shard_map/ppermute | solution.py:35
  32.7 20.0 %collective-permute-start.1 = (bf16[68,1120]{1,0:T(8,128)(2,1)S(1)}, bf16[68,1120]{1,0:T(8,128)(2,1)S(1)}, u32[]{:S(2)}, u32[]{:S(2)}) collective-permute-start(bf16[68,1120]{1,0:T(8,128)(2,1)S(1)} %get-tuple-element.43), channel_id=1, source_target_pairs={{0,24},{2,26},{4,28},{6,30},{8,0},{10,2},{12,4},{14,6},{16,8},{18,... | collective-permute-start | bytes 456968 | tf_op jit(solution)/shard_map/ppermute | solution.py:35
  42.1 40.0 %copy-start.12 = (f32[12]{0:T(128)S(1)}, f32[12]{0:T(128)}, u32[]{:S(2)}) copy-start(f32[12]{0:T(128)} %param.23) | copy-start | bytes 148
  42.1 40.3 %copy-start.8 = (bf16[136,1120]{1,0:T(8,128)(2,1)S(1)}, bf16[136,1120]{1,0:T(8,128)(2,1)}, u32[]{:S(2)}) copy-start(bf16[136,1120]{1,0:T(8,128)(2,1)} %prepare.1) | copy-start | bytes 913924
  42.1 1.4 copy-start
  43.4 36.7 %all-to-all-start.1 = ((bf16[16,192,384]{2,1,0:T(8,128)(2,1)}), bf16[16,192,384]{2,1,0:T(8,128)(2,1)S(1)}, u32[]{:S(2)}, u32[]{:S(2)}) async-start(bf16[16,192,384]{2,1,0:T(8,128)(2,1)} %broadcast_in_dim.6), calls=%async_computation.1 | async-start | bytes 4718592 | tf_op jit(solution)/shard_map/all_to_all | solution.py:53
  52.7 26.1 %collective-permute-start.7 = (bf16[16,176,384]{2,1,0:T(8,128)(2,1)}, bf16[16,176,384]{2,1,0:T(8,128)(2,1)S(1)}, u32[]{:S(2)}, u32[]{:S(2)}) collective-permute-start(bf16[16,176,384]{2,1,0:T(8,128)(2,1)} %copy-done), channel_id=1, source_target_pairs={{0,1},{1,0},{2,3},{3,2},{4,5},{5,4},{6,7},{7,6},{8,9},{9,8},{10,11... | collective-permute-start | bytes 6488072 | tf_op jit(solution)/shard_map/ppermute | solution.py:31
  54.6 20.5 %collective-permute-start.4 = (bf16[68,1120]{1,0:T(8,128)(2,1)S(1)}, bf16[68,1120]{1,0:T(8,128)(2,1)S(1)}, u32[]{:S(2)}, u32[]{:S(2)}) collective-permute-start(bf16[68,1120]{1,0:T(8,128)(2,1)S(1)} %collective-permute-done.1), channel_id=1, source_target_pairs={{0,24},{2,26},{4,28},{6,30},{8,0},{10,2},{12,4},{14,6},{16,8},{18,... | collective-permute-start | bytes 456968 | tf_op jit(solution)/shard_map/ppermute | solution.py:35
  61.0 17.7 %collective-permute-start.3 = (bf16[68,1120]{1,0:T(8,128)(2,1)S(1)}, bf16[68,1120]{1,0:T(8,128)(2,1)S(1)}, u32[]{:S(2)}, u32[]{:S(2)}) collective-permute-start(bf16[68,1120]{1,0:T(8,128)(2,1)S(1)} %collective-permute-done), channel_id=1, source_target_pairs={{0,8},{2,10},{4,12},{6,14},{8,16},{10,18},{12,20},{14,22},{16,24},... | collective-permute-start | bytes 456968 | tf_op jit(solution)/shard_map/ppermute | solution.py:35
  78.7 1.4 copy-start.2
  80.1 21.7 %collective-permute-start.8 = (bf16[16,192,384]{2,1,0:T(8,128)(2,1)S(1)}, bf16[16,192,384]{2,1,0:T(8,128)(2,1)}, u32[]{:S(2)}, u32[]{:S(2)}) collective-permute-start(bf16[16,192,384]{2,1,0:T(8,128)(2,1)S(1)} %all-to-all-done.1.other_m), channel_id=1, source_target_pairs={{0,1},{1,0},{2,3},{3,2},{4,5},{5,4},{6,7},{7,6},{8,9},{9,8},{10,11... | collective-permute-start | bytes 7077896 | tf_op jit(solution)/shard_map/ppermute | solution.py:31
  82.5 17.2 %collective-permute-start.5 = (bf16[2,64,1120]{2,1,0:T(8,128)(2,1)S(1)}, bf16[2,64,1120]{2,1,0:T(8,128)(2,1)S(1)}, u32[]{:S(2)}, u32[]{:S(2)}) collective-permute-start(bf16[2,64,1120]{2,1,0:T(8,128)(2,1)S(1)} %get-tuple-element.39), channel_id=1, source_target_pairs={{0,15},{2,1},{4,3},{6,5},{8,7},{10,9},{12,11},{14,13},{15,0},{1,2}... | collective-permute-start | bytes 860168 | tf_op jit(solution)/shard_map/ppermute | solution.py:45
  91.8 7.9 %collective-permute-start.6 = (bf16[2,64,1120]{2,1,0:T(8,128)(2,1)S(1)}, bf16[2,64,1120]{2,1,0:T(8,128)(2,1)S(1)}, u32[]{:S(2)}, u32[]{:S(2)}) collective-permute-start(bf16[2,64,1120]{2,1,0:T(8,128)(2,1)S(1)} %get-tuple-element.40), channel_id=1, source_target_pairs={{0,1},{1,0},{2,3},{3,2},{4,5},{5,4},{6,7},{7,6},{8,9},{9,8},{10,11... | collective-permute-start | bytes 860168 | tf_op jit(solution)/shard_map/ppermute | solution.py:31
  93.7 6.1 %copy-start.13 = (bf16[1120,1280]{1,0:T(8,128)(2,1)S(1)}, bf16[1120,1280]{1,0:T(8,128)(2,1)}, u32[]{:S(2)}) copy-start(bf16[1120,1280]{1,0:T(8,128)(2,1)} %constant.44.clone) | copy-start | bytes 8601604
  99.9 1.9 %copy-start.1 = (bf16[16,176,384]{2,1,0:T(8,128)(2,1)S(1)}, bf16[16,176,384]{2,1,0:T(8,128)(2,1)}, u32[]{:S(2)}) copy-start(bf16[16,176,384]{2,1,0:T(8,128)(2,1)} %copy-done) | copy-start | bytes 6488068
  99.9 2.3 %copy-start.3 = (bf16[16,176,384]{2,1,0:T(8,128)(2,1)S(1)}, bf16[16,176,384]{2,1,0:T(8,128)(2,1)}, u32[]{:S(2)}) copy-start(bf16[16,176,384]{2,1,0:T(8,128)(2,1)} %copy-done.2) | copy-start | bytes 6488068
  99.9 2.2 %copy-start.4 = (bf16[256,256]{1,0:T(8,128)(2,1)S(1)}, bf16[256,256]{1,0:T(8,128)(2,1)}, u32[]{:S(2)}) copy-start(bf16[256,256]{1,0:T(8,128)(2,1)} %constant.45.clone.order) | copy-start | bytes 393220
  113.6 14.8 %all-to-all-start.2 = ((bf16[16,16,768]{2,1,0:T(8,128)(2,1)}), bf16[16,16,768]{2,1,0:T(8,128)(2,1)S(1)}, u32[]{:S(2)}, u32[]{:S(2)}) async-start(bf16[16,16,768]{2,1,0:T(8,128)(2,1)} %bitcast.15), calls=%async_computation.2 | async-start | bytes 786432 | tf_op jit(solution)/shard_map/all_to_all | solution.py:53
  121.5 7.0 %copy-start.6 = (bf16[256,256]{1,0:T(8,128)(2,1)S(1)}, bf16[256,256]{1,0:T(8,128)(2,1)}, u32[]{:S(2)}) copy-start(bf16[256,256]{1,0:T(8,128)(2,1)} %constant.46.clone.order) | copy-start | bytes 393220
  121.5 7.0 %copy-start.7 = (bf16[128,128]{1,0:T(8,128)(2,1)S(1)}, bf16[128,128]{1,0:T(8,128)(2,1)}, u32[]{:S(2)}) copy-start(bf16[128,128]{1,0:T(8,128)(2,1)} %constant.47.clone.back_order) | copy-start | bytes 98308
  133.4 12.0 %all-to-all-start.3 = ((bf16[16,8,768]{2,1,0:T(8,128)(2,1)}), bf16[16,8,768]{2,1,0:T(8,128)(2,1)S(1)}, u32[]{:S(2)}, u32[]{:S(2)}) async-start(bf16[16,8,768]{2,1,0:T(8,128)(2,1)} %bitcast.19), calls=%async_computation.3 | async-start | bytes 393216 | tf_op jit(solution)/shard_map/all_to_all | solution.py:53
  140.0 1.0 copy-start.9
  140.1 1.2 copy-start.10
  141.4 4.0 %copy-start.5 = (bf16[128,128]{1,0:T(8,128)(2,1)S(1)}, bf16[128,128]{1,0:T(8,128)(2,1)}, u32[]{:S(2)}) copy-start(bf16[128,128]{1,0:T(8,128)(2,1)} %constant.43.clone.order) | copy-start | bytes 98308

commit v7 on v6

--- a/solution.py
+++ b/solution.py
@@ -411,7 +411,8 @@
         (copies_of(jnp.concatenate([theirs, readers], axis=0)), own_all)
     )
     up, down, own_sent = lax.optimization_barrier((up, down, own_all))
-    partner = jnp.concatenate([shifted(up, 4), shifted(down, -4)], axis=0)
+    up = shifted(up, 4)
+    partner = jnp.concatenate([up, shifted(down, -4)], axis=0)
     other_main = exchanged(copies)
     inside = np.arange(BLOCK)[None, None, :]
     place = np.arange(16)[None, :, None] * 2 + np.arange(2)[:, None, None]
@@ -428,7 +429,7 @@
     states = states.reshape(2, 2 * count, 2 * SIDE)
 
     own_all_p = swapped(own_sent, "core")
-    other_main, own_all_p, _ = lax.optimization_barrier((other_main, own_all_p, partner))
+    other_main, own_all_p, _ = lax.optimization_barrier((other_main, own_all_p, up))
     other_main_p = swapped(other_main, "core")
     scale = jnp.repeat(cosine_logit_scale, HEAD)[None, :]
     weights = (own_all, other_main, own_all_p, other_main_p)

time: 148 us -> 148 us (level)
  starting transfers between devices: 73.6 us -> 71.1 us
  waiting for transfers between devices: 34.4 us -> 36.5 us
    all_to_all x4, waiting for transfers between devices: 6.83 us -> 14.7 us  [exchanged(): lax.all_to_all(blocks, PLANE, split_axis=0, concat_axis=0, tiled=True)]
    ppermute x4, waiting for transfers between devices: 16.4 us -> 10.4 us  [shifted(): lax.ppermute(value, ('zh', 'zl'), [(z, (z + by) % 16) for z in range(16)])]
    ppermute x1, starting transfers between devices: 9.31 us -> 6.73 us  [between_chips(): return lax.ppermute(value, TILE, pairs + [(b, a) for a, b in pairs])]
  transfers between devices with their start and end apart: 13 -> 13, of which waited for: 7 -> 8; matrix products, arithmetic and copies ran while one was open for 8% -> 8% of each run, Pallas kernels for 1% -> 1%
where the time goes in v7:
time: 148 us; the launch traced here: 147 us
  starting transfers between devices  71.1 us (48%)
  waiting for transfers between devices  36.5 us (25%)
  Pallas kernels  20.4 us (14%)
  local copies, waits for them, and re-layouts  10.4 us (7%)
  other arithmetic  5.81 us (4%)
  matrix products  2.49 us (2%)
    all_to_all x4, starting transfers between devices, exchanged(): lax.all_to_all(blocks, PLANE, split_axis=0, concat_axis=0, tiled=True)  29.3 us
    ppermute x4, starting transfers between devices, shifted(): lax.ppermute(value, ('zh', 'zl'), [(z, (z + by) % 16) for z in range(16)])  19.8 us
    all_to_all x4, waiting for transfers between devices, exchanged(): lax.all_to_all(blocks, PLANE, split_axis=0, concat_axis=0, tiled=True)  14.7 us
    pallas_call x1, Pallas kernels, front_latents(): pl.pallas_call(front_kernel, in_specs=[pl.BlockSpec(memory_space=pltpu.SM...  11.4 us
    ppermute x4, waiting for transfers between devices, shifted(): lax.ppermute(value, ('zh', 'zl'), [(z, (z + by) % 16) for z in range(16)])  10.4 us
    ppermute x1, starting transfers between devices, crossed(): return lax.ppermute(value, ('zh', 'zl'), pairs)  9.45 us
    ppermute x1, starting transfers between devices, between_chips(): return lax.ppermute(value, TILE, pairs + [(b, a) for a, b in pairs])  6.73 us
    ppermute x1, waiting for transfers between devices, between_chips(): return lax.ppermute(value, TILE, pairs + [(b, a) for a, b in pairs])  5.98 us
  transfers between devices with their start and end apart: 13, of which 8 were waited for; matrix products, arithmetic and copies ran while one was open for 8% of the time, Pallas kernels for 1%

profile of v7, /device:TPU:8, one launch (start us, length us, event | category | flops | bytes accessed | tf_op | source)
XLA Modules:
  0.0 147.0 jit_solution(7452117497610184758)
XLA Ops:
  0.0 1.0 fusion.9
  1.0 1.6 %broadcast_in_dim.7 = bf16[16,176,384]{2,1,0:T(8,128)(2,1)} broadcast(bf16[176,384]{1,0:T(8,128)(2,1)S(1)} %slice_select_fusion), dimensions={1,2} | broadcast | bytes 2297856 | tf_op jit(solution)/shard_map/broadcast_in_dim | solution.py:49
  2.6 9.5 %all-to-all-start = ((bf16[16,176,384]{2,1,0:T(8,128)(2,1)}), bf16[16,176,384]{2,1,0:T(8,128)(2,1)S(1)}, u32[]{:S(2)}, u32[]{:S(2)}) async-start(bf16[16,176,384]{2,1,0:T(8,128)(2,1)} %broadcast_in_dim.7), calls=%async_computation | async-start | bytes 4325376 | tf_op jit(solution)/shard_map/all_to_all | solution.py:53
  12.1 2.0 %prepare.1 = bf16[136,1120]{1,0:T(8,128)(2,1)} custom-call(bf16[128,1120]{1,0:T(8,128)(2,1)} %bitcast.53, bf16[128,128]{1,0:T(8,128)(2,1)} %constant.43.clone.order, s32[1,256]{1,0:T(1,128)} %bitcast.59, s32[1,256]{1,0:T(1,128)} %bitcast.60, s32[1,256]{1,0:T(1,128)} %bitcast.61, f32[1,256]{1,0:T(1,128)} %bitcast.62, f32[1,256]{1,0:T(1,128)} %bitcast.63), custom_call_target="tpu_custom_call" | custom-call | tf_op jit(solution)/shard_map/prepare/pallas_call | solution.py:228
  14.0 9.5 %collective-permute-start.2 = (bf16[176,384]{1,0:T(8,128)(2,1)S(1)}, bf16[176,384]{1,0:T(8,128)(2,1)S(1)}, u32[]{:S(2)}, u32[]{:S(2)}) collective-permute-start(bf16[176,384]{1,0:T(8,128)(2,1)S(1)} %slice_select_fusion), channel_id=1, source_target_pairs={{0,30},{2,28},{4,26},{6,24},{8,22},{10,20},{12,18},{14,16},{16,14}... | collective-permute-start | bytes 405512 | tf_op jit(solution)/shard_map/ppermute | solution.py:40
  23.5 1.0 fusion.25
  24.5 8.2 %collective-permute-start = (bf16[68,1120]{1,0:T(8,128)(2,1)S(1)}, bf16[68,1120]{1,0:T(8,128)(2,1)S(1)}, u32[]{:S(2)}, u32[]{:S(2)}) collective-permute-start(bf16[68,1120]{1,0:T(8,128)(2,1)S(1)} %get-tuple-element.44), channel_id=1, source_target_pairs={{0,8},{2,10},{4,12},{6,14},{8,16},{10,18},{12,20},{14,22},{16,24},... | collective-permute-start | bytes 456968 | tf_op jit(solution)/shard_map/ppermute | solution.py:35
  32.7 1.9 %collective-permute-start.1 = (bf16[68,1120]{1,0:T(8,128)(2,1)S(1)}, bf16[68,1120]{1,0:T(8,128)(2,1)S(1)}, u32[]{:S(2)}, u32[]{:S(2)}) collective-permute-start(bf16[68,1120]{1,0:T(8,128)(2,1)S(1)} %get-tuple-element.43), channel_id=1, source_target_pairs={{0,24},{2,26},{4,28},{6,30},{8,0},{10,2},{12,4},{14,6},{16,8},{18,... | collective-permute-start | bytes 456968 | tf_op jit(solution)/shard_map/ppermute | solution.py:35
  34.7 0.1 reshape.93
  34.8 5.3 %collective-permute-done.2 = bf16[176,384]{1,0:T(8,128)(2,1)S(1)} collective-permute-done((bf16[176,384]{1,0:T(8,128)(2,1)S(1)}, bf16[176,384]{1,0:T(8,128)(2,1)S(1)}, u32[]{:S(2)}, u32[]{:S(2)}) %collective-permute-start.2) | collective-permute-done | bytes 135200 | tf_op jit(solution)/shard_map/ppermute | solution.py:40
  40.2 0.1 convolution_convert_fusion.1
  40.3 1.7 %broadcast_in_dim.6 = bf16[16,192,384]{2,1,0:T(8,128)(2,1)} broadcast(bf16[192,384]{1,0:T(8,128)(2,1)S(1)} %pad_maximum_fusion.4), dimensions={1,2} | broadcast | bytes 2506752 | tf_op jit(solution)/shard_map/broadcast_in_dim | solution.py:49
  42.1 1.4 copy-done
  43.4 7.2 %all-to-all-start.1 = ((bf16[16,192,384]{2,1,0:T(8,128)(2,1)}), bf16[16,192,384]{2,1,0:T(8,128)(2,1)S(1)}, u32[]{:S(2)}, u32[]{:S(2)}) async-start(bf16[16,192,384]{2,1,0:T(8,128)(2,1)} %broadcast_in_dim.6), calls=%async_computation.1 | async-start | bytes 4718592 | tf_op jit(solution)/shard_map/all_to_all | solution.py:53
  50.7 2.0 %collective-permute-done.1 = bf16[68,1120]{1,0:T(8,128)(2,1)S(1)} collective-permute-done((bf16[68,1120]{1,0:T(8,128)(2,1)S(1)}, bf16[68,1120]{1,0:T(8,128)(2,1)S(1)}, u32[]{:S(2)}, u32[]{:S(2)}) %collective-permute-start.1) | collective-permute-done | bytes 152352 | tf_op jit(solution)/shard_map/ppermute | solution.py:35
  52.7 1.9 %collective-permute-start.7 = (bf16[16,176,384]{2,1,0:T(8,128)(2,1)}, bf16[16,176,384]{2,1,0:T(8,128)(2,1)S(1)}, u32[]{:S(2)}, u32[]{:S(2)}) collective-permute-start(bf16[16,176,384]{2,1,0:T(8,128)(2,1)} %copy-done), channel_id=1, source_target_pairs={{0,1},{1,0},{2,3},{3,2},{4,5},{5,4},{6,7},{7,6},{8,9},{9,8},{10,11... | collective-permute-start | bytes 6488072 | tf_op jit(solution)/shard_map/ppermute | solution.py:31
  54.6 3.5 %collective-permute-start.3 = (bf16[68,1120]{1,0:T(8,128)(2,1)S(1)}, bf16[68,1120]{1,0:T(8,128)(2,1)S(1)}, u32[]{:S(2)}, u32[]{:S(2)}) collective-permute-start(bf16[68,1120]{1,0:T(8,128)(2,1)S(1)} %collective-permute-done), channel_id=1, source_target_pairs={{0,8},{2,10},{4,12},{6,14},{8,16},{10,18},{12,20},{14,22},{16,24},... | collective-permute-start | bytes 456968 | tf_op jit(solution)/shard_map/ppermute | solution.py:35
  58.1 6.2 %collective-permute-start.4 = (bf16[68,1120]{1,0:T(8,128)(2,1)S(1)}, bf16[68,1120]{1,0:T(8,128)(2,1)S(1)}, u32[]{:S(2)}, u32[]{:S(2)}) collective-permute-start(bf16[68,1120]{1,0:T(8,128)(2,1)S(1)} %collective-permute-done.1), channel_id=1, source_target_pairs={{0,24},{2,26},{4,28},{6,30},{8,0},{10,2},{12,4},{14,6},{16,8},{18,... | collective-permute-start | bytes 456968 | tf_op jit(solution)/shard_map/ppermute | solution.py:35
  64.4 5.0 %collective-permute-done.3 = bf16[68,1120]{1,0:T(8,128)(2,1)S(1)} collective-permute-done((bf16[68,1120]{1,0:T(8,128)(2,1)S(1)}, bf16[68,1120]{1,0:T(8,128)(2,1)S(1)}, u32[]{:S(2)}, u32[]{:S(2)}) %collective-permute-start.3) | collective-permute-done | bytes 152352 | tf_op jit(solution)/shard_map/ppermute | solution.py:35
  69.3 1.4 copy-done.2
  70.7 7.9 %all-to-all-done.1.other_m = bf16[16,192,384]{2,1,0:T(8,128)(2,1)S(1)} async-done(((bf16[16,192,384]{2,1,0:T(8,128)(2,1)}), bf16[16,192,384]{2,1,0:T(8,128)(2,1)S(1)}, u32[]{:S(2)}, u32[]{:S(2)}) %all-to-all-start.1) | async-done | bytes 2359328 | tf_op jit(solution)/shard_map/all_to_all | solution.py:53
  78.6 1.9 %collective-permute-start.8 = (bf16[16,192,384]{2,1,0:T(8,128)(2,1)S(1)}, bf16[16,192,384]{2,1,0:T(8,128)(2,1)}, u32[]{:S(2)}, u32[]{:S(2)}) collective-permute-start(bf16[16,192,384]{2,1,0:T(8,128)(2,1)S(1)} %all-to-all-done.1.other_m), channel_id=1, source_target_pairs={{0,1},{1,0},{2,3},{3,2},{4,5},{5,4},{6,7},{7,6},{8,9},{9,8},{10,11... | collective-permute-start | bytes 7077896 | tf_op jit(solution)/shard_map/ppermute | solution.py:31
  80.8 3.5 %collective-permute-done.4 = bf16[68,1120]{1,0:T(8,128)(2,1)S(1)} collective-permute-done((bf16[68,1120]{1,0:T(8,128)(2,1)S(1)}, bf16[68,1120]{1,0:T(8,128)(2,1)S(1)}, u32[]{:S(2)}, u32[]{:S(2)}) %collective-permute-start.4) | collective-permute-done | bytes 152352 | tf_op jit(solution)/shard_map/ppermute | solution.py:35
  84.3 0.1 broadcast_select_fusion.3
  84.4 6.7 %collective-permute-start.5 = (bf16[2,64,1120]{2,1,0:T(8,128)(2,1)S(1)}, bf16[2,64,1120]{2,1,0:T(8,128)(2,1)S(1)}, u32[]{:S(2)}, u32[]{:S(2)}) collective-permute-start(bf16[2,64,1120]{2,1,0:T(8,128)(2,1)S(1)} %get-tuple-element.39), channel_id=1, source_target_pairs={{0,15},{2,1},{4,3},{6,5},{8,7},{10,9},{12,11},{14,13},{15,0},{1,2}... | collective-permute-start | bytes 860168 | tf_op jit(solution)/shard_map/ppermute | solution.py:45
  91.2 1.9 %collective-permute-start.6 = (bf16[2,64,1120]{2,1,0:T(8,128)(2,1)S(1)}, bf16[2,64,1120]{2,1,0:T(8,128)(2,1)S(1)}, u32[]{:S(2)}, u32[]{:S(2)}) collective-permute-start(bf16[2,64,1120]{2,1,0:T(8,128)(2,1)S(1)} %get-tuple-element.40), channel_id=1, source_target_pairs={{0,1},{1,0},{2,3},{3,2},{4,5},{5,4},{6,7},{7,6},{8,9},{9,8},{10,11... | collective-permute-start | bytes 860168 | tf_op jit(solution)/shard_map/ppermute | solution.py:31
  93.2 6.0 %collective-permute-done.5 = bf16[2,64,1120]{2,1,0:T(8,128)(2,1)S(1)} collective-permute-done((bf16[2,64,1120]{2,1,0:T(8,128)(2,1)S(1)}, bf16[2,64,1120]{2,1,0:T(8,128)(2,1)S(1)}, u32[]{:S(2)}, u32[]{:S(2)}) %collective-permute-start.5) | collective-permute-done | bytes 286752 | tf_op jit(solution)/shard_map/ppermute | solution.py:45
  99.3 0.1 pad_maximum_fusion
  99.4 1.9 %convolution_convert_fusion = bf16[512,1280]{1,0:T(8,128)(2,1)S(1)} fusion(bf16[512,1120]{1,0:T(8,128)(2,1)S(1)} %bitcast.52, bf16[1120,1280]{1,0:T(8,128)(2,1)S(1)} %copy-done.13), kind=kOutput, calls=%fused_computation | convolution fusion | flops 1468661760 | bytes 5324800 | tf_op jit(solution)/shard_map/dot_general | solution.py:57
  101.3 0.3 copy-done.3
  101.6 11.4 %front.1 = bf16[256,768]{1,0:T(8,128)(2,1)} custom-call(s32[2]{0:T(128)S(1)} %pad_add_fusion.flags, bf16[2,256,1280]{2,1,0:T(8,128)(2,1)S(1)} %bitcast.45, bf16[16,176,384]{2,1,0:T(8,128)(2,1)S(1)} %copy-done.1, bf16[16,192,384]{2,1,0:T(8,128)(2,1)S(1)} %all-to-all-done.1.other_m, bf16[16,176,384]{2,1,0:T(8,128)(2,1)S(1)} %copy-done.3, ...), custom_call_target="tpu_custom_call" | custom-call | tf_op jit(solution)/shard_map/front/pallas_call | solution.py:201
  113.1 7.3 %all-to-all-start.2 = ((bf16[16,16,768]{2,1,0:T(8,128)(2,1)}), bf16[16,16,768]{2,1,0:T(8,128)(2,1)S(1)}, u32[]{:S(2)}, u32[]{:S(2)}) async-start(bf16[16,16,768]{2,1,0:T(8,128)(2,1)} %bitcast.15), calls=%async_computation.2 | async-start | bytes 786432 | tf_op jit(solution)/shard_map/all_to_all | solution.py:53
  120.5 0.5 fusion.obs
  121.0 1.0 slice.107
  122.0 2.8 %select_bitcast_fusion.1 = (bf16[16,1,35,384]{3,2,0,1:T(8,128)(2,1)}, bf16[16,1,35,384]{3,2,0,1:T(8,128)(2,1)}, bf16[16,1,35,384]{3,2,0,1:T(8,128)(2,1)}, bf16[16,1,35,384]{3,2,0,1:T(8,128)(2,1)}) fusion(pred[]{:T(512)S(6)} %eq.19, bf16[16,192,384]{2,1,0:T(8,128)(2,1)} %collective-permute-done.8.other_p, bf16[16,176,384]{2,1,0:T(8,128)(2,1)} %copy-done.2, ...), kind=kLoop, calls=%fused_computation.20 | loop fusion | flops 860160 | bytes 3440641 | tf_op jit(solution)/shard_map/jit(_where)/select_n | solution.py:71
  124.8 3.2 %all-to-all-done.2 = bf16[16,16,768]{2,1,0:T(8,128)(2,1)S(1)} async-done(((bf16[16,16,768]{2,1,0:T(8,128)(2,1)}), bf16[16,16,768]{2,1,0:T(8,128)(2,1)S(1)}, u32[]{:S(2)}, u32[]{:S(2)}) %all-to-all-start.2) | async-done | bytes 393248 | tf_op jit(solution)/shard_map/all_to_all | solution.py:53
  128.0 5.0 %analysis.1 = bf16[128,768]{1,0:T(8,128)(2,1)} custom-call(s32[2]{0:T(128)S(1)} %pad_add_fusion.flags, bf16[256,768]{1,0:T(8,128)(2,1)S(1)} %bitcast.44, bf16[256,256]{1,0:T(8,128)(2,1)S(1)} %copy-done.6, bf16[128,128]{1,0:T(8,128)(2,1)S(1)} %copy-done.7, f32[2,4,512]{2,1,0:T(4,128)S(1)} %fusion.obs, bf16[256,384]{1,0:T(8,128)(2,1)S(1)} %bitcast.47, ...), custom_call_target="tpu_custom_call" | custom-call | tf_op jit(solution)/shard_map/analysis/pallas_call | solution.py:306
  132.9 5.3 %all-to-all-start.3 = ((bf16[16,8,768]{2,1,0:T(8,128)(2,1)}), bf16[16,8,768]{2,1,0:T(8,128)(2,1)S(1)}, u32[]{:S(2)}, u32[]{:S(2)}) async-start(bf16[16,8,768]{2,1,0:T(8,128)(2,1)} %bitcast.19), calls=%async_computation.3 | async-start | bytes 393216 | tf_op jit(solution)/shard_map/all_to_all | solution.py:53
  138.2 1.3 pad_maximum_fusion.1
  139.6 0.1 copy.21
  139.7 0.3 reshape.104.d_mine
  140.0 0.6 copy-done.9
  140.6 0.1 copy-done.10
  140.7 0.1 pad_maximum_fusion.2
  140.9 0.1 copy.22
  141.0 0.3 reshape.105.d_part
  141.3 3.6 %all-to-all-done.3 = bf16[16,8,768]{2,1,0:T(8,128)(2,1)S(1)} async-done(((bf16[16,8,768]{2,1,0:T(8,128)(2,1)}), bf16[16,8,768]{2,1,0:T(8,128)(2,1)S(1)}, u32[]{:S(2)}, u32[]{:S(2)}) %all-to-all-start.3) | async-done | bytes 196640 | tf_op jit(solution)/shard_map/all_to_all | solution.py:53
  144.9 2.1 %decode.1 = bf16[128,1120]{1,0:T(8,128)(2,1)} custom-call(s32[2]{0:T(128)S(1)} %pad_add_fusion.flags, bf16[128,768]{1,0:T(8,128)(2,1)S(1)} %bitcast.46, bf16[128,128]{1,0:T(8,128)(2,1)S(1)} %copy-done.5, bf16[1120,384]{1,0:T(8,128)(2,1)S(1)} %reshape.104.d_mine, bf16[1120,384]{1,0:T(8,128)(2,1)S(1)} %reshape.105.d_part), custom_call_target="tpu_custom_call" | custom-call | tf_op jit(solution)/shard_map/decode/pallas_call | solution.py:323
  (50 shorter events, 0.8 us)
Async XLA Ops:
  2.6 32.0 %copy-start.11 = (bf16[16,70]{1,0:T(8,128)(2,1)S(1)}, bf16[16,70]{1,0:T(8,128)(2,1)}, u32[]{:S(2)}) copy-start(bf16[16,70]{1,0:T(8,128)(2,1)} %param.24) | copy-start | bytes 6724
  2.6 39.5 %all-to-all-start = ((bf16[16,176,384]{2,1,0:T(8,128)(2,1)}), bf16[16,176,384]{2,1,0:T(8,128)(2,1)S(1)}, u32[]{:S(2)}, u32[]{:S(2)}) async-start(bf16[16,176,384]{2,1,0:T(8,128)(2,1)} %broadcast_in_dim.7), calls=%async_computation | async-start | bytes 4325376 | tf_op jit(solution)/shard_map/all_to_all | solution.py:53
  14.0 26.1 %collective-permute-start.2 = (bf16[176,384]{1,0:T(8,128)(2,1)S(1)}, bf16[176,384]{1,0:T(8,128)(2,1)S(1)}, u32[]{:S(2)}, u32[]{:S(2)}) collective-permute-start(bf16[176,384]{1,0:T(8,128)(2,1)S(1)} %slice_select_fusion), channel_id=1, source_target_pairs={{0,30},{2,28},{4,26},{6,24},{8,22},{10,20},{12,18},{14,16},{16,14}... | collective-permute-start | bytes 405512 | tf_op jit(solution)/shard_map/ppermute | solution.py:40
  24.5 26.2 %collective-permute-start = (bf16[68,1120]{1,0:T(8,128)(2,1)S(1)}, bf16[68,1120]{1,0:T(8,128)(2,1)S(1)}, u32[]{:S(2)}, u32[]{:S(2)}) collective-permute-start(bf16[68,1120]{1,0:T(8,128)(2,1)S(1)} %get-tuple-element.44), channel_id=1, source_target_pairs={{0,8},{2,10},{4,12},{6,14},{8,16},{10,18},{12,20},{14,22},{16,24},... | collective-permute-start | bytes 456968 | tf_op jit(solution)/shard_map/ppermute | solution.py:35
  32.7 20.0 %collective-permute-start.1 = (bf16[68,1120]{1,0:T(8,128)(2,1)S(1)}, bf16[68,1120]{1,0:T(8,128)(2,1)S(1)}, u32[]{:S(2)}, u32[]{:S(2)}) collective-permute-start(bf16[68,1120]{1,0:T(8,128)(2,1)S(1)} %get-tuple-element.43), channel_id=1, source_target_pairs={{0,24},{2,26},{4,28},{6,30},{8,0},{10,2},{12,4},{14,6},{16,8},{18,... | collective-permute-start | bytes 456968 | tf_op jit(solution)/shard_map/ppermute | solution.py:35
  42.1 38.5 %copy-start.12 = (f32[12]{0:T(128)S(1)}, f32[12]{0:T(128)}, u32[]{:S(2)}) copy-start(f32[12]{0:T(128)} %param.23) | copy-start | bytes 148
  42.1 42.3 %copy-start.8 = (bf16[136,1120]{1,0:T(8,128)(2,1)S(1)}, bf16[136,1120]{1,0:T(8,128)(2,1)}, u32[]{:S(2)}) copy-start(bf16[136,1120]{1,0:T(8,128)(2,1)} %prepare.1) | copy-start | bytes 913924
  42.1 1.4 copy-start
  43.4 35.2 %all-to-all-start.1 = ((bf16[16,192,384]{2,1,0:T(8,128)(2,1)}), bf16[16,192,384]{2,1,0:T(8,128)(2,1)S(1)}, u32[]{:S(2)}, u32[]{:S(2)}) async-start(bf16[16,192,384]{2,1,0:T(8,128)(2,1)} %broadcast_in_dim.6), calls=%async_computation.1 | async-start | bytes 4718592 | tf_op jit(solution)/shard_map/all_to_all | solution.py:53
  52.7 16.7 %collective-permute-start.7 = (bf16[16,176,384]{2,1,0:T(8,128)(2,1)}, bf16[16,176,384]{2,1,0:T(8,128)(2,1)S(1)}, u32[]{:S(2)}, u32[]{:S(2)}) collective-permute-start(bf16[16,176,384]{2,1,0:T(8,128)(2,1)} %copy-done), channel_id=1, source_target_pairs={{0,1},{1,0},{2,3},{3,2},{4,5},{5,4},{6,7},{7,6},{8,9},{9,8},{10,11... | collective-permute-start | bytes 6488072 | tf_op jit(solution)/shard_map/ppermute | solution.py:31
  54.6 14.7 %collective-permute-start.3 = (bf16[68,1120]{1,0:T(8,128)(2,1)S(1)}, bf16[68,1120]{1,0:T(8,128)(2,1)S(1)}, u32[]{:S(2)}, u32[]{:S(2)}) collective-permute-start(bf16[68,1120]{1,0:T(8,128)(2,1)S(1)} %collective-permute-done), channel_id=1, source_target_pairs={{0,8},{2,10},{4,12},{6,14},{8,16},{10,18},{12,20},{14,22},{16,24},... | collective-permute-start | bytes 456968 | tf_op jit(solution)/shard_map/ppermute | solution.py:35
  58.1 26.1 %collective-permute-start.4 = (bf16[68,1120]{1,0:T(8,128)(2,1)S(1)}, bf16[68,1120]{1,0:T(8,128)(2,1)S(1)}, u32[]{:S(2)}, u32[]{:S(2)}) collective-permute-start(bf16[68,1120]{1,0:T(8,128)(2,1)S(1)} %collective-permute-done.1), channel_id=1, source_target_pairs={{0,24},{2,26},{4,28},{6,30},{8,0},{10,2},{12,4},{14,6},{16,8},{18,... | collective-permute-start | bytes 456968 | tf_op jit(solution)/shard_map/ppermute | solution.py:35
  69.3 1.4 copy-start.2
  78.6 22.7 %collective-permute-start.8 = (bf16[16,192,384]{2,1,0:T(8,128)(2,1)S(1)}, bf16[16,192,384]{2,1,0:T(8,128)(2,1)}, u32[]{:S(2)}, u32[]{:S(2)}) collective-permute-start(bf16[16,192,384]{2,1,0:T(8,128)(2,1)S(1)} %all-to-all-done.1.other_m), channel_id=1, source_target_pairs={{0,1},{1,0},{2,3},{3,2},{4,5},{5,4},{6,7},{7,6},{8,9},{9,8},{10,11... | collective-permute-start | bytes 7077896 | tf_op jit(solution)/shard_map/ppermute | solution.py:31
  84.4 14.8 %collective-permute-start.5 = (bf16[2,64,1120]{2,1,0:T(8,128)(2,1)S(1)}, bf16[2,64,1120]{2,1,0:T(8,128)(2,1)S(1)}, u32[]{:S(2)}, u32[]{:S(2)}) collective-permute-start(bf16[2,64,1120]{2,1,0:T(8,128)(2,1)S(1)} %get-tuple-element.39), channel_id=1, source_target_pairs={{0,15},{2,1},{4,3},{6,5},{8,7},{10,9},{12,11},{14,13},{15,0},{1,2}... | collective-permute-start | bytes 860168 | tf_op jit(solution)/shard_map/ppermute | solution.py:45
  91.2 8.0 %collective-permute-start.6 = (bf16[2,64,1120]{2,1,0:T(8,128)(2,1)S(1)}, bf16[2,64,1120]{2,1,0:T(8,128)(2,1)S(1)}, u32[]{:S(2)}, u32[]{:S(2)}) collective-permute-start(bf16[2,64,1120]{2,1,0:T(8,128)(2,1)S(1)} %get-tuple-element.40), channel_id=1, source_target_pairs={{0,1},{1,0},{2,3},{3,2},{4,5},{5,4},{6,7},{7,6},{8,9},{9,8},{10,11... | collective-permute-start | bytes 860168 | tf_op jit(solution)/shard_map/ppermute | solution.py:31
  93.1 6.2 %copy-start.13 = (bf16[1120,1280]{1,0:T(8,128)(2,1)S(1)}, bf16[1120,1280]{1,0:T(8,128)(2,1)}, u32[]{:S(2)}) copy-start(bf16[1120,1280]{1,0:T(8,128)(2,1)} %constant.44.clone) | copy-start | bytes 8601604
  99.4 1.9 %copy-start.1 = (bf16[16,176,384]{2,1,0:T(8,128)(2,1)S(1)}, bf16[16,176,384]{2,1,0:T(8,128)(2,1)}, u32[]{:S(2)}) copy-start(bf16[16,176,384]{2,1,0:T(8,128)(2,1)} %copy-done) | copy-start | bytes 6488068
  99.4 2.3 %copy-start.3 = (bf16[16,176,384]{2,1,0:T(8,128)(2,1)S(1)}, bf16[16,176,384]{2,1,0:T(8,128)(2,1)}, u32[]{:S(2)}) copy-start(bf16[16,176,384]{2,1,0:T(8,128)(2,1)} %copy-done.2) | copy-start | bytes 6488068
  99.4 2.2 %copy-start.4 = (bf16[256,256]{1,0:T(8,128)(2,1)S(1)}, bf16[256,256]{1,0:T(8,128)(2,1)}, u32[]{:S(2)}) copy-start(bf16[256,256]{1,0:T(8,128)(2,1)} %constant.45.clone.order) | copy-start | bytes 393220
  113.1 14.8 %all-to-all-start.2 = ((bf16[16,16,768]{2,1,0:T(8,128)(2,1)}), bf16[16,16,768]{2,1,0:T(8,128)(2,1)S(1)}, u32[]{:S(2)}, u32[]{:S(2)}) async-start(bf16[16,16,768]{2,1,0:T(8,128)(2,1)} %bitcast.15), calls=%async_computation.2 | async-start | bytes 786432 | tf_op jit(solution)/shard_map/all_to_all | solution.py:53
  121.0 7.0 %copy-start.6 = (bf16[256,256]{1,0:T(8,128)(2,1)S(1)}, bf16[256,256]{1,0:T(8,128)(2,1)}, u32[]{:S(2)}) copy-start(bf16[256,256]{1,0:T(8,128)(2,1)} %constant.46.clone.order) | copy-start | bytes 393220
  121.0 7.0 %copy-start.7 = (bf16[128,128]{1,0:T(8,128)(2,1)S(1)}, bf16[128,128]{1,0:T(8,128)(2,1)}, u32[]{:S(2)}) copy-start(bf16[128,128]{1,0:T(8,128)(2,1)} %constant.47.clone.back_order) | copy-start | bytes 98308
  132.9 12.0 %all-to-all-start.3 = ((bf16[16,8,768]{2,1,0:T(8,128)(2,1)}), bf16[16,8,768]{2,1,0:T(8,128)(2,1)S(1)}, u32[]{:S(2)}, u32[]{:S(2)}) async-start(bf16[16,8,768]{2,1,0:T(8,128)(2,1)} %bitcast.19), calls=%async_computation.3 | async-start | bytes 393216 | tf_op jit(solution)/shard_map/all_to_all | solution.py:53
  139.5 1.0 copy-start.9
  139.6 1.2 copy-start.10
  140.9 4.0 %copy-start.5 = (bf16[128,128]{1,0:T(8,128)(2,1)S(1)}, bf16[128,128]{1,0:T(8,128)(2,1)}, u32[]{:S(2)}) copy-start(bf16[128,128]{1,0:T(8,128)(2,1)} %constant.43.clone.order) | copy-start | bytes 98308
